TPU v7x, 128 devices: a whole 4x4x4 slice. The times are simulated.
128 devices in a mesh: row: 8 (over y, core), seq: 4 (over x), head: 4 (over z).
Axes of the slice: x: 4, y: 4, z: 4, core: 2. Of those that a mesh axis runs over, the one named last changes fastest.
Arguments:
- tokens: bfloat16 [8, 2048, 512], P('row', ('seq', 'head')), may hold values from -6 to 6
- starts: int32 [8, 6], P('row'), may hold values from 0 to 2047, as said below
- gain_one: float32 [512], replicated, may hold values from 0.25 to 1.75
- w_in: bfloat16 [512, 2048], replicated, may hold values from -0.25 to 0.25
- conv_weight: float32 [4, 1024], replicated, may hold values from -3 to 3
- conv_bias: float32 [1024], replicated, may hold values from -4 to 4
- w_x: bfloat16 [1024, 64], replicated, may hold values from -0.75 to 0.75
- w_dt: bfloat16 [32, 1024], replicated, may hold values from -0.5 to 0.5
- dt_bias: float32 [1024], replicated, may hold values from -9 to -3
- a_log: float32 [16, 1024], replicated, may hold values from 0 to 1.4
- d_skip: float32 [1024], replicated, may hold values from 0.5 to 1.5
- w_out: bfloat16 [1024, 512], replicated, may hold values from -0.375 to 0.375
- gain_two: float32 [512], replicated, may hold values from 0.25 to 1.75
- w_q: bfloat16 [512, 512], replicated, may hold values from -0.375 to 0.375
- w_k: bfloat16 [512, 512], replicated, may hold values from -0.375 to 0.375
- w_v: bfloat16 [512, 512], replicated, may hold values from -0.25 to 0.25
- w_o: bfloat16 [512, 512], replicated, may hold values from -2 to 2
- cotangent: bfloat16 [8, 2048, 512], P('row', ('seq', 'head')), may hold values from -6 to 6
Outputs:
- mixed: bfloat16 [8, 2048, 512], P('row', ('seq', 'head'))
- grad_tokens: float32 [8, 2048, 512], P('row', ('seq', 'head'))
- grad_gain_one: float32 [512], replicated
- grad_w_in: float32 [512, 2048], replicated
- grad_conv_weight: float32 [4, 1024], replicated
- grad_conv_bias: float32 [1024], replicated
- grad_w_x: float32 [1024, 64], replicated
- grad_w_dt: float32 [32, 1024], replicated
- grad_dt_bias: float32 [1024], replicated
- grad_a_log: float32 [16, 1024], replicated
- grad_d_skip: float32 [1024], replicated
- grad_w_out: float32 [1024, 512], replicated
- grad_gain_two: float32 [512], replicated
- grad_w_q: float32 [512, 512], replicated
- grad_w_k: float32 [512, 512], replicated
- grad_w_v: float32 [512, 512], replicated
- grad_w_o: float32 [512, 512], replicated
Inputs may be any that keep to these rules, and one draw needn't show every extreme that they name: `starts`: each row holds the first positions of its 6 documents in strictly rising order, the first being 0. In each group of 1 row that share an index of row, one row drawn from the seed has a document that covers positions 127 to 1920, and that row's last document is the single position 2047.
All inputs are finite; a program needn't handle non-finite values.
Results may differ from a plain program's by a relative error of at most 0.03.
The roundings to bfloat16 on the way count: a program that leaves them out, or rounds other values in their place, can miss the bound.
Values may be sent and summed in bfloat16 or wider, within the bound.
No kernel may reach another device: no remote copies, remote signals or barrier semaphores. Data moves between devices by JAX's collectives and lax.ppermute only.
A program may use at most 192 MiB of HBM per device.

v0:
```python
import functools

import jax
import jax.numpy as jnp
from jax import lax
from jax.experimental import pallas as pl
from jax.experimental.pallas import tpu as pltpu
from jax.sharding import Mesh, PartitionSpec as P

T, D, E, N, R, HD = 128, 512, 1024, 16, 32, 64
HEADS, BLOCKS, HALF, DOCS, KERNEL, HALO = 8, 16, 64, 6, 4, 16
CHUNK, STEPS = 512, 8
ROWS = T + HALF
RESET = 1e4
LOG2E = 1.4426950408889634
EPS = 1e-05
MASKED = -1e30
PLACE = ("seq", "head")
ALL = ("y", "core", "seq", "head")
bf16, f32, i32 = jnp.bfloat16, jnp.float32, jnp.int32


def mm(a, b):
    return jnp.dot(a, b, preferred_element_type=f32)


def mm_nt(a, b):
    return lax.dot_general(a, b, (((1,), (1,)), ((), ())), preferred_element_type=f32)


def mm_tn(a, b):
    return lax.dot_general(a, b, (((0,), (0,)), ((), ())), preferred_element_type=f32)


def doc_of(meta, pos):
    count = jnp.zeros(pos.shape, i32)
    for k in range(DOCS):
        count = count + (meta[2 + k] <= pos).astype(i32)
    return count


def reset_of(meta, pos):
    hit = meta[2] == pos
    for k in range(1, DOCS):
        hit = hit | (meta[2 + k] == pos)
    return jnp.where(hit, RESET, 0.0)


def inverse_rms(x):
    return lax.rsqrt(jnp.mean(x * x, axis=-1, keepdims=True) + EPS)


def sigmoid(x):
    return 1.0 / (1.0 + jnp.exp(-x))


def silu_slope(x):
    s = sigmoid(x)
    return s * (1.0 + x * (1.0 - s))


def norm_back(values, inverse, gain, upstream):
    scaled = upstream * gain
    inner = jnp.mean(values * scaled, axis=-1, keepdims=True)
    back = inverse * scaled - values * (inverse * inverse * inverse) * inner
    return back, jnp.sum(upstream * values * inverse, axis=0, keepdims=True)


def columns(offset, meta):
    first = meta[0]
    return first + offset + lax.broadcasted_iota(i32, (T, 1), 0)


def scan_forward(dec_ref, sa_ref, bc_ref, rates2, start, part, emit):
    def block(i, h):
        bc = bc_ref[i]
        base = pl.multiple_of(i * STEPS, STEPS)
        for k in range(STEPS):
            t = base + k
            dec = dec_ref[pl.ds(t, 1), part]
            sa = sa_ref[pl.ds(t, 1), part]
            drive = bc[0:N, k : k + 1] * sa
            h = jnp.exp2(dec * rates2) * h + drive
            if emit is not None:
                emit(i, k, t, h, bc)
        return h

    return lax.fori_loop(0, T // STEPS, block, start)


def mamba_in(
    meta, tokens, halo, gain, w_in, conv_w, conv_b, w_x, w_dt, dt_b, a_log,
    send, ext_out, gate_out, conv_out, act_out, step_out, pre_out, bc_out, dt_out, total_out,
    ext, dec, sa, xp,
):
    own = tokens[...].astype(f32)
    before = halo[...].astype(f32)
    low_own = (own * inverse_rms(own) * gain[...]).astype(bf16)
    low_before = (before * inverse_rms(before) * gain[...]).astype(bf16)
    conv_own = mm(low_own, w_in[:, :E]).astype(bf16)
    conv_before = mm(low_before, w_in[:, :E]).astype(bf16)
    ext_out[0:HALO] = conv_before
    ext_out[HALO : HALO + T] = conv_own
    ext[0:HALO] = conv_before.astype(f32)
    ext[HALO : HALO + T] = conv_own.astype(f32)
    gate_out[...] = mm(low_own, w_in[:, E:]).astype(bf16)
    own_doc = doc_of(meta, columns(0, meta))
    conv = jnp.broadcast_to(conv_b[...], (T, E))
    for offset in range(KERNEL):
        same = (doc_of(meta, columns(offset - KERNEL + 1, meta)) == own_doc).astype(f32)
        low = HALO - KERNEL + 1 + offset
        conv = conv + conv_w[offset : offset + 1] * ext[low : low + T] * same
    conv_out[...] = conv
    act = (conv * sigmoid(conv)).astype(bf16)
    act_out[...] = act
    proj = mm(act, w_x[...])
    dt_low = proj[:, :R].astype(bf16)
    dt_out[...] = dt_low
    pre = mm(dt_low, w_dt[...]) + dt_b[...]
    pre_out[...] = pre
    step = jnp.maximum(pre, 0.0) + jnp.log1p(jnp.exp(-jnp.abs(pre)))
    step_out[...] = step
    held = step + reset_of(meta, columns(0, meta))
    dec[...] = held
    sa[...] = step * act.astype(f32)
    xp[...] = jnp.zeros((T, 128), f32)
    xp[:, 0 : R + 2 * N] = proj
    turned = xp[...].T
    for i in range(T // STEPS):
        bc_out[i, :, 0:STEPS] = turned[R : R + 2 * N, i * STEPS : (i + 1) * STEPS]
    total = jnp.sum(held, axis=0, keepdims=True)
    high = total.astype(bf16)
    rest = (total - high.astype(f32)).astype(bf16)
    send[N : N + 8] = jnp.concatenate([high, rest, jnp.zeros((6, E), bf16)], axis=0)
    for c in range(E // CHUNK):
        part = slice(c * CHUNK, (c + 1) * CHUNK)
        rates2 = -jnp.exp(a_log[:, part]) * LOG2E
        h = scan_forward(dec, sa, bc_out, rates2, jnp.zeros((N, CHUNK), f32), part, None)
        send[0:N, part] = h.astype(bf16)
    total_out[...] = total


def roll_half(x):
    return pltpu.roll(x, HALF, axis=1)


def mamba_out(
    meta, got, tokens, step, act, bc, gate, a_log, d_skip, w_out, gain, w_q, w_k, w_v, grad_att,
    send, start_out, ssm_out, gated_out, middle_out, normed_out,
    dec, sa, ssm,
):
    place = meta[1]
    dec[...] = step[...] + reset_of(meta, columns(0, meta))
    act_f = act[...].astype(f32)
    sa[...] = step[...] * act_f
    for c in range(E // CHUNK):
        part = slice(c * CHUNK, (c + 1) * CHUNK)
        rates2 = -jnp.exp(a_log[:, part]) * LOG2E

        def join(j, state):
            tail = got[j, N : N + 8, part].astype(f32)
            total = tail[0:1] + tail[1:2]
            return jnp.exp2(rates2 * total) * state + got[j, 0:N, part].astype(f32)

        start = lax.fori_loop(0, place, join, jnp.zeros((N, CHUNK), f32))
        start_out[:, part] = start

        def emit(i, k, t, h, cols):
            ssm[pl.ds(t, 1), part] = jnp.sum(h * cols[N : 2 * N, k : k + 1], axis=0, keepdims=True)

        scan_forward(dec, sa, bc, rates2, start, part, emit)
    result = ssm[...] + d_skip[...] * act_f
    ssm_out[...] = result
    gates = gate[...].astype(f32)
    gated = (result * (gates * sigmoid(gates))).astype(bf16)
    gated_out[...] = gated
    middle = tokens[...].astype(f32) + mm(gated, w_out[...])
    middle_out[...] = middle
    normed = (middle * inverse_rms(middle) * gain[...]).astype(bf16)
    normed_out[...] = normed
    queries = mm(normed, w_q[...]).astype(bf16).astype(f32) * (HD ** -0.5)
    keys = mm(normed, w_k[...])
    vals = mm(normed, w_v[...])
    grads = grad_att[...].astype(f32)
    low = lax.broadcasted_iota(i32, (T, 128), 1) < HALF
    for m in range(HEADS // 2):
        tile = slice(m * 128, (m + 1) * 128)
        for odd in range(2):
            for first, second, at, rows in ((keys, vals, 0, T), (queries, grads, T, HALF)):
                a, b = first[:, tile], second[:, tile]
                pair = jnp.where(low, a, roll_half(b)) if odd == 0 else jnp.where(low, roll_half(a), b)
                pair = pair.astype(bf16)
                dest = 2 * (2 * m + odd)
                if rows == T:
                    send[dest, 0:T] = pair
                    send[dest + 1, 0:T] = pair
                else:
                    send[dest, T:ROWS] = pair[0:HALF]
                    send[dest + 1, T:ROWS] = pair[HALF:T]


QCHUNK, QBLOCKS = 256, 4


def attention(meta, got, send, kv_t, scores, grads, kv_grad):
    parity = lax.rem(meta[1], 2)
    for i in range(BLOCKS):
        kv_t[:, i * T : (i + 1) * T] = got[i, 0:T].astype(f32).T.astype(bf16)
    lane = lax.broadcasted_iota(i32, (1, QCHUNK), 1)
    low_q = lax.broadcasted_iota(i32, (QCHUNK, 128), 1) < HD
    low_k = lax.broadcasted_iota(i32, (T, 128), 1) < HD
    key_row = lax.broadcasted_iota(i32, (T, QCHUNK), 0)
    for c in range(BLOCKS // QBLOCKS):
        qg = jnp.concatenate([got[c * QBLOCKS + b, T:ROWS] for b in range(QBLOCKS)], axis=0)
        q_only = jnp.where(low_q, qg.astype(f32), 0.0).astype(bf16)
        g_only = jnp.where(low_q, 0.0, qg.astype(f32)).astype(bf16)
        pos = (c * QBLOCKS + lane // HALF) * T + parity * HALF + lane % HALF
        begin = jnp.zeros((1, QCHUNK), i32)
        for k in range(DOCS):
            begin = jnp.maximum(begin, jnp.where(meta[2 + k] <= pos, meta[2 + k], 0))
        tiles = (c + 1) * QBLOCKS
        top = jnp.full((8, QCHUNK), MASKED, f32)
        for i in range(tiles):
            s = mm_nt(got[i, 0:T], q_only)
            allowed = key_row >= begin - i * T
            if i >= c * QBLOCKS:
                allowed = allowed & (key_row <= pos - i * T)
            s = jnp.where(allowed, s, MASKED)
            scores[i] = s
            top = jnp.maximum(top, jnp.max(s.reshape(T // 8, 8, QCHUNK), axis=0))
        top = jnp.max(top, axis=0, keepdims=True)
        total = jnp.zeros((8, QCHUNK), f32)
        cross = jnp.zeros((8, QCHUNK), f32)
        for i in range(tiles):
            p = jnp.exp2((scores[i] - top) * LOG2E)
            scores[i] = p
            g = mm_nt(got[i, 0:T], g_only)
            grads[i] = g
            total = total + jnp.sum(p.reshape(T // 8, 8, QCHUNK), axis=0)
            cross = cross + jnp.sum((p * g).reshape(T // 8, 8, QCHUNK), axis=0)
        inverse = 1.0 / jnp.sum(total, axis=0, keepdims=True)
        cross = jnp.sum(cross, axis=0, keepdims=True) * inverse
        out_t = jnp.zeros((128, QCHUNK), f32)
        dq_t = jnp.zeros((128, QCHUNK), f32)
        for i in range(tiles):
            prob = scores[i] * inverse
            low_p = prob.astype(bf16)
            low_s = (prob * (grads[i] - cross)).astype(bf16)
            turned = kv_t[:, i * T : (i + 1) * T]
            out_t = out_t + mm(turned, low_p)
            dq_t = dq_t + mm(turned, low_s)
            both = jnp.where(low_k, mm(low_s, qg), mm(low_p, qg))
            if i >= c * QBLOCKS:
                kv_grad[i] = both
            else:
                kv_grad[i] = kv_grad[i] + both
        pair = jnp.where(low_q, dq_t.T * (HD ** -0.5), out_t.T).astype(bf16)
        for b in range(QBLOCKS):
            send[c * QBLOCKS + b, T:ROWS] = pair[b * HALF : (b + 1) * HALF]
    for i in range(BLOCKS):
        send[i, 0:T] = kv_grad[i].astype(bf16)


def middle_back(
    meta, got, cot, middle, normed, gated, gate, ssm, act, step, bc, a_log, d_skip,
    w_o, w_q, w_k, w_v, w_out, gain,
    send, mixed, grad_mid_out, g_out, grad_gate_out,
    gw_o, gw_q, gw_k, gw_v, gw_out, g_gain, g_skip,
    att, dq, dk, dv, dec,
):
    low = lax.broadcasted_iota(i32, (HALF, 128), 1) < HALF
    low_t = lax.broadcasted_iota(i32, (T, 128), 1) < HALF
    for m in range(HEADS // 2):
        tile = slice(m * 128, (m + 1) * 128)
        for p in range(2):
            a = got[4 * m + p, T:ROWS].astype(f32)
            b = got[4 * m + 2 + p, T:ROWS].astype(f32)
            rows = slice(p * HALF, (p + 1) * HALF)
            dq[rows, tile] = jnp.where(low, a, roll_half(b)).astype(bf16)
            att[rows, tile] = jnp.where(low, roll_half(a), b).astype(bf16)
        a = got[4 * m, 0:T].astype(f32) + got[4 * m + 1, 0:T].astype(f32)
        b = got[4 * m + 2, 0:T].astype(f32) + got[4 * m + 3, 0:T].astype(f32)
        dk[:, tile] = jnp.where(low_t, a, roll_half(b)).astype(bf16)
        dv[:, tile] = jnp.where(low_t, roll_half(a), b).astype(bf16)
    cot_low = cot[...]
    values = middle[...]
    mixed[...] = (values + mm(att[...], w_o[...])).astype(bf16)
    gw_o[...] = mm_tn(att[...], cot_low)
    gw_q[...] = mm_tn(normed[...], dq[...])
    gw_k[...] = mm_tn(normed[...], dk[...])
    gw_v[...] = mm_tn(normed[...], dv[...])
    upstream = mm_nt(dq[...], w_q[...]) + mm_nt(dk[...], w_k[...]) + mm_nt(dv[...], w_v[...])
    back, gain_grad = norm_back(values, inverse_rms(values), gain[...], upstream)
    g_gain[...] = gain_grad
    grad_mid = cot_low.astype(f32) + back
    grad_mid_out[...] = grad_mid
    mid_low = grad_mid.astype(bf16)
    gw_out[...] = mm_tn(gated[...], mid_low)
    grad_gated = mm_nt(mid_low, w_out[...]).astype(bf16).astype(f32)
    gates = gate[...].astype(f32)
    sig = sigmoid(gates)
    g = grad_gated * (gates * sig)
    g_out[...] = g
    grad_gate_out[...] = (grad_gated * ssm[...] * (sig * (1.0 + gates * (1.0 - sig)))).astype(bf16)
    g_skip[...] = jnp.sum(g * act[...].astype(f32), axis=0, keepdims=True)
    dec[...] = step[...] + reset_of(meta, columns(0, meta))
    for c in range(E // CHUNK):
        part = slice(c * CHUNK, (c + 1) * CHUNK)
        rates2 = -jnp.exp(a_log[:, part]) * LOG2E

        def block(turn, carry):
            i = T // STEPS - 1 - turn
            cols = bc[i]
            base = pl.multiple_of(i * STEPS, STEPS)
            for k in reversed(range(STEPS)):
                t = base + k
                adjoint = g_out[pl.ds(t, 1), part] * cols[N : 2 * N, k : k + 1] + carry
                carry = jnp.exp2(dec[pl.ds(t, 1), part] * rates2) * adjoint
            return carry

        carry = lax.fori_loop(0, T // STEPS, block, jnp.zeros((N, CHUNK), f32))
        send[:, part] = carry.astype(bf16)


def mamba_back(
    meta, got, forward, start, g, act, step, pre, bc, dt_low, conv, ext_low, a_log, d_skip,
    conv_w, w_x, w_dt,
    own_out, edge_out, gw_x, gw_dt, g_dt_b, g_a_log, g_conv_w, g_conv_b,
    dec, sa, decay, kept, gs, ab, ext, padded,
):
    place = meta[1]
    dec[...] = step[...] + reset_of(meta, columns(0, meta))
    act_f = act[...].astype(f32)
    sa[...] = step[...] * act_f
    lane = lax.broadcasted_iota(i32, (N, 128), 1)
    grad_b = jnp.zeros((N, 128), f32)
    grad_c = jnp.zeros((N, 128), f32)
    for c in range(E // CHUNK):
        part = slice(c * CHUNK, (c + 1) * CHUNK)
        rates = -jnp.exp(a_log[:, part])
        rates2 = rates * LOG2E

        def join(turn, state):
            j = BLOCKS - 1 - turn
            tail = forward[j, N : N + 8, part].astype(f32)
            total = tail[0:1] + tail[1:2]
            return jnp.exp2(rates2 * total) * state + got[j, :, part].astype(f32)

        carry = lax.fori_loop(0, BLOCKS - 1 - place, join, jnp.zeros((N, CHUNK), f32))

        def ahead(i, state):
            h, acc = state
            cols = bc[i]
            base = pl.multiple_of(i * STEPS, STEPS)
            for k in range(STEPS):
                t = base + k
                factor = jnp.exp2(dec[pl.ds(t, 1), part] * rates2)
                moved = factor * h
                decay[t] = factor
                kept[t] = moved
                h = moved + cols[0:N, k : k + 1] * sa[pl.ds(t, 1), part]
                col = jnp.sum(h * g[pl.ds(t, 1), part], axis=1, keepdims=True)
                acc = acc + jnp.where(lane == t, col, 0.0)
            return h, acc

        _, grad_c = lax.fori_loop(0, T // STEPS, ahead, (start[:, part], grad_c))

        def behind(turn, state):
            carry, acc, along = state
            i = T // STEPS - 1 - turn
            cols = bc[i]
            base = pl.multiple_of(i * STEPS, STEPS)
            for k in reversed(range(STEPS)):
                t = base + k
                adjoint = g[pl.ds(t, 1), part] * cols[N : 2 * N, k : k + 1] + carry
                carry = decay[t] * adjoint
                log_grad = adjoint * kept[t]
                along = along + log_grad * step[pl.ds(t, 1), part]
                gs[pl.ds(t, 1), part] = jnp.sum(log_grad * rates, axis=0, keepdims=True)
                ab[pl.ds(t, 1), part] = jnp.sum(adjoint * cols[0:N, k : k + 1], axis=0, keepdims=True)
                col = jnp.sum(adjoint * sa[pl.ds(t, 1), part], axis=1, keepdims=True)
                acc = acc + jnp.where(lane == t, col, 0.0)
            return carry, acc, along

        _, grad_b, along = lax.fori_loop(
            0, T // STEPS, behind, (carry, grad_b, jnp.zeros((N, CHUNK), f32))
        )
        g_a_log[:, part] = along * rates
    adjoint_b = ab[...]
    grad_step = gs[...] + adjoint_b * act_f
    grad_act = g[...] * d_skip[...] + adjoint_b * step[...]
    grad_pre = (grad_step * sigmoid(pre[...])).astype(bf16)
    g_dt_b[...] = jnp.sum(grad_pre.astype(f32), axis=0, keepdims=True)
    gw_dt[...] = mm_tn(dt_low[...], grad_pre)
    turned = jnp.concatenate([grad_b, grad_c, jnp.zeros((128 - 2 * N, 128), f32)], axis=0).T
    grad_proj = jnp.concatenate([mm_nt(grad_pre, w_dt[...]), turned[:, 0 : 2 * N]], axis=1).astype(bf16)
    gw_x[...] = mm_tn(act[...], grad_proj)
    grad_act = grad_act + mm_nt(grad_proj, w_x[...])
    grad_conv = grad_act * silu_slope(conv[...])
    g_conv_b[...] = jnp.sum(grad_conv, axis=0, keepdims=True)
    padded[0:T] = grad_conv
    padded[T : T + 8] = jnp.zeros((8, E), f32)
    ext[...] = ext_low[...].astype(f32)
    own_doc = doc_of(meta, columns(0, meta))
    own = jnp.zeros((T, E), f32)
    lift = KERNEL - 1
    rows = lax.broadcasted_iota(i32, (T, 1), 0)
    for offset in range(KERNEL):
        same = (doc_of(meta, columns(offset - lift, meta)) == own_doc).astype(f32)
        low = HALO - lift + offset
        g_conv_w[offset : offset + 1] = jnp.sum(grad_conv * ext[low : low + T] * same, axis=0, keepdims=True)
        up = lift - offset
        ahead_same = (doc_of(meta, columns(0, meta)) == doc_of(meta, columns(up, meta))) & (rows < T - up)
        own = own + conv_w[offset : offset + 1] * padded[up : up + T] * ahead_same.astype(f32)
    own_out[...] = own
    first = meta[0]
    edges = []
    for row in range(lift):
        edge = jnp.zeros((1, E), f32)
        here = doc_of(meta, first - lift + row + jnp.zeros((1, 1), i32))
        for offset in range(row + 1):
            at = row - offset
            same = (doc_of(meta, first + at + jnp.zeros((1, 1), i32)) == here).astype(f32)
            edge = edge + conv_w[offset : offset + 1] * padded[at : at + 1] * same
        edges.append(edge)
    edge_out[...] = jnp.concatenate(edges + [jnp.zeros((8 - lift, E), f32)], axis=0)


def input_back(
    tokens, gain, w_in, own, edge, grad_gate, grad_mid,
    grad_tokens, gw_in, g_gain, full,
):
    full[...] = own[...]
    lift = KERNEL - 1
    full[T - lift : T] = own[T - lift : T] + edge[0:lift]
    values = tokens[...].astype(f32)
    inverse = inverse_rms(values)
    normed = (values * inverse * gain[...]).astype(bf16)
    grad_input = full[...].astype(bf16)
    gate = grad_gate[...]
    gw_in[:, :E] = mm_tn(normed, grad_input)
    gw_in[:, E:] = mm_tn(normed, gate)
    upstream = mm_nt(grad_input, w_in[:, :E]) + mm_nt(gate, w_in[:, E:])
    back, gain_grad = norm_back(values, inverse, gain[...], upstream)
    grad_tokens[...] = grad_mid[...] + back
    g_gain[...] = gain_grad


def call(body, name, outs, scratch, *args, smem=True):
    specs = [pl.BlockSpec(memory_space=pltpu.VMEM)] * len(args)
    if smem:
        specs[0] = pl.BlockSpec(memory_space=pltpu.SMEM)
    return pl.pallas_call(
        body,
        name=name,
        out_shape=[jax.ShapeDtypeStruct(s, t) for s, t in outs],
        in_specs=specs,
        out_specs=[pl.BlockSpec(memory_space=pltpu.VMEM)] * len(outs),
        scratch_shapes=[pltpu.VMEM(s, t) for s, t in scratch],
        compiler_params=pltpu.CompilerParams(vmem_limit_bytes=56 * 1024 * 1024),
    )(*args)


def shift(x, by):
    pairs = [(i, i + by) for i in range(BLOCKS) if 0 <= i + by < BLOCKS]
    return lax.ppermute(x, PLACE, pairs)


def swap(x):
    return lax.all_to_all(x, PLACE, 0, 0, tiled=True)


def spread(x):
    return swap(jnp.broadcast_to(x[None], (BLOCKS,) + x.shape))


def layer(
    tokens, starts, gain_one, w_in, conv_w, conv_b, w_x, w_dt, dt_bias, a_log, d_skip, w_out,
    gain_two, w_q, w_k, w_v, w_o, cotangent,
):
    tokens, cot = tokens[0], cotangent[0]
    place = lax.axis_index(PLACE)
    meta = jnp.concatenate([jnp.stack([place * T, place]).astype(i32), starts[0]])
    row = lambda v: v.reshape(1, -1)
    halo = shift(tokens[T - HALO :], 1)
    grad_att = mm_nt(cot, w_o).astype(bf16)
    te, tel = ((T, E), f32), ((T, E), bf16)
    send, ext, gate, conv, act, step, pre, bc, dt_low, _ = call(
        mamba_in, "mamba_in",
        [((N + 8, E), bf16), ((HALO + T, E), bf16), tel, te, tel, te, te,
         ((T // STEPS, 2 * N, 128), f32), ((T, R), bf16), ((1, E), f32)],
        [((HALO + T, E), f32), te, te, ((T, 128), f32)],
        meta, tokens, halo, row(gain_one), w_in, conv_w, row(conv_b), w_x, w_dt, row(dt_bias), a_log,
    )
    forward = spread(send)
    packed, start, ssm, gated, middle, normed = call(
        mamba_out, "mamba_out",
        [((BLOCKS, ROWS, 128), bf16), ((N, E), f32), te, tel, ((T, D), f32), ((T, D), bf16)],
        [te, te, te],
        meta, forward, tokens, step, act, bc, gate, a_log, row(d_skip), w_out, row(gain_two),
        w_q, w_k, w_v, grad_att,
    )
    (back,) = call(
        attention, "attention",
        [((BLOCKS, ROWS, 128), bf16)],
        [((128, BLOCKS * T), bf16), ((BLOCKS, T, QCHUNK), f32), ((BLOCKS, T, QCHUNK), f32),
         ((BLOCKS, T, 128), f32)],
        meta, swap(packed),
    )
    send, mixed, grad_mid, g, grad_gate, gw_o, gw_q, gw_k, gw_v, gw_out, g_gain_two, g_skip = call(
        middle_back, "middle_back",
        [((N, E), bf16), ((T, D), bf16), ((T, D), f32), te, tel,
         ((D, D), f32), ((D, D), f32), ((D, D), f32), ((D, D), f32), ((E, D), f32),
         ((1, D), f32), ((1, E), f32)],
        [((T, D), bf16)] * 4 + [te],
        meta, swap(back), cot, middle, normed, gated, gate, ssm, act, step, bc, a_log, row(d_skip),
        w_o, w_q, w_k, w_v, w_out, row(gain_two),
    )
    own, edge, gw_x, gw_dt, g_dt_b, g_a_log, g_conv_w, g_conv_b = call(
        mamba_back, "mamba_back",
        [te, ((8, E), f32), ((E, R + 2 * N), f32), ((R, E), f32), ((1, E), f32), ((N, E), f32),
         ((KERNEL, E), f32), ((1, E), f32)],
        [te, te, ((T, N, CHUNK), f32), ((T, N, CHUNK), f32), te, te, ((HALO + T, E), f32),
         ((T + 8, E), f32)],
        meta, spread(send), forward, start, g, act, step, pre, bc, dt_low, conv, ext, a_log,
        row(d_skip), conv_w, w_x, w_dt,
    )
    grad_tokens, gw_in, g_gain_one = call(
        input_back, "input_back",
        [((T, D), f32), ((D, 2 * E), f32), ((1, D), f32)],
        [te],
        tokens, row(gain_one), w_in, own, shift(edge, -1), grad_gate, grad_mid,
        smem=False,
    )
    summed = lax.psum(
        (g_gain_one[0], gw_in, g_conv_w, g_conv_b[0], gw_x, gw_dt, g_dt_b[0], g_a_log, g_skip[0],
         gw_out, g_gain_two[0], gw_q, gw_k, gw_v, gw_o),
        ALL,
    )
    return (mixed[None], grad_tokens[None]) + tuple(summed)


def solution(mesh):
    rows, seq, head = mesh.devices.shape
    fine = Mesh(mesh.devices.reshape(rows // 2, 2, seq, head), ALL)
    split = P(("y", "core"), PLACE, None)
    return jax.shard_map(
        layer,
        mesh=fine,
        in_specs=(split, P(("y", "core"), None)) + (P(),) * 15 + (split,),
        out_specs=(split, split) + (P(),) * 15,
        check_vma=False,
    )
```

profile of v0, /device:TPU:1, one launch (start us, length us, event | category | flops | bytes accessed | tf_op | source)
XLA Modules:
  0.0 358.4 jit_solution(9216609567496761817)
XLA Ops:
  7.2 0.7 slice_bitcast_fusion
  7.9 4.4 %collective-permute-start = (bf16[16,512]{1,0:T(8,128)(2,1)S(1)}, bf16[16,512]{1,0:T(8,128)(2,1)S(1)}, u32[]{:S(2)}, u32[]{:S(2)}) collective-permute-start(bf16[16,512]{1,0:T(8,128)(2,1)S(1)} %slice_bitcast_fusion), channel_id=1, source_target_pairs={{0,1},{1,2},{2,3},{3,4},{4,5},{5,6},{6,7},{7,8},{8,9},{9,10},{10,1... | collective-permute-start | bytes 49160 | tf_op jit(solution)/shard_map/ppermute | solution.py:466
  12.3 1.3 pad_add_fusion.meta
  13.5 1.7 copy.35.w_x
  15.9 8.1 %mamba_in.1 = (bf16[24,1024]{1,0:T(8,128)(2,1)}, bf16[144,1024]{1,0:T(8,128)(2,1)}, bf16[128,1024]{1,0:T(8,128)(2,1)}, f32[128,1024]{1,0:T(8,128)}, bf16[128,102...) custom-call(s32[8]{0:T(128)} %pad_add_fusion.meta, ...), custom_call_target="tpu_custom_call" | custom-call | tf_op jit(solution)/shard_map/mamba_in/pallas_call | solution.py:453
  24.0 1.8 broadcast_in_dim.8
  25.7 7.1 %all-to-all-start = ((bf16[16,24,1024]{2,1,0:T(8,128)(2,1)}), bf16[16,24,1024]{2,1,0:T(8,128)(2,1)S(1)}, u32[]{:S(2)}, u32[]{:S(2)}) async-start(bf16[16,24,1024]{2,1,0:T(8,128)(2,1)} %broadcast_in_dim.8), calls=%async_computation | async-start | bytes 1572864 | tf_op jit(solution)/shard_map/all_to_all | solution.py:470
  33.0 1.0 convolution_convert_fusion.grad_att
  33.9 11.7 %all-to-all-done.got.forward = bf16[16,24,1024]{2,1,0:T(8,128)(2,1)S(1)} async-done(((bf16[16,24,1024]{2,1,0:T(8,128)(2,1)}), bf16[16,24,1024]{2,1,0:T(8,128)(2,1)S(1)}, u32[]{:S(2)}, u32[]{:S(2)}) %all-to-all-start) | async-done | bytes 786464 | tf_op jit(solution)/shard_map/all_to_all | solution.py:470
  45.6 0.9 copy-done
  46.5 9.1 %mamba_out.1 = (bf16[16,192,128]{2,1,0:T(8,128)(2,1)}, f32[16,1024]{1,0:T(8,128)}, f32[128,1024]{1,0:T(8,128)}, bf16[128,1024]{1,0:T(8,128)(2,1)}, f32[128,512]{1,0:T(8,128)}, /*index=5*/bf16[128,512]{1,0:T(8,128)(2,1)}) custom-call(s32[8]{0:T(128)} %pad_add_fusion.meta, bf16[16,24,1024]{2,1,0:T(8,128)(2,1)} %copy-done, bf16[128,512]{1,0:T(8,128)(2,1)} %bitcast.23, ...), custom_call_target="tpu_custom_call" | custom-call | tf_op jit(solution)/shard_map/mamba_out/pallas_call | solution.py:453
  55.6 16.0 %all_to_all.20.got = bf16[16,192,128]{2,1,0:T(8,128)(2,1)} all-to-all(bf16[16,192,128]{2,1,0:T(8,128)(2,1)} %get-tuple-element.60), channel_id=1, replica_groups=mesh['y'=4,'core'=2,'seq'=4,'head'=4] {'seq','head'}, dimensions={0} | all-to-all | bytes 1572864 | tf_op jit(solution)/shard_map/all_to_all | solution.py:470
  71.7 8.5 %attention.1 = bf16[16,192,128]{2,1,0:T(8,128)(2,1)} custom-call(s32[8]{0:T(128)} %pad_add_fusion.meta, bf16[16,192,128]{2,1,0:T(8,128)(2,1)} %all_to_all.20.got), custom_call_target="tpu_custom_call" | custom-call | tf_op jit(solution)/shard_map/attention/pallas_call | solution.py:453
  80.2 14.7 %all_to_all.21.got = bf16[16,192,128]{2,1,0:T(8,128)(2,1)} all-to-all(bf16[16,192,128]{2,1,0:T(8,128)(2,1)} %attention.1), channel_id=1, replica_groups=mesh['y'=4,'core'=2,'seq'=4,'head'=4] {'seq','head'}, dimensions={0} | all-to-all | bytes 1572864 | tf_op jit(solution)/shard_map/all_to_all | solution.py:470
  94.9 11.5 %middle_back.1 = (bf16[16,1024]{1,0:T(8,128)(2,1)}, bf16[128,512]{1,0:T(8,128)(2,1)}, f32[128,512]{1,0:T(8,128)}, f32[128,1024]{1,0:T(8,128)}, bf16[128,1024]{1,...) custom-call(s32[8]{0:T(128)} %pad_add_fusion.meta, ...), custom_call_target="tpu_custom_call" | custom-call | tf_op jit(solution)/shard_map/middle_back/pallas_call | solution.py:453
  106.4 0.8 broadcast_in_dim.20
  107.2 12.8 %all_to_all.22.got = bf16[16,16,1024]{2,1,0:T(8,128)(2,1)} all-to-all(bf16[16,16,1024]{2,1,0:T(8,128)(2,1)S(1)} %broadcast_in_dim.20), channel_id=1, replica_groups=mesh['y'=4,'core'=2,'seq'=4,'head'=4] {'seq','head'}, dimensions={0} | all-to-all | bytes 1048576 | tf_op jit(solution)/shard_map/all_to_all | solution.py:470
  120.0 31.8 %mamba_back.1 = (f32[128,1024]{1,0:T(8,128)}, f32[8,1024]{1,0:T(8,128)}, f32[1024,64]{1,0:T(8,128)}, f32[32,1024]{1,0:T(8,128)}, f32[1,1024]{1,0:T(1,128)}, /*in...) custom-call(s32[8]{0:T(128)} %pad_add_fusion.meta, bf16[16,16,1024]{2,1,0:T(8,128)(2,1)} %all_to_all.22.got, ...), custom_call_target="tpu_custom_call" | custom-call | tf_op jit(solution)/shard_map/mamba_back/pallas_call | solution.py:453
  151.7 1.3 collective-permute-start.1
  153.0 3.6 collective-permute-done.1.edge
  157.2 4.8 %input_back.1 = (f32[128,512]{1,0:T(8,128)}, f32[512,2048]{1,0:T(8,128)}, f32[1,512]{1,0:T(1,128)}) custom-call(bf16[128,512]{1,0:T(8,128)(2,1)} %bitcast.24, f32[1,512]{1,0:T(1,128)} %bitcast.32, bf16[512,2048]{1,0:T(8,128)(2,1)} %w_in.3, f32[128,1024]{1,0:T(8,128)} %get-tuple-element.73.own, f32[8,1024]{1,0:T(8,128)} %copy-done.10, ...), custom_call_target="tpu_custom_call" | custom-call | tf_op jit(solution)/shard_map/input_back/pallas_call | solution.py:453
  162.1 0.6 copy-done.12
  162.8 71.8 %all-reduce = (f32[512]{0:T(512)}, f32[4,1024]{1,0:T(4,128)}, f32[1024]{0:T(1024)}, f32[1024]{0:T(1024)}, f32[1024]{0:T(1024)}, /*index=5*/f32[512]{0:T(512)}) all-reduce(f32[512]{0:T(512)S(1)} %bitcast.39, f32[4,1024]{1,0:T(4,128)S(1)} %copy-done.12, ...), channel_id=1, replica_groups=mesh['y'=4,'core'=2,'seq'=4,'head'=4] {'y','core','seq','head'}, use_global_device_ids=true, to_apply=%region_0.0 | all-reduce | flops 8192 | bytes 65536 | tf_op jit(solution)/shard_map/psum | solution.py:535
  234.6 102.9 %all-reduce.4.cloned.1.call-done = (f32[512,2048]{1,0:T(8,128)}, f32[1024,64]{1,0:T(8,128)}, f32[32,1024]{1,0:T(8,128)}, f32[16,1024]{1,0:T(8,128)}, f32[1024,51...) async-done(((f32[512,2048]{1,0:T(8,128)}, f32[1024,64]{1,0:T(8,128)}, f32[32,1024]{1,0:T(8,128)}, ...) | async-done | bytes 10944528 | tf_op jit(solution)/shard_map/psum | solution.py:535
  337.6 1.9 copy.37
  339.5 4.8 %copy.47 = f32[512,2048]{1,0:T(8,128)} copy(f32[512,2048]{1,0:T(8,128)} %get-tuple-element.128) | data formatting | bytes 8388608
  344.4 0.7 copy.48
  345.7 1.3 copy.50
  347.6 1.0 copy.51
  348.6 1.0 copy.52
  349.6 1.0 copy.53
  350.5 1.0 copy.54
  (38 shorter events, 2.6 us)
Async XLA Ops:
  7.9 7.4 %collective-permute-start = (bf16[16,512]{1,0:T(8,128)(2,1)S(1)}, bf16[16,512]{1,0:T(8,128)(2,1)S(1)}, u32[]{:S(2)}, u32[]{:S(2)}) collective-permute-start(bf16[16,512]{1,0:T(8,128)(2,1)S(1)} %slice_bitcast_fusion), channel_id=1, source_target_pairs={{0,1},{1,2},{2,3},{3,4},{4,5},{5,6},{6,7},{7,8},{8,9},{9,10},{10,1... | collective-permute-start | bytes 49160 | tf_op jit(solution)/shard_map/ppermute | solution.py:466
  15.3 0.6 copy-start.11
  15.9 17.1 %copy-start.2 = (bf16[512,512]{1,0:T(8,128)(2,1)S(1)}, bf16[512,512]{1,0:T(8,128)(2,1)}, u32[]{:S(2)}) copy-start(bf16[512,512]{1,0:T(8,128)(2,1)} %w_o.1) | copy-start | bytes 1572868
  15.9 17.1 %copy-start.7 = (bf16[1,128,512]{2,1,0:T(8,128)(2,1)S(1)}, bf16[1,128,512]{2,1,0:T(8,128)(2,1)}, u32[]{:S(2)}) copy-start(bf16[1,128,512]{2,1,0:T(8,128)(2,1)} %param.35) | copy-start | bytes 393220
  25.7 19.9 %all-to-all-start = ((bf16[16,24,1024]{2,1,0:T(8,128)(2,1)}), bf16[16,24,1024]{2,1,0:T(8,128)(2,1)S(1)}, u32[]{:S(2)}, u32[]{:S(2)}) async-start(bf16[16,24,1024]{2,1,0:T(8,128)(2,1)} %broadcast_in_dim.8), calls=%async_computation | async-start | bytes 1572864 | tf_op jit(solution)/shard_map/all_to_all | solution.py:470
  32.9 304.7 %all-reduce.4.cloned.1.call-start = ((), (), s32[]{:S(2)}) async-start(), calls=%async_computation.4 | async-start | bytes 22413312 | tf_op jit(solution)/shard_map/psum | solution.py:535
  45.6 0.9 copy-start
  151.7 4.9 %collective-permute-start.1 = (f32[8,1024]{1,0:T(8,128)}, f32[8,1024]{1,0:T(8,128)S(1)}, u32[]{:S(2)}, u32[]{:S(2)}) collective-permute-start(f32[8,1024]{1,0:T(8,128)} %get-tuple-element.74), channel_id=1, source_target_pairs={{1,0},{2,1},{3,2},{4,3},{5,4},{6,5},{7,6},{8,7},{9,8},{10,9},{11,1... | collective-permute-start | bytes 98312 | tf_op jit(solution)/shard_map/ppermute | solution.py:466
  156.6 0.6 copy-start.10
  162.1 0.7 copy-start.12
  162.1 0.7 copy-start.13
  162.1 0.7 copy-start.14
  162.1 0.7 copy-start.15
  162.1 0.7 copy-start.16
  162.1 0.7 copy-start.17
  339.5 4.9 %copy-start.8 = (f32[32,1024]{1,0:T(8,128)S(1)}, f32[32,1024]{1,0:T(8,128)}, u32[]{:S(2)}) copy-start(f32[32,1024]{1,0:T(8,128)} %get-tuple-element.132) | copy-start | bytes 393220
  339.5 5.5 %copy-start.9 = (f32[16,1024]{1,0:T(8,128)S(1)}, f32[16,1024]{1,0:T(8,128)}, u32[]{:S(2)}) copy-start(f32[16,1024]{1,0:T(8,128)} %get-tuple-element.134) | copy-start | bytes 196612
  339.5 6.1 %copy-start.1 = (f32[1024,512]{1,0:T(8,128)S(1)}, f32[1024,512]{1,0:T(8,128)}, u32[]{:S(2)}) copy-start(f32[1024,512]{1,0:T(8,128)} %get-tuple-element.136) | copy-start | bytes 6291460
  345.7 2.0 copy-start.6
  345.7 2.9 copy-start.5
  347.6 1.9 copy-start.4
  348.6 1.9 copy-start.3
Sparse Core Ops, SparseCore 0:
  162.2 175.2 all-reduce.3
where the time goes:
time: 359 us; the launch traced here: 358 us
  waiting for transfers between devices  118 us (33%)
  blocking collectives  115 us (32%)
  Pallas kernels  73.8 us (21%)
  local copies, waits for them, and re-layouts  21.8 us (6%)
  between operations  14.2 us (4%)
  starting transfers between devices  12.8 us (4%)
    psum x1, waiting for transfers between devices, layer(): lax.psum((g_gain_one[0], gw_in, g_conv_w, g_conv_b[0], gw_x, gw_dt, g_dt_...  103 us
    pallas_call x6, Pallas kernels, call(): pl.pallas_call(body, name=name, out_shape=[jax.ShapeDtypeStruct(s, t) for...  73.8 us
    psum x1, blocking collectives, layer(): lax.psum((g_gain_one[0], gw_in, g_conv_w, g_conv_b[0], gw_x, gw_dt, g_dt_...  71.8 us
    all_to_all x3, blocking collectives, swap(): return lax.all_to_all(x, PLACE, 0, 0, tiled=True)  43.5 us
    unnamed x46, local copies, waits for them, and re-layouts  18.5 us
    all_to_all x1, waiting for transfers between devices, swap(): return lax.all_to_all(x, PLACE, 0, 0, tiled=True)  11.7 us
  transfers between devices with their start and end apart: 4, of which 3 were waited for; matrix products, arithmetic and copies ran while one was open for 1% of the time, Pallas kernels for 0%

commit v1 on v0

v1 whole, which is shorter than its diff:
```python
import functools

import jax
import jax.numpy as jnp
from jax import lax
from jax.experimental import pallas as pl
from jax.experimental.pallas import tpu as pltpu
from jax.sharding import Mesh, PartitionSpec as P

T, D, E, N, R, HD = 128, 512, 1024, 16, 32, 64
HEADS, BLOCKS, HALF, DOCS, KERNEL, HALO = 8, 16, 64, 6, 4, 16
LANES, STEPS = 128, 8
TILES = [slice(q * LANES, (q + 1) * LANES) for q in range(E // LANES)]
ROWS = T + HALF
RESET = 1e4
LOG2E = 1.4426950408889634
EPS = 1e-05
MASKED = -1e30
PLACE = ("seq", "head")
ALL = ("y", "core", "seq", "head")
SAME, SHARES, MAIN, SMALL = ("y", "seq", "head"), 64, 32, 8
bf16, f32, i32 = jnp.bfloat16, jnp.float32, jnp.int32


def mm(a, b):
    return jnp.dot(a, b, preferred_element_type=f32)


def mm_nt(a, b):
    return lax.dot_general(a, b, (((1,), (1,)), ((), ())), preferred_element_type=f32)


def mm_tn(a, b):
    return lax.dot_general(a, b, (((0,), (0,)), ((), ())), preferred_element_type=f32)


def doc_of(meta, pos):
    count = jnp.zeros(pos.shape, i32)
    for k in range(DOCS):
        count = count + (meta[2 + k] <= pos).astype(i32)
    return count


def reset_of(meta, pos):
    hit = meta[2] == pos
    for k in range(1, DOCS):
        hit = hit | (meta[2 + k] == pos)
    return jnp.where(hit, RESET, 0.0)


def inverse_rms(x):
    return lax.rsqrt(jnp.mean(x * x, axis=-1, keepdims=True) + EPS)


def sigmoid(x):
    return 1.0 / (1.0 + jnp.exp(-x))


def silu_slope(x):
    s = sigmoid(x)
    return s * (1.0 + x * (1.0 - s))


def norm_back(values, inverse, gain, upstream):
    scaled = upstream * gain
    inner = jnp.mean(values * scaled, axis=-1, keepdims=True)
    back = inverse * scaled - values * (inverse * inverse * inverse) * inner
    return back, jnp.sum(upstream * values * inverse, axis=0, keepdims=True)


def columns(offset, meta):
    first = meta[0]
    return first + offset + lax.broadcasted_iota(i32, (T, 1), 0)


def stack_sums(parts):
    row = lax.broadcasted_iota(i32, parts[0].shape, 0)
    for by in (1, 2, 4):
        first = (row & by) == 0
        parts = [
            jnp.where(first, a, b) + pltpu.roll(jnp.where(first, b, a), by, axis=0)
            for a, b in zip(parts[0::2], parts[1::2])
        ]
    return parts[0]


def column(block, low, k):
    return jnp.broadcast_to(block[low : low + N, k : k + 1], (N, LANES))


def halves(x):
    return x[0:8] + x[8:16]


def scan_forward(dec, sa, bc, rates2, start, result=None):
    def block(i, states):
        states = list(states)
        base = pl.multiple_of(i * STEPS, STEPS)
        cols = bc[i]
        sums = [[None] * STEPS for _ in TILES]
        for k in range(STEPS):
            b_col = column(cols, 0, k)
            c_col = column(cols, N, k)
            for q, tile in enumerate(TILES):
                factor = jnp.exp2(dec[pl.ds(base, STEPS), tile][k : k + 1] * rates2[:, tile])
                states[q] = factor * states[q] + b_col * sa[pl.ds(base, STEPS), tile][k : k + 1]
                if result is not None:
                    sums[q][k] = halves(states[q] * c_col)
        if result is not None:
            for q, tile in enumerate(TILES):
                result[pl.ds(base, STEPS), tile] = stack_sums(sums[q])
        return tuple(states)

    return lax.fori_loop(0, T // STEPS, block, tuple(start[:, tile] for tile in TILES))


def mamba_in(
    meta, tokens, halo, gain, w_in, conv_w, conv_b, w_x, w_dt, dt_b, a_log, cot, w_o,
    send, grad_att, low_out, ext_out, gate_out, conv_out, act_out, step_out, pre_out, bc_out, dt_out,
    ext, dec, sa, xp, end, rates2, zero,
):
    grad_att[...] = mm_nt(cot[...], w_o[...]).astype(bf16)
    own = tokens[...].astype(f32)
    before = halo[...].astype(f32)
    low_own = (own * inverse_rms(own) * gain[...]).astype(bf16)
    low_before = (before * inverse_rms(before) * gain[...]).astype(bf16)
    conv_own = mm(low_own, w_in[:, :E]).astype(bf16)
    conv_before = mm(low_before, w_in[:, :E]).astype(bf16)
    low_out[0:HALO] = low_before
    low_out[HALO : HALO + T] = low_own
    ext_out[0:HALO] = conv_before
    ext_out[HALO : HALO + T] = conv_own
    ext[0:HALO] = conv_before.astype(f32)
    ext[HALO : HALO + T] = conv_own.astype(f32)
    gate_out[...] = mm(low_own, w_in[:, E:]).astype(bf16)
    own_doc = doc_of(meta, columns(0, meta))
    conv = jnp.broadcast_to(conv_b[...], (T, E))
    for offset in range(KERNEL):
        same = (doc_of(meta, columns(offset - KERNEL + 1, meta)) == own_doc).astype(f32)
        low = HALO - KERNEL + 1 + offset
        conv = conv + conv_w[offset : offset + 1] * ext[low : low + T] * same
    conv_out[...] = conv
    act = (conv * sigmoid(conv)).astype(bf16)
    act_out[...] = act
    proj = mm_nt(act, w_x[...])
    dt_low = proj[:, :R].astype(bf16)
    dt_out[...] = dt_low
    pre = mm(dt_low, w_dt[...]) + dt_b[...]
    pre_out[...] = pre
    step = jnp.maximum(pre, 0.0) + jnp.log1p(jnp.exp(-jnp.abs(pre)))
    step_out[...] = step
    held = step + reset_of(meta, columns(0, meta))
    dec[...] = held
    sa[...] = step * act.astype(f32)
    xp[...] = jnp.zeros((T, 128), f32)
    xp[:, 0 : R + 2 * N] = proj
    turned = xp[...].T
    for i in range(T // STEPS):
        bc_out[i, :, 0:STEPS] = turned[R : R + 2 * N, i * STEPS : (i + 1) * STEPS]
    total = jnp.sum(held, axis=0, keepdims=True)
    high = total.astype(bf16)
    rest = (total - high.astype(f32)).astype(bf16)
    end[N : N + 8] = jnp.concatenate([high.astype(f32), rest.astype(f32), jnp.zeros((6, E), f32)], axis=0)
    rates2[...] = -jnp.exp(a_log[...]) * LOG2E
    zero[...] = jnp.zeros((N, E), f32)
    states = scan_forward(dec, sa, bc_out, rates2, zero)
    for q, tile in enumerate(TILES):
        end[0:N, tile] = states[q]
    ended = end[...].astype(bf16)
    for j in range(BLOCKS):
        send[j] = ended


def roll_half(x):
    return pltpu.roll(x, HALF, axis=1)


def mamba_out(
    meta, got, tokens, step, act, bc, gate, a_log, d_skip, w_out, gain, w_q, w_k, w_v, grad_att,
    send, start_out, ssm_out, gated_out, middle_out, normed_out,
    dec, sa, ssm, rates2,
):
    place = meta[1]
    rates2[...] = -jnp.exp(a_log[...]) * LOG2E
    dec[...] = step[...] + reset_of(meta, columns(0, meta))
    act_f = act[...].astype(f32)
    sa[...] = step[...] * act_f

    def join(j, state):
        tail = got[j, N : N + 8].astype(f32)
        total = tail[0:1] + tail[1:2]
        return jnp.exp2(rates2[...] * total) * state + got[j, 0:N].astype(f32)

    start_out[...] = lax.fori_loop(0, place, join, jnp.zeros((N, E), f32))
    scan_forward(dec, sa, bc, rates2, start_out, ssm)
    result = ssm[...] + d_skip[...] * act_f
    ssm_out[...] = result
    gates = gate[...].astype(f32)
    gated = (result * (gates * sigmoid(gates))).astype(bf16)
    gated_out[...] = gated
    middle = tokens[...].astype(f32) + mm(gated, w_out[...])
    middle_out[...] = middle
    normed = (middle * inverse_rms(middle) * gain[...]).astype(bf16)
    normed_out[...] = normed
    queries = mm(normed, w_q[...]).astype(bf16).astype(f32) * (HD ** -0.5)
    keys = mm(normed, w_k[...])
    vals = mm(normed, w_v[...])
    grads = grad_att[...].astype(f32)
    low = lax.broadcasted_iota(i32, (T, 128), 1) < HALF
    for m in range(HEADS // 2):
        tile = slice(m * 128, (m + 1) * 128)
        for odd in range(2):
            for first, second, at, rows in ((keys, vals, 0, T), (queries, grads, T, HALF)):
                a, b = first[:, tile], second[:, tile]
                pair = jnp.where(low, a, roll_half(b)) if odd == 0 else jnp.where(low, roll_half(a), b)
                pair = pair.astype(bf16)
                dest = 2 * (2 * m + odd)
                if rows == T:
                    send[dest, 0:T] = pair
                    send[dest + 1, 0:T] = pair
                else:
                    send[dest, T:ROWS] = pair[0:HALF]
                    send[dest + 1, T:ROWS] = pair[HALF:T]


QCHUNK, QBLOCKS = 256, 4


def attention(meta, got, send, kv_t, scores, grads, kv_grad):
    parity = lax.rem(meta[1], 2)
    for i in range(BLOCKS):
        kv_t[:, i * T : (i + 1) * T] = got[i, 0:T].astype(f32).T.astype(bf16)
    lane = lax.broadcasted_iota(i32, (1, QCHUNK), 1)
    low_q = lax.broadcasted_iota(i32, (QCHUNK, 128), 1) < HD
    low_k = lax.broadcasted_iota(i32, (T, 128), 1) < HD
    key_row = lax.broadcasted_iota(i32, (T, QCHUNK), 0)
    for c in range(BLOCKS // QBLOCKS):
        qg = jnp.concatenate([got[c * QBLOCKS + b, T:ROWS] for b in range(QBLOCKS)], axis=0)
        q_only = jnp.where(low_q, qg.astype(f32), 0.0).astype(bf16)
        g_only = jnp.where(low_q, 0.0, qg.astype(f32)).astype(bf16)
        pos = (c * QBLOCKS + lane // HALF) * T + parity * HALF + lane % HALF
        begin = jnp.zeros((1, QCHUNK), i32)
        for k in range(DOCS):
            begin = jnp.maximum(begin, jnp.where(meta[2 + k] <= pos, meta[2 + k], 0))
        tiles = (c + 1) * QBLOCKS
        top = jnp.full((8, QCHUNK), MASKED, f32)
        for i in range(tiles):
            s = mm_nt(got[i, 0:T], q_only)
            allowed = key_row >= begin - i * T
            if i >= c * QBLOCKS:
                allowed = allowed & (key_row <= pos - i * T)
            s = jnp.where(allowed, s, MASKED)
            scores[i] = s
            top = jnp.maximum(top, jnp.max(s.reshape(T // 8, 8, QCHUNK), axis=0))
        top = jnp.max(top, axis=0, keepdims=True)
        total = jnp.zeros((8, QCHUNK), f32)
        cross = jnp.zeros((8, QCHUNK), f32)
        for i in range(tiles):
            p = jnp.exp2((scores[i] - top) * LOG2E)
            scores[i] = p
            g = mm_nt(got[i, 0:T], g_only)
            grads[i] = g
            total = total + jnp.sum(p.reshape(T // 8, 8, QCHUNK), axis=0)
            cross = cross + jnp.sum((p * g).reshape(T // 8, 8, QCHUNK), axis=0)
        inverse = 1.0 / jnp.sum(total, axis=0, keepdims=True)
        cross = jnp.sum(cross, axis=0, keepdims=True) * inverse
        out_t = jnp.zeros((128, QCHUNK), f32)
        dq_t = jnp.zeros((128, QCHUNK), f32)
        for i in range(tiles):
            prob = scores[i] * inverse
            low_p = prob.astype(bf16)
            low_s = (prob * (grads[i] - cross)).astype(bf16)
            turned = kv_t[:, i * T : (i + 1) * T]
            out_t = out_t + mm(turned, low_p)
            dq_t = dq_t + mm(turned, low_s)
            both = jnp.where(low_k, mm(low_s, qg), mm(low_p, qg))
            if i >= c * QBLOCKS:
                kv_grad[i] = both
            else:
                kv_grad[i] = kv_grad[i] + both
        pair = jnp.where(low_q, dq_t.T * (HD ** -0.5), out_t.T).astype(bf16)
        for b in range(QBLOCKS):
            send[c * QBLOCKS + b, T:ROWS] = pair[b * HALF : (b + 1) * HALF]
    for i in range(BLOCKS):
        send[i, 0:T] = kv_grad[i].astype(bf16)


def middle_back(
    meta, got, cot, middle, normed, low_ext, gated, gate, ssm, act, step, bc, a_log, d_skip,
    w_o, w_q, w_k, w_v, w_out, gain,
    send, mixed, grad_mid_out, g_out, grad_gate_out, keep, give, g_gain, g_skip,
    att, dq, dk, dv, dec, end, rates2,
):
    low = lax.broadcasted_iota(i32, (HALF, 128), 1) < HALF
    low_t = lax.broadcasted_iota(i32, (T, 128), 1) < HALF
    for m in range(HEADS // 2):
        tile = slice(m * 128, (m + 1) * 128)
        for p in range(2):
            a = got[4 * m + p, T:ROWS].astype(f32)
            b = got[4 * m + 2 + p, T:ROWS].astype(f32)
            rows = slice(p * HALF, (p + 1) * HALF)
            dq[rows, tile] = jnp.where(low, a, roll_half(b)).astype(bf16)
            att[rows, tile] = jnp.where(low, roll_half(a), b).astype(bf16)
        a = got[4 * m, 0:T].astype(f32) + got[4 * m + 1, 0:T].astype(f32)
        b = got[4 * m + 2, 0:T].astype(f32) + got[4 * m + 3, 0:T].astype(f32)
        dk[:, tile] = jnp.where(low_t, a, roll_half(b)).astype(bf16)
        dv[:, tile] = jnp.where(low_t, roll_half(a), b).astype(bf16)
    cot_low = cot[...]
    values = middle[...]
    mixed[...] = (values + mm(att[...], w_o[...])).astype(bf16)
    upstream = mm_nt(dq[...], w_q[...]) + mm_nt(dk[...], w_k[...]) + mm_nt(dv[...], w_v[...])
    back, gain_grad = norm_back(values, inverse_rms(values), gain[...], upstream)
    g_gain[...] = gain_grad
    grad_mid = cot_low.astype(f32) + back
    grad_mid_out[...] = grad_mid
    mid_low = grad_mid.astype(bf16)
    grad_gated = mm_nt(mid_low, w_out[...]).astype(bf16).astype(f32)
    gates = gate[...].astype(f32)
    sig = sigmoid(gates)
    g = grad_gated * (gates * sig)
    g_out[...] = g
    grad_gate = (grad_gated * ssm[...] * (sig * (1.0 + gates * (1.0 - sig)))).astype(bf16)
    grad_gate_out[...] = grad_gate
    for first, second, core in ((keep, give, 0), (give, keep, 1)):

        @pl.when(meta[2 + DOCS] == core)
        def _():
            first[:, 0:D] = att[...]
            first[:, D : 2 * D] = cot_low
            first[:, 2 * D : 3 * D] = normed[...]
            first[:, 3 * D : 4 * D] = dq[...]
            first[:, 4 * D : 5 * D] = dk[...]
            first[:, 5 * D : 6 * D] = dv[...]
            second[:, 0:E] = gated[...]
            second[:, E : E + D] = mid_low
            second[:, E + D : 2 * E] = low_ext[HALO : HALO + T]
            second[:, 2 * E : 3 * E] = grad_gate

    g_skip[...] = jnp.sum(g * act[...].astype(f32), axis=0, keepdims=True)
    dec[...] = step[...] + reset_of(meta, columns(0, meta))
    rates2[...] = -jnp.exp(a_log[...]) * LOG2E

    def block(turn, carry):
        carry = list(carry)
        i = T // STEPS - 1 - turn
        base = pl.multiple_of(i * STEPS, STEPS)
        cols = bc[i]
        for k in reversed(range(STEPS)):
            c_col = column(cols, N, k)
            for q, tile in enumerate(TILES):
                factor = jnp.exp2(dec[pl.ds(base, STEPS), tile][k : k + 1] * rates2[:, tile])
                carry[q] = factor * (carry[q] + c_col * g_out[pl.ds(base, STEPS), tile][k : k + 1])
        return tuple(carry)

    carry = lax.fori_loop(0, T // STEPS, block, tuple(jnp.zeros((N, LANES), f32) for _ in TILES))
    for q, tile in enumerate(TILES):
        end[:, tile] = carry[q]
    ended = end[...].astype(bf16)
    for j in range(BLOCKS):
        send[j] = ended


def mamba_back(
    meta, got, forward, start, g, act, step, pre, bc, dt_low, conv, ext_low, a_log, d_skip,
    conv_w, w_x, w_dt, tokens, halo, gain, w_in, grad_gate, grad_mid, g_gain_two, g_skip,
    grad_tokens, tail, keep, give, part_keep,
    dec, sa, decay, kept, gs, ab, ext, padded, grad_ext, vec, wide, rates, rates2, sum_b, sum_c,
):
    place = meta[1]
    dec[...] = step[...] + reset_of(meta, columns(0, meta))
    act_f = act[...].astype(f32)
    sa[...] = step[...] * act_f
    rates[...] = -jnp.exp(a_log[...])
    rates2[...] = rates[...] * LOG2E

    def join(turn, state):
        j = BLOCKS - 1 - turn
        tail = forward[j, N : N + 8].astype(f32)
        total = tail[0:1] + tail[1:2]
        return jnp.exp2(rates2[...] * total) * state + got[j].astype(f32)

    wide[R : R + N] = lax.fori_loop(0, BLOCKS - 1 - place, join, jnp.zeros((N, E), f32))

    def ahead(i, states):
        states = list(states)
        base = pl.multiple_of(i * STEPS, STEPS)
        cols = bc[i]
        for k in range(STEPS):
            b_col = column(cols, 0, k)
            total = jnp.zeros((N, LANES), f32)
            for q, tile in enumerate(TILES):
                rows = pl.ds(base, STEPS), tile
                factor = jnp.exp2(dec[rows][k : k + 1] * rates2[:, tile])
                moved = factor * states[q]
                decay[base + k, :, tile] = factor
                kept[base + k, :, tile] = moved
                states[q] = moved + b_col * sa[rows][k : k + 1]
                total = total + states[q] * g[rows][k : k + 1]
            sum_c[base + k] = total
        return tuple(states)

    lax.fori_loop(0, T // STEPS, ahead, tuple(start[:, tile] for tile in TILES))
    first_carry = tuple(wide[R : R + N, tile] for tile in TILES)
    wide[R + N : R + 2 * N] = jnp.zeros((N, E), f32)

    def behind(turn, carry):
        carry = list(carry)
        i = T // STEPS - 1 - turn
        base = pl.multiple_of(i * STEPS, STEPS)
        cols = bc[i]
        by_rate = [[None] * STEPS for _ in TILES]
        by_b = [[None] * STEPS for _ in TILES]
        along = [wide[R + N : R + 2 * N, tile] for tile in TILES]
        for k in reversed(range(STEPS)):
            b_col = column(cols, 0, k)
            c_col = column(cols, N, k)
            total = jnp.zeros((N, LANES), f32)
            for q, tile in enumerate(TILES):
                rows = pl.ds(base, STEPS), tile
                adjoint = g[rows][k : k + 1] * c_col + carry[q]
                carry[q] = decay[base + k, :, tile] * adjoint
                log_grad = adjoint * kept[base + k, :, tile]
                along[q] = along[q] + log_grad * step[rows][k : k + 1]
                by_rate[q][k] = halves(log_grad * rates[:, tile])
                by_b[q][k] = halves(adjoint * b_col)
                total = total + adjoint * sa[rows][k : k + 1]
            sum_b[base + k] = total
        for q, tile in enumerate(TILES):
            wide[R + N : R + 2 * N, tile] = along[q]
            gs[pl.ds(base, STEPS), tile] = stack_sums(by_rate[q])
            ab[pl.ds(base, STEPS), tile] = stack_sums(by_b[q])
        return tuple(carry)

    lax.fori_loop(0, T // STEPS, behind, first_carry)
    wide[R : R + N] = wide[R + N : R + 2 * N] * rates[...]
    lane = lax.broadcasted_iota(i32, (LANES, LANES), 1)
    turned = jnp.zeros((T, LANES), f32)
    for at, sums in ((0, sum_b), (N, sum_c)):
        for n in range(N):
            one = (lane == at + n).astype(f32).astype(bf16)
            values = sums[:, n, :]
            high = values.astype(bf16)
            turned = turned + mm(high, one) + mm((values - high.astype(f32)).astype(bf16), one)
    adjoint_b = ab[...]
    grad_step = gs[...] + adjoint_b * act_f
    grad_act = g[...] * d_skip[...] + adjoint_b * step[...]
    grad_pre = (grad_step * sigmoid(pre[...])).astype(bf16)
    vec[...] = jnp.zeros((N, E), f32)
    vec[KERNEL + 1 : KERNEL + 2] = jnp.sum(grad_pre.astype(f32), axis=0, keepdims=True)
    vec[KERNEL + 2 : KERNEL + 3] = g_skip[...]
    wide[0:R] = mm_tn(dt_low[...], grad_pre)
    grad_proj = jnp.concatenate([mm_nt(grad_pre, w_dt[...]), turned[:, 0 : 2 * N]], axis=1).astype(bf16)
    gw_x = mm_tn(grad_proj, act[...])
    grad_act = grad_act + mm(grad_proj, w_x[...])
    grad_conv = grad_act * silu_slope(conv[...])
    vec[KERNEL : KERNEL + 1] = jnp.sum(grad_conv, axis=0, keepdims=True)
    padded[0:T] = grad_conv
    padded[T : T + 8] = jnp.zeros((8, E), f32)
    ext[...] = ext_low[...].astype(f32)
    own_doc = doc_of(meta, columns(0, meta))
    own = jnp.zeros((T, E), f32)
    lift = KERNEL - 1
    rows = lax.broadcasted_iota(i32, (T, 1), 0)
    for offset in range(KERNEL):
        same = (doc_of(meta, columns(offset - lift, meta)) == own_doc).astype(f32)
        low = HALO - lift + offset
        vec[offset : offset + 1] = jnp.sum(grad_conv * ext[low : low + T] * same, axis=0, keepdims=True)
        up = lift - offset
        ahead_same = (doc_of(meta, columns(0, meta)) == doc_of(meta, columns(up, meta))) & (rows < T - up)
        own = own + conv_w[offset : offset + 1] * padded[up : up + T] * ahead_same.astype(f32)
    grad_ext[HALO : HALO + T] = own
    first = meta[0]
    edges = [jnp.zeros((HALO - lift, E), f32)]
    for row in range(lift):
        edge = jnp.zeros((1, E), f32)
        here = doc_of(meta, first - lift + row + jnp.zeros((1, 1), i32))
        for offset in range(row + 1):
            at = row - offset
            same = (doc_of(meta, first + at + jnp.zeros((1, 1), i32)) == here).astype(f32)
            edge = edge + conv_w[offset : offset + 1] * padded[at : at + 1] * same
        edges.append(edge)
    grad_ext[0:HALO] = jnp.concatenate(edges, axis=0)
    low_edge = grad_ext[0:HALO].astype(bf16)
    low_own = grad_ext[HALO : HALO + T].astype(bf16)
    values = tokens[...].astype(f32)
    upstream = mm_nt(low_own, w_in[:, :E]) + mm_nt(grad_gate[...], w_in[:, E:])
    back, gain_own = norm_back(values, inverse_rms(values), gain[...], upstream)
    grad_tokens[...] = grad_mid[...] + back
    before = halo[...].astype(f32)
    back, gain_edge = norm_back(before, inverse_rms(before), gain[...], mm_nt(low_edge, w_in[:, :E]))
    tail[...] = back[HALO - 8 : HALO]
    vec[KERNEL + 3 : KERNEL + 4, 0:D] = gain_own + gain_edge
    vec[KERNEL + 3 : KERNEL + 4, D:E] = g_gain_two[...]
    wide[R + N : R + 2 * N] = vec[...]
    for core in range(2):

        @pl.when(meta[2 + DOCS] == core)
        def _():
            for j in range(D // 128):
                cols = slice(core * D + j * 128, core * D + (j + 1) * 128)
                keep[0:HALO, j * 128 : (j + 1) * 128] = low_edge[:, cols]
                keep[HALO : HALO + T, j * 128 : (j + 1) * 128] = low_own[:, cols]
                cols = slice((1 - core) * D + j * 128, (1 - core) * D + (j + 1) * 128)
                base = j * (HALO + T)
                give[base : base + HALO] = low_edge[:, cols]
                give[base + HALO : base + HALO + T] = low_own[:, cols]
            base = D // 128 * (HALO + T)
            for j in range(E // 128):
                cols = slice(j * 128, (j + 1) * 128)
                mine, other = (gw_x, wide) if core == 0 else (wide, gw_x)
                part_keep[j * 64 : (j + 1) * 64] = mine[:, cols]
                give[base + j * 64 : base + (j + 1) * 64] = other[:, cols].astype(bf16)


def early_weights(meta, keep, got, out, both):
    both[0:T] = keep[...]
    both[T : 2 * T] = got[...]
    left_right = (((0, 1), (2, 3), (2, 4), (2, 5)), ((0, 2), (1, 2), (3, 4), (3, 5)))
    for core in range(2):

        @pl.when(meta[2 + DOCS] == core)
        def _():
            for j, (a, b) in enumerate(left_right[core]):
                left, right = both[:, a * D : (a + 1) * D], both[:, b * D : (b + 1) * D]
                result = mm_tn(left, right).astype(bf16)
                for q in range(D // LANES):
                    out[(4 * j + q) * D : (4 * j + q + 1) * D] = result[:, q * LANES : (q + 1) * LANES]


def late_weights(keep, part_keep, low_own, low_other, got, out, whole):
    left = jnp.concatenate([low_own[...], low_other[...]], axis=0)
    rows = HALO + T
    for j in range(D // LANES):
        right = jnp.concatenate([keep[:, j * LANES : (j + 1) * LANES], got[j * rows : (j + 1) * rows]], axis=0)
        whole[j * D : (j + 1) * D] = mm_tn(left, right)
    base = D // LANES * rows
    whole[4 * D : 5 * D] = part_keep[...] + got[base : base + D].astype(f32)
    for d in range(SHARES):
        main = whole[d * MAIN : (d + 1) * MAIN]
        small = whole[4 * D + d * SMALL : 4 * D + (d + 1) * SMALL]
        out[d] = jnp.concatenate([main, small], axis=0).astype(bf16)


def add_up(early, late, out):
    first = early[0].astype(f32)
    second = late[0].astype(f32)
    for j in range(1, SHARES):
        first = first + early[j].astype(f32)
        second = second + late[j].astype(f32)
    low = jnp.concatenate([first, second], axis=0).astype(bf16)
    for j in range(SHARES):
        out[j] = low


def finish(meta, mine, other, gw_o, gw_q, gw_k, gw_v, gw_out, gw_in, gw_x, gw_dt, g_a_log, vec):
    is_zero = meta[2 + DOCS] == 0
    for d in range(SHARES):
        a, b = mine[d].astype(f32), other[d].astype(f32)
        zero = jnp.where(is_zero, a, b)
        one = jnp.where(is_zero, b, a)
        j, q, r = d // 16, d // 4 % 4, d % 4 * T
        tile = TILES[q]
        (gw_o, gw_q, gw_k, gw_v)[j][r : r + T, tile] = zero[0:T]
        if j < 2:
            gw_out[j * D + r : j * D + r + T, tile] = one[0:T]
        else:
            low = E + (j - 2) * D + q * LANES
            gw_in[r : r + T, low : low + LANES] = one[0:T]
        r = d % 16 * MAIN
        gw_in[r : r + MAIN, j * LANES : (j + 1) * LANES] = zero[T : T + MAIN]
        gw_in[r : r + MAIN, D + j * LANES : D + (j + 1) * LANES] = one[T : T + MAIN]
        tile, r = TILES[d // 8], d % 8 * SMALL
        gw_x[r : r + SMALL, tile] = zero[T + MAIN :]
        for out, low, high in ((gw_dt, 0, R), (g_a_log, R, R + N), (vec, R + N, R + 2 * N)):
            if low <= r < high:
                out[r - low : r - low + SMALL, tile] = one[T + MAIN :]


def call(body, name, outs, scratch, *args, smem=True):
    specs = [pl.BlockSpec(memory_space=pltpu.VMEM)] * len(args)
    if smem:
        specs[0] = pl.BlockSpec(memory_space=pltpu.SMEM)
    return pl.pallas_call(
        body,
        name=name,
        out_shape=[jax.ShapeDtypeStruct(s, t) for s, t in outs],
        in_specs=specs,
        out_specs=[pl.BlockSpec(memory_space=pltpu.VMEM)] * len(outs),
        scratch_shapes=[pltpu.VMEM(s, t) for s, t in scratch],
        compiler_params=pltpu.CompilerParams(vmem_limit_bytes=56 * 1024 * 1024),
    )(*args)


def shift(x, by):
    pairs = [(i, i + by) for i in range(BLOCKS) if 0 <= i + by < BLOCKS]
    return lax.ppermute(x, PLACE, pairs)


def swap(x):
    return lax.all_to_all(x, PLACE, 0, 0, tiled=True)


def partner(x):
    return lax.ppermute(x, "core", [(0, 1), (1, 0)])


def trade(x):
    return lax.all_to_all(x, SAME, 0, 0, tiled=True)


def layer(
    tokens, starts, gain_one, w_in, conv_w, conv_b, w_x, w_dt, dt_bias, a_log, d_skip, w_out,
    gain_two, w_q, w_k, w_v, w_o, cotangent,
):
    tokens, cot = tokens[0], cotangent[0]
    place = lax.axis_index(PLACE)
    core = lax.axis_index("core").astype(i32)
    meta = jnp.concatenate([jnp.stack([place * T, place]).astype(i32), starts[0], core[None]])
    row = lambda v: v.reshape(1, -1)
    halo = shift(tokens[T - HALO :], 1)
    tn = ((N, E), f32)
    te, tel, td, tdl = ((T, E), f32), ((T, E), bf16), ((T, D), f32), ((T, D), bf16)
    w_x = w_x.T
    send, grad_att, low_ext, ext, gate, conv, act, step, pre, bc, dt_low = call(
        mamba_in, "mamba_in",
        [((BLOCKS, N + 8, E), bf16), tdl, ((HALO + T, D), bf16), ((HALO + T, E), bf16), tel, te, tel, te, te,
         ((T // STEPS, 2 * N, 128), f32), ((T, R), bf16)],
        [((HALO + T, E), f32), te, te, ((T, 128), f32), ((N + 8, E), f32), tn, tn],
        meta, tokens, halo, row(gain_one), w_in, conv_w, row(conv_b), w_x, w_dt, row(dt_bias), a_log, cot, w_o,
    )
    low_other = partner(low_ext)
    forward = swap(send)
    packed, start, ssm, gated, middle, normed = call(
        mamba_out, "mamba_out",
        [((BLOCKS, ROWS, 128), bf16), ((N, E), f32), te, tel, td, tdl],
        [te, te, te, tn],
        meta, forward, tokens, step, act, bc, gate, a_log, row(d_skip), w_out, row(gain_two),
        w_q, w_k, w_v, grad_att,
    )
    (back,) = call(
        attention, "attention",
        [((BLOCKS, ROWS, 128), bf16)],
        [((128, BLOCKS * T), bf16), ((BLOCKS, T, QCHUNK), f32), ((BLOCKS, T, QCHUNK), f32),
         ((BLOCKS, T, 128), f32)],
        meta, swap(packed),
    )
    wide = ((T, 6 * D), bf16)
    send, mixed, grad_mid, g, grad_gate, keep, give, g_gain_two, g_skip = call(
        middle_back, "middle_back",
        [((BLOCKS, N, E), bf16), tdl, td, te, tel, wide, wide, ((1, D), f32), ((1, E), f32)],
        [tdl] * 4 + [te, tn, tn],
        meta, swap(back), cot, middle, normed, low_ext, gated, gate, ssm, act, step, bc, a_log,
        row(d_skip), w_o, w_q, w_k, w_v, w_out, row(gain_two),
    )
    (early,) = call(
        early_weights, "early_weights", [((16 * D, LANES), bf16)], [((2 * T, 6 * D), bf16)],
        meta, keep, partner(give),
    )
    early, behind = lax.optimization_barrier((early, swap(send)))
    early = trade(early.reshape(SHARES, T, LANES))
    grad_tokens, tail, keep, give, part_keep = call(
        mamba_back, "mamba_back",
        [td, ((8, D), f32), ((HALO + T, D), bf16), ((4 * (HALO + T) + D, 128), bf16), ((D, 128), f32)],
        [te, te, ((T, N, E), f32), ((T, N, E), f32), te, te, ((HALO + T, E), f32),
         ((T + 8, E), f32), ((HALO + T, E), f32), ((N, E), f32), ((64, E), f32), tn, tn,
         ((T, N, LANES), f32), ((T, N, LANES), f32)],
        meta, behind, forward, start, g, act, step, pre, bc, dt_low, conv, ext, a_log,
        row(d_skip), conv_w, w_x, w_dt, tokens, halo, row(gain_one), w_in, grad_gate, grad_mid,
        g_gain_two, g_skip,
    )
    (late,) = call(
        late_weights, "late_weights", [((SHARES, MAIN + SMALL, LANES), bf16)], [((5 * D, LANES), f32)],
        keep, part_keep, low_ext, low_other, partner(give), smem=False,
    )
    early, late = lax.optimization_barrier((early, late))
    late = trade(late)
    (total,) = call(
        add_up, "add_up", [((SHARES, T + MAIN + SMALL, LANES), bf16)], [], early, late, smem=False
    )
    total = trade(total)
    gw_o, gw_q, gw_k, gw_v, gw_out, gw_in, gw_x, gw_dt, g_a_log, vec = call(
        finish, "finish",
        [((D, D), f32)] * 4 + [((E, D), f32), ((D, 2 * E), f32), ((64, E), f32), ((R, E), f32), tn, tn],
        [],
        meta, total, partner(total),
    )
    grad_tokens = grad_tokens.at[T - 8 :].add(shift(tail, -1))
    return (
        mixed[None], grad_tokens[None], vec[KERNEL + 3, 0:D], gw_in, vec[0:KERNEL], vec[KERNEL], gw_x.T,
        gw_dt, vec[KERNEL + 1], g_a_log, vec[KERNEL + 2], gw_out, vec[KERNEL + 3, D:E], gw_q, gw_k,
        gw_v, gw_o,
    )


def solution(mesh):
    rows, seq, head = mesh.devices.shape
    fine = Mesh(mesh.devices.reshape(rows // 2, 2, seq, head), ALL)
    split = P(("y", "core"), PLACE, None)
    return jax.shard_map(
        layer,
        mesh=fine,
        in_specs=(split, P(("y", "core"), None)) + (P(),) * 15 + (split,),
        out_specs=(split, split) + (P(),) * 15,
        check_vma=False,
    )
```

time: 359 us -> 232 us (0.65)
  waiting for transfers between devices: 118 us -> 11.1 us
  starting transfers between devices: 12.8 us -> 27.6 us
  between operations: 14.2 us -> 0.78 us
  local copies, waits for them, and re-layouts: 21.8 us -> 8.71 us
  Pallas kernels: 73.8 us -> 69.8 us
  blocking collectives: 115 us -> 111 us
    psum x1 -> x0, waiting for transfers between devices: 103 us -> none  [layer(): lax.psum((g_gain_one[0], gw_in, g_conv_w, g_conv_b[0], gw_x, gw_dt, g_dt_...]
    psum x1 -> x0, blocking collectives: 71.8 us -> none  [layer(): lax.psum((g_gain_one[0], gw_in, g_conv_w, g_conv_b[0], gw_x, gw_dt, g_dt_...]
    all_to_all x0 -> x2, blocking collectives: none -> 62.9 us  [trade(): return lax.all_to_all(x, SAME, 0, 0, tiled=True)]
    unnamed x46 -> x25, local copies, waits for them, and re-layouts: 18.5 us -> 3.82 us
    ppermute x0 -> x4, starting transfers between devices: none -> 10.8 us  [partner(): return lax.ppermute(x, 'core', [(0, 1), (1, 0)])]
    all_to_all x0 -> x1, starting transfers between devices: none -> 7.65 us  [trade(): return lax.all_to_all(x, SAME, 0, 0, tiled=True)]
    all_to_all x1, waiting for transfers between devices: 11.7 us -> 6.04 us  [swap(): return lax.all_to_all(x, PLACE, 0, 0, tiled=True)]
    all_to_all x3, blocking collectives: 43.5 us -> 48.2 us  [swap(): return lax.all_to_all(x, PLACE, 0, 0, tiled=True)]
  transfers between devices with their start and end apart: 4 -> 8, of which waited for: 3 -> 5; matrix products, arithmetic and copies ran while one was open for 1% -> 1% of each run, Pallas kernels for 0% -> 12%
where the time goes in v1:
time: 232 us; the launch traced here: 230 us
  blocking collectives  111 us (48%)
  Pallas kernels  69.8 us (30%)
  starting transfers between devices  27.6 us (12%)
  waiting for transfers between devices  11.1 us (5%)
  local copies, waits for them, and re-layouts  8.71 us (4%)
    pallas_call x9, Pallas kernels, call(): pl.pallas_call(body, name=name, out_shape=[jax.ShapeDtypeStruct(s, t) for...  69.8 us
    all_to_all x2, blocking collectives, trade(): return lax.all_to_all(x, SAME, 0, 0, tiled=True)  62.9 us
    all_to_all x3, blocking collectives, swap(): return lax.all_to_all(x, PLACE, 0, 0, tiled=True)  48.2 us
    ppermute x4, starting transfers between devices, partner(): return lax.ppermute(x, 'core', [(0, 1), (1, 0)])  10.8 us
    all_to_all x1, starting transfers between devices, trade(): return lax.all_to_all(x, SAME, 0, 0, tiled=True)  7.65 us
    all_to_all x1, waiting for transfers between devices, swap(): return lax.all_to_all(x, PLACE, 0, 0, tiled=True)  6.04 us
    ppermute x2, starting transfers between devices, shift(): return lax.ppermute(x, PLACE, pairs)  5.64 us
  transfers between devices with their start and end apart: 8, of which 5 were waited for; matrix products, arithmetic and copies ran while one was open for 1% of the time, Pallas kernels for 12%

profile of v1, /device:TPU:1, one launch (start us, length us, event | category | flops | bytes accessed | tf_op | source)
XLA Modules:
  0.0 230.3 jit_solution(6260155961976386646)
XLA Ops:
  0.7 0.7 slice_bitcast_fusion
  1.4 4.4 %collective-permute-start = (bf16[16,512]{1,0:T(8,128)(2,1)S(1)}, bf16[16,512]{1,0:T(8,128)(2,1)S(1)}, u32[]{:S(2)}, u32[]{:S(2)}) collective-permute-start(bf16[16,512]{1,0:T(8,128)(2,1)S(1)} %slice_bitcast_fusion), channel_id=1, source_target_pairs={{0,1},{1,2},{2,3},{3,4},{4,5},{5,6},{6,7},{7,8},{8,9},{9,10},{10,1... | collective-permute-start | bytes 49160 | tf_op jit(solution)/shard_map/ppermute | solution.py:596
  5.8 1.2 pad_add_fusion.meta
  7.6 7.5 %mamba_in.1 = (bf16[16,24,1024]{2,1,0:T(8,128)(2,1)}, bf16[128,512]{1,0:T(8,128)(2,1)}, bf16[144,512]{1,0:T(8,128)(2,1)}, bf16[144,1024]{1,0:T(8,128)(2,1)}, bf1...) custom-call(s32[9]{0:T(128)} %pad_add_fusion.meta, ...), custom_call_target="tpu_custom_call" | custom-call | tf_op jit(solution)/shard_map/mamba_in/pallas_call | solution.py:583
  15.1 19.1 %all_to_all.35.got.forward = bf16[16,24,1024]{2,1,0:T(8,128)(2,1)} all-to-all(bf16[16,24,1024]{2,1,0:T(8,128)(2,1)} %get-tuple-element.74), channel_id=1, replica_groups=mesh['y'=4,'core'=2,'seq'=4,'head'=4] {'seq','head'}, dimensions={0} | all-to-all | bytes 1572864 | tf_op jit(solution)/shard_map/all_to_all | solution.py:600
  34.2 7.4 %mamba_out.1 = (bf16[16,192,128]{2,1,0:T(8,128)(2,1)}, f32[16,1024]{1,0:T(8,128)}, f32[128,1024]{1,0:T(8,128)}, bf16[128,1024]{1,0:T(8,128)(2,1)}, f32[128,512]{1,0:T(8,128)}, /*index=5*/bf16[128,512]{1,0:T(8,128)(2,1)}) custom-call(s32[9]{0:T(128)} %pad_add_fusion.meta, bf16[16,24,1024]{2,1,0:T(8,128)(2,1)} %all_to_all.35.got.forward, ...), custom_call_target="tpu_custom_call" | custom-call | tf_op jit(solution)/shard_map/mamba_out/pallas_call | solution.py:583
  41.5 14.7 %all_to_all.36.got = bf16[16,192,128]{2,1,0:T(8,128)(2,1)} all-to-all(bf16[16,192,128]{2,1,0:T(8,128)(2,1)} %get-tuple-element.80), channel_id=1, replica_groups=mesh['y'=4,'core'=2,'seq'=4,'head'=4] {'seq','head'}, dimensions={0} | all-to-all | bytes 1572864 | tf_op jit(solution)/shard_map/all_to_all | solution.py:600
  56.2 8.5 %attention.1 = bf16[16,192,128]{2,1,0:T(8,128)(2,1)} custom-call(s32[9]{0:T(128)} %pad_add_fusion.meta, bf16[16,192,128]{2,1,0:T(8,128)(2,1)} %all_to_all.36.got), custom_call_target="tpu_custom_call" | custom-call | tf_op jit(solution)/shard_map/attention/pallas_call | solution.py:583
  64.7 14.5 %all_to_all.37.got = bf16[16,192,128]{2,1,0:T(8,128)(2,1)} all-to-all(bf16[16,192,128]{2,1,0:T(8,128)(2,1)} %attention.1), channel_id=1, replica_groups=mesh['y'=4,'core'=2,'seq'=4,'head'=4] {'seq','head'}, dimensions={0} | all-to-all | bytes 1572864 | tf_op jit(solution)/shard_map/all_to_all | solution.py:600
  79.2 8.6 %middle_back.1 = (bf16[16,16,1024]{2,1,0:T(8,128)(2,1)}, bf16[128,512]{1,0:T(8,128)(2,1)}, f32[128,512]{1,0:T(8,128)}, f32[128,1024]{1,0:T(8,128)}, bf16[128,102...) custom-call(s32[9]{0:T(128)} %pad_add_fusion.meta, ...), custom_call_target="tpu_custom_call" | custom-call | tf_op jit(solution)/shard_map/middle_back/pallas_call | solution.py:583
  87.8 5.9 %collective-permute-start.1 = (bf16[128,3072]{1,0:T(8,128)(2,1)}, bf16[128,3072]{1,0:T(8,128)(2,1)S(1)}, u32[]{:S(2)}, u32[]{:S(2)}) collective-permute-start(bf16[128,3072]{1,0:T(8,128)(2,1)} %get-tuple-element.88), channel_id=1, source_target_pairs={{0,16},{16,0},{1,17},{17,1},{2,18},{18,2},{3,19},{19,3},{4,20},{20... | collective-permute-start | bytes 2359304 | tf_op jit(solution)/shard_map/ppermute | solution.py:604
  93.7 3.6 %all-to-all-start.3 = ((bf16[16,16,1024]{2,1,0:T(8,128)(2,1)}), bf16[16,16,1024]{2,1,0:T(8,128)(2,1)S(1)}, u32[]{:S(2)}, u32[]{:S(2)}) async-start(bf16[16,16,1024]{2,1,0:T(8,128)(2,1)} %get-tuple-element.89), calls=%async_computation.3 | async-start | bytes 1048576 | tf_op jit(solution)/shard_map/all_to_all | solution.py:600
  97.3 0.9 copy-done.4
  98.2 3.6 %early_weights.1 = bf16[8192,128]{1,0:T(8,128)(2,1)} custom-call(s32[9]{0:T(128)} %pad_add_fusion.meta, bf16[128,3072]{1,0:T(8,128)(2,1)} %get-tuple-element.87.keep, bf16[128,3072]{1,0:T(8,128)(2,1)} %copy-done.4), custom_call_target="tpu_custom_call" | custom-call | tf_op jit(solution)/shard_map/early_weights/pallas_call | solution.py:583
  101.8 6.0 %all-to-all-done.3.got = bf16[16,16,1024]{2,1,0:T(8,128)(2,1)S(1)} async-done(((bf16[16,16,1024]{2,1,0:T(8,128)(2,1)}), bf16[16,16,1024]{2,1,0:T(8,128)(2,1)S(1)}, u32[]{:S(2)}, u32[]{:S(2)}) %all-to-all-start.3) | async-done | bytes 524320 | tf_op jit(solution)/shard_map/all_to_all | solution.py:600
  107.8 7.7 %all-to-all-start.4 = ((bf16[64,128,128]{2,1,0:T(8,128)(2,1)}), bf16[64,128,128]{2,1,0:T(8,128)(2,1)S(1)}, u32[]{:S(2)}, u32[]{:S(2)}) async-start(bf16[64,128,128]{2,1,0:T(8,128)(2,1)} %bitcast.25), calls=%async_computation.4 | async-start | bytes 4194304 | tf_op jit(solution)/shard_map/all_to_all | solution.py:608
  115.5 20.5 %mamba_back.1 = (f32[128,512]{1,0:T(8,128)}, f32[8,512]{1,0:T(8,128)}, bf16[144,512]{1,0:T(8,128)(2,1)}, bf16[1088,128]{1,0:T(8,128)(2,1)}, f32[512,128]{1,0:T(8,128)}) custom-call(s32[9]{0:T(128)} %pad_add_fusion.meta, bf16[16,16,1024]{2,1,0:T(8,128)(2,1)} %copy-done.3, bf16[16,24,1024]{2,1,0:T(8,128)(2,1)} %all_to_all.35.got.forward, ...), custom_call_target="tpu_custom_call" | custom-call | tf_op jit(solution)/shard_map/mamba_back/pallas_call | solution.py:583
  136.0 1.6 collective-permute-start.4
  137.7 1.3 collective-permute-done.3.low_other
  139.0 0.7 copy-done.9
  139.8 2.7 %late_weights.1 = bf16[64,40,128]{2,1,0:T(8,128)(2,1)} custom-call(bf16[144,512]{1,0:T(8,128)(2,1)} %get-tuple-element.104.keep, f32[512,128]{1,0:T(8,128)} %get-tuple-element.105.part_keep, bf16[144,512]{1,0:T(8,128)(2,1)} %get-tuple-element.83.low_ext.low_own, bf16[144,512]{1,0:T(8,128)(2,1)} %copy-done.9, bf16[1088,128]{1,0:T(8,128)(2,1)} %copy-done.7), custom_call_target="tpu_custom_call" | custom-call | tf_op jit(solution)/shard_map/late_weights/pallas_call | solution.py:583
  142.8 23.1 %all_to_all.38.late = bf16[64,40,128]{2,1,0:T(8,128)(2,1)} all-to-all(bf16[64,40,128]{2,1,0:T(8,128)(2,1)} %late_weights.1), channel_id=1, replica_groups=mesh['y'=4,'core'=2,'seq'=4,'head'=4] {'y','seq','head'}, dimensions={0} | all-to-all | bytes 1310720 | tf_op jit(solution)/shard_map/all_to_all | solution.py:608
  165.9 3.7 %add_up.1 = bf16[64,168,128]{2,1,0:T(8,128)(2,1)} custom-call(bf16[64,128,128]{2,1,0:T(8,128)(2,1)} %copy-done.1, bf16[64,40,128]{2,1,0:T(8,128)(2,1)} %all_to_all.38.late), custom_call_target="tpu_custom_call" | custom-call | tf_op jit(solution)/shard_map/add_up/pallas_call | solution.py:583
  169.7 39.8 %all_to_all.39.mine = bf16[64,168,128]{2,1,0:T(8,128)(2,1)S(1)} all-to-all(bf16[64,168,128]{2,1,0:T(8,128)(2,1)} %add_up.1), channel_id=1, replica_groups=mesh['y'=4,'core'=2,'seq'=4,'head'=4] {'y','seq','head'}, dimensions={0} | all-to-all | bytes 5505024 | tf_op jit(solution)/shard_map/all_to_all | solution.py:608
  209.5 3.2 %collective-permute-start.5 = (bf16[64,168,128]{2,1,0:T(8,128)(2,1)S(1)}, bf16[64,168,128]{2,1,0:T(8,128)(2,1)S(1)}, u32[]{:S(2)}, u32[]{:S(2)}) collective-permute-start(bf16[64,168,128]{2,1,0:T(8,128)(2,1)S(1)} %all_to_all.39.mine), channel_id=1, source_target_pairs={{0,16},{16,0},{1,17},{17,1},{2,18},{18,2},{3,19},{19,3},{4,20},{20... | collective-permute-start | bytes 8257544 | tf_op jit(solution)/shard_map/ppermute | solution.py:604
  212.7 1.3 collective-permute-start.2
  214.0 3.1 %collective-permute-done.2 = f32[8,512]{1,0:T(8,128)S(1)} collective-permute-done((f32[8,512]{1,0:T(8,128)S(1)}, f32[8,512]{1,0:T(8,128)S(1)}, u32[]{:S(2)}, u32[]{:S(2)}) %collective-permute-start.2) | collective-permute-done | bytes 16416 | tf_op jit(solution)/shard_map/ppermute | solution.py:596
  217.4 1.5 copy-done.2
  218.9 7.3 %finish.1 = (f32[512,512]{1,0:T(8,128)}, f32[512,512]{1,0:T(8,128)}, f32[512,512]{1,0:T(8,128)}, f32[512,512]{1,0:T(8,128)}, f32[1024,512]{1,0:T(8,128)}, /*inde...) custom-call(s32[9]{0:T(128)} %pad_add_fusion.meta, ...), custom_call_target="tpu_custom_call" | custom-call | tf_op jit(solution)/shard_map/finish/pallas_call | solution.py:583
  226.2 1.3 fusion
  227.5 1.5 fusion.1
  229.0 1.4 slice.47
  (29 shorter events, 1.4 us)
Async XLA Ops:
  1.4 5.6 %collective-permute-start = (bf16[16,512]{1,0:T(8,128)(2,1)S(1)}, bf16[16,512]{1,0:T(8,128)(2,1)S(1)}, u32[]{:S(2)}, u32[]{:S(2)}) collective-permute-start(bf16[16,512]{1,0:T(8,128)(2,1)S(1)} %slice_bitcast_fusion), channel_id=1, source_target_pairs={{0,1},{1,2},{2,3},{3,4},{4,5},{5,6},{6,7},{7,8},{8,9},{9,10},{10,1... | collective-permute-start | bytes 49160 | tf_op jit(solution)/shard_map/ppermute | solution.py:596
  7.0 0.6 copy-start.10
  87.8 9.5 %collective-permute-start.1 = (bf16[128,3072]{1,0:T(8,128)(2,1)}, bf16[128,3072]{1,0:T(8,128)(2,1)S(1)}, u32[]{:S(2)}, u32[]{:S(2)}) collective-permute-start(bf16[128,3072]{1,0:T(8,128)(2,1)} %get-tuple-element.88), channel_id=1, source_target_pairs={{0,16},{16,0},{1,17},{17,1},{2,18},{18,2},{3,19},{19,3},{4,20},{20... | collective-permute-start | bytes 2359304 | tf_op jit(solution)/shard_map/ppermute | solution.py:604
  93.7 14.1 %all-to-all-start.3 = ((bf16[16,16,1024]{2,1,0:T(8,128)(2,1)}), bf16[16,16,1024]{2,1,0:T(8,128)(2,1)S(1)}, u32[]{:S(2)}, u32[]{:S(2)}) async-start(bf16[16,16,1024]{2,1,0:T(8,128)(2,1)} %get-tuple-element.89), calls=%async_computation.3 | async-start | bytes 1048576 | tf_op jit(solution)/shard_map/all_to_all | solution.py:600
  97.3 0.9 copy-start.4
  107.8 7.7 %copy-start.3 = (bf16[16,16,1024]{2,1,0:T(8,128)(2,1)}, bf16[16,16,1024]{2,1,0:T(8,128)(2,1)S(1)}, u32[]{:S(2)}) copy-start(bf16[16,16,1024]{2,1,0:T(8,128)(2,1)S(1)} %all-to-all-done.3.got) | copy-start | bytes 1572868
  107.8 35.0 %all-to-all-start.4 = ((bf16[64,128,128]{2,1,0:T(8,128)(2,1)}), bf16[64,128,128]{2,1,0:T(8,128)(2,1)S(1)}, u32[]{:S(2)}, u32[]{:S(2)}) async-start(bf16[64,128,128]{2,1,0:T(8,128)(2,1)} %bitcast.25), calls=%async_computation.4 | async-start | bytes 4194304 | tf_op jit(solution)/shard_map/all_to_all | solution.py:608
  115.5 22.2 %copy-start.5 = (bf16[144,512]{1,0:T(8,128)(2,1)S(1)}, bf16[144,512]{1,0:T(8,128)(2,1)}, u32[]{:S(2)}) copy-start(bf16[144,512]{1,0:T(8,128)(2,1)} %get-tuple-element.83.low_ext.low_own) | copy-start | bytes 442372
  136.0 3.0 %collective-permute-start.4 = (bf16[1088,128]{1,0:T(8,128)(2,1)}, bf16[1088,128]{1,0:T(8,128)(2,1)S(1)}, u32[]{:S(2)}, u32[]{:S(2)}) collective-permute-start(bf16[1088,128]{1,0:T(8,128)(2,1)} %get-tuple-element.106), channel_id=1, source_target_pairs={{0,16},{16,0},{1,17},{17,1},{2,18},{18,2},{3,19},{19,3},{4,20},{20... | collective-permute-start | bytes 835592 | tf_op jit(solution)/shard_map/ppermute | solution.py:604
  137.6 1.4 collective-permute-start.3
  139.0 0.7 copy-start.9
  139.0 0.8 copy-start.7
  142.8 23.1 %copy-start.1 = (bf16[64,128,128]{2,1,0:T(8,128)(2,1)}, bf16[64,128,128]{2,1,0:T(8,128)(2,1)S(1)}, u32[]{:S(2)}) copy-start(bf16[64,128,128]{2,1,0:T(8,128)(2,1)S(1)} %all-to-all-done.4.early) | copy-start | bytes 6291460
  169.7 43.0 %copy-start.11 = (f32[8,512]{1,0:T(8,128)S(1)}, f32[8,512]{1,0:T(8,128)}, u32[]{:S(2)}) copy-start(f32[8,512]{1,0:T(8,128)} %get-tuple-element.102) | copy-start | bytes 49156
  169.7 44.3 %copy-start.6 = (f32[128,512]{1,0:T(8,128)S(1)}, f32[128,512]{1,0:T(8,128)}, u32[]{:S(2)}) copy-start(f32[128,512]{1,0:T(8,128)} %get-tuple-element.101) | copy-start | bytes 786436
  209.5 7.9 %copy-start = (bf16[64,168,128]{2,1,0:T(8,128)(2,1)}, bf16[64,168,128]{2,1,0:T(8,128)(2,1)S(1)}, u32[]{:S(2)}) copy-start(bf16[64,168,128]{2,1,0:T(8,128)(2,1)S(1)} %all_to_all.39.mine) | copy-start | bytes 8257540
  209.5 7.9 %collective-permute-start.5 = (bf16[64,168,128]{2,1,0:T(8,128)(2,1)S(1)}, bf16[64,168,128]{2,1,0:T(8,128)(2,1)S(1)}, u32[]{:S(2)}, u32[]{:S(2)}) collective-permute-start(bf16[64,168,128]{2,1,0:T(8,128)(2,1)S(1)} %all_to_all.39.mine), channel_id=1, source_target_pairs={{0,16},{16,0},{1,17},{17,1},{2,18},{18,2},{3,19},{19,3},{4,20},{20... | collective-permute-start | bytes 8257544 | tf_op jit(solution)/shard_map/ppermute | solution.py:604
  212.7 4.5 %collective-permute-start.2 = (f32[8,512]{1,0:T(8,128)S(1)}, f32[8,512]{1,0:T(8,128)S(1)}, u32[]{:S(2)}, u32[]{:S(2)}) collective-permute-start(f32[8,512]{1,0:T(8,128)S(1)} %copy-done.11), channel_id=1, source_target_pairs={{1,0},{2,1},{3,2},{4,3},{5,4},{6,5},{7,6},{8,7},{9,8},{10,9},{11,1... | collective-permute-start | bytes 49160 | tf_op jit(solution)/shard_map/ppermute | solution.py:596
  217.1 13.2 %copy-start.8 = (f32[1,128,512]{2,1,0:T(8,128)}, f32[1,128,512]{2,1,0:T(8,128)S(1)}, u32[]{:S(2)}) copy-start(f32[1,128,512]{2,1,0:T(8,128)S(1)} %bitcast_dynamic-update-slice_fusion) | copy-start | bytes 786436
  217.4 1.5 copy-start.2

commit v2 on v1

--- a/solution.py
+++ b/solution.py
@@ -527,7 +527,10 @@
                     out[(4 * j + q) * D : (4 * j + q + 1) * D] = result[:, q * LANES : (q + 1) * LANES]
 
 
-def late_weights(keep, part_keep, low_own, low_other, got, out, whole):
+def late_weights(keep, part_keep, low_own, low_other, got, early, out, whole):
+    total = early[0].astype(f32)
+    for j in range(1, SHARES):
+        total = total + early[j].astype(f32)
     left = jnp.concatenate([low_own[...], low_other[...]], axis=0)
     rows = HALO + T
     for j in range(D // LANES):
@@ -538,56 +541,89 @@
     for d in range(SHARES):
         main = whole[d * MAIN : (d + 1) * MAIN]
         small = whole[4 * D + d * SMALL : 4 * D + (d + 1) * SMALL]
-        out[d] = jnp.concatenate([main, small], axis=0).astype(bf16)
-
-
-def add_up(early, late, out):
-    first = early[0].astype(f32)
-    second = late[0].astype(f32)
+        out[d] = jnp.concatenate([total, main, small], axis=0).astype(bf16)
+
+
+def add_late(got, out):
+    total = got[0].astype(f32)[T:]
     for j in range(1, SHARES):
-        first = first + early[j].astype(f32)
-        second = second + late[j].astype(f32)
-    low = jnp.concatenate([first, second], axis=0).astype(bf16)
+        total = total + got[j].astype(f32)[T:]
+    low = total.astype(bf16)
     for j in range(SHARES):
         out[j] = low
 
 
-def finish(meta, mine, other, gw_o, gw_q, gw_k, gw_v, gw_out, gw_in, gw_x, gw_dt, g_a_log, vec):
+def finish_early(meta, mine, other, gw_o, gw_q, gw_k, gw_v, gw_out, gw_in, gate, sem):
+    is_zero = meta[2 + DOCS] == 0
+    for d in reversed(range(SHARES)):
+        a, b = mine[d].astype(f32)[0:T], other[d].astype(f32)[0:T]
+        j, q, r = d // 16, d // 4 % 4, d % 4 * T
+        tile = TILES[q]
+        (gw_o, gw_q, gw_k, gw_v)[j][r : r + T, tile] = jnp.where(is_zero, a, b)
+        one = jnp.where(is_zero, b, a)
+        if j < 2:
+            gw_out[j * D + r : j * D + r + T, tile] = one
+        else:
+            low = (j - 2) * D + q * LANES
+            gate[r : r + T, low : low + LANES] = one
+        if d == SHARES // 2:
+            copy = pltpu.make_async_copy(gate, gw_in.at[:, pl.ds(E, E)], sem)
+            copy.start()
+    copy.wait()
+
+
+def finish_late(
+    meta, mine, other, _, gw_in, gw_x, gw_dt, g_a_log, g_conv_w, g_conv_b, g_dt_b, g_skip, g_gain_one,
+    g_gain_two, conv, sem,
+):
     is_zero = meta[2 + DOCS] == 0
     for d in range(SHARES):
         a, b = mine[d].astype(f32), other[d].astype(f32)
         zero = jnp.where(is_zero, a, b)
         one = jnp.where(is_zero, b, a)
-        j, q, r = d // 16, d // 4 % 4, d % 4 * T
+        j, r = d // 16, d % 16 * MAIN
+        conv[r : r + MAIN, j * LANES : (j + 1) * LANES] = zero[0:MAIN]
+        conv[r : r + MAIN, D + j * LANES : D + (j + 1) * LANES] = one[0:MAIN]
+        q, r = d // 8, d % 8 * SMALL
         tile = TILES[q]
-        (gw_o, gw_q, gw_k, gw_v)[j][r : r + T, tile] = zero[0:T]
-        if j < 2:
-            gw_out[j * D + r : j * D + r + T, tile] = one[0:T]
-        else:
-            low = E + (j - 2) * D + q * LANES
-            gw_in[r : r + T, low : low + LANES] = one[0:T]
-        r = d % 16 * MAIN
-        gw_in[r : r + MAIN, j * LANES : (j + 1) * LANES] = zero[T : T + MAIN]
-        gw_in[r : r + MAIN, D + j * LANES : D + (j + 1) * LANES] = one[T : T + MAIN]
-        tile, r = TILES[d // 8], d % 8 * SMALL
-        gw_x[r : r + SMALL, tile] = zero[T + MAIN :]
-        for out, low, high in ((gw_dt, 0, R), (g_a_log, R, R + N), (vec, R + N, R + 2 * N)):
+        gw_x[r : r + SMALL, tile] = zero[MAIN:]
+        for out, low, high in ((gw_dt, 0, R), (g_a_log, R, R + N)):
             if low <= r < high:
-                out[r - low : r - low + SMALL, tile] = one[T + MAIN :]
-
-
-def call(body, name, outs, scratch, *args, smem=True):
-    specs = [pl.BlockSpec(memory_space=pltpu.VMEM)] * len(args)
+                out[r - low : r - low + SMALL, tile] = one[MAIN:]
+        if r == R + N:
+            g_conv_w[:, tile] = one[MAIN : MAIN + KERNEL]
+            at = MAIN + KERNEL
+            for i, out in enumerate((g_conv_b, g_dt_b, g_skip)):
+                out[:, tile] = one[at + i : at + i + 1]
+            out = g_gain_one if q < 4 else g_gain_two
+            out[:, TILES[q % 4]] = one[at + 3 : at + 4]
+    copy = pltpu.make_async_copy(conv, gw_in.at[:, pl.ds(0, E)], sem)
+    copy.start()
+    copy.wait()
+
+
+MEGABYTES = dict(
+    mamba_in=16, mamba_out=16, attention=16, middle_back=20, early_weights=12, mamba_back=36, late_weights=12,
+    add_late=10, finish_early=24, finish_late=12,
+)
+
+
+def call(body, name, outs, scratch, *args, smem=True, outside=(), aliases=None, far=(), far_out=()):
+    aliases = aliases or {}
+    args = [pltpu.with_memory_space_constraint(x, pltpu.HBM) if i in far else x for i, x in enumerate(args)]
+    specs = [pl.BlockSpec(memory_space=pl.ANY if i in aliases else pltpu.VMEM) for i in range(len(args))]
     if smem:
         specs[0] = pl.BlockSpec(memory_space=pltpu.SMEM)
     return pl.pallas_call(
         body,
         name=name,
-        out_shape=[jax.ShapeDtypeStruct(s, t) for s, t in outs],
+        out_shape=[pltpu.HBM(s, t) if i in far_out else jax.ShapeDtypeStruct(s, t) for i, (s, t) in enumerate(outs)],
         in_specs=specs,
-        out_specs=[pl.BlockSpec(memory_space=pltpu.VMEM)] * len(outs),
-        scratch_shapes=[pltpu.VMEM(s, t) for s, t in scratch],
-        compiler_params=pltpu.CompilerParams(vmem_limit_bytes=56 * 1024 * 1024),
+        out_specs=[pl.BlockSpec(memory_space=pl.ANY if i in outside else pltpu.VMEM) for i in range(len(outs))],
+        scratch_shapes=[pltpu.VMEM(s, t) for s, t in scratch]
+        + ([pltpu.SemaphoreType.DMA] if outside else []),
+        input_output_aliases=aliases,
+        compiler_params=pltpu.CompilerParams(vmem_limit_bytes=MEGABYTES[name] << 20),
     )(*args)
 
 
@@ -627,6 +663,7 @@
          ((T // STEPS, 2 * N, 128), f32), ((T, R), bf16)],
         [((HALO + T, E), f32), te, te, ((T, 128), f32), ((N + 8, E), f32), tn, tn],
         meta, tokens, halo, row(gain_one), w_in, conv_w, row(conv_b), w_x, w_dt, row(dt_bias), a_log, cot, w_o,
+        far=(1, 3, 4, 5, 6, 7, 8, 9, 10, 11, 12), far_out=(2, 3, 5, 8, 10),
     )
     low_other = partner(low_ext)
     forward = swap(send)
@@ -635,7 +672,7 @@
         [((BLOCKS, ROWS, 128), bf16), ((N, E), f32), te, tel, td, tdl],
         [te, te, te, tn],
         meta, forward, tokens, step, act, bc, gate, a_log, row(d_skip), w_out, row(gain_two),
-        w_q, w_k, w_v, grad_att,
+        w_q, w_k, w_v, grad_att, far_out=(1,),
     )
     (back,) = call(
         attention, "attention",
@@ -650,7 +687,7 @@
         [((BLOCKS, N, E), bf16), tdl, td, te, tel, wide, wide, ((1, D), f32), ((1, E), f32)],
         [tdl] * 4 + [te, tn, tn],
         meta, swap(back), cot, middle, normed, low_ext, gated, gate, ssm, act, step, bc, a_log,
-        row(d_skip), w_o, w_q, w_k, w_v, w_out, row(gain_two),
+        row(d_skip), w_o, w_q, w_k, w_v, w_out, row(gain_two), far_out=(1, 2, 3, 4, 7, 8),
     )
     (early,) = call(
         early_weights, "early_weights", [((16 * D, LANES), bf16)], [((2 * T, 6 * D), bf16)],
@@ -666,29 +703,33 @@
          ((T, N, LANES), f32), ((T, N, LANES), f32)],
         meta, behind, forward, start, g, act, step, pre, bc, dt_low, conv, ext, a_log,
         row(d_skip), conv_w, w_x, w_dt, tokens, halo, row(gain_one), w_in, grad_gate, grad_mid,
-        g_gain_two, g_skip,
+        g_gain_two, g_skip, far=tuple(range(1, 25)), far_out=(0, 1, 2, 4),
     )
     (late,) = call(
-        late_weights, "late_weights", [((SHARES, MAIN + SMALL, LANES), bf16)], [((5 * D, LANES), f32)],
-        keep, part_keep, low_ext, low_other, partner(give), smem=False,
-    )
-    early, late = lax.optimization_barrier((early, late))
+        late_weights, "late_weights", [((SHARES, T + MAIN + SMALL, LANES), bf16)], [((5 * D, LANES), f32)],
+        keep, part_keep, low_ext, low_other, partner(give), early, smem=False,
+        far=(0, 1, 2, 3, 4, 5), far_out=(0,),
+    )
+    shares = trade(late)
+    (late,) = call(add_late, "add_late", [((SHARES, MAIN + SMALL, LANES), bf16)], [], shares, smem=False, far=(0,))
     late = trade(late)
-    (total,) = call(
-        add_up, "add_up", [((SHARES, T + MAIN + SMALL, LANES), bf16)], [], early, late, smem=False
-    )
-    total = trade(total)
-    gw_o, gw_q, gw_k, gw_v, gw_out, gw_in, gw_x, gw_dt, g_a_log, vec = call(
-        finish, "finish",
-        [((D, D), f32)] * 4 + [((E, D), f32), ((D, 2 * E), f32), ((64, E), f32), ((R, E), f32), tn, tn],
-        [],
-        meta, total, partner(total),
+    gw_o, gw_q, gw_k, gw_v, gw_out, gw_in = call(
+        finish_early, "finish_early",
+        [((D, D), f32)] * 4 + [((E, D), f32), ((D, 2 * E), f32)], [((D, E), f32)],
+        meta, shares, partner(shares), outside=(5,), far=(1, 2),
     )
     grad_tokens = grad_tokens.at[T - 8 :].add(shift(tail, -1))
+    late, gw_in, grad_tokens = lax.optimization_barrier((late, gw_in, grad_tokens))
+    gw_in, gw_x, gw_dt, g_a_log, g_conv_w, g_conv_b, g_dt_b, g_skip, g_gain_one, g_gain_two = call(
+        finish_late, "finish_late",
+        [((D, 2 * E), f32), ((64, E), f32), ((R, E), f32), tn, ((KERNEL, E), f32), ((1, E), f32),
+         ((1, E), f32), ((1, E), f32), ((1, D), f32), ((1, D), f32)],
+        [((D, E), f32)],
+        meta, late, partner(late), gw_in, outside=(0,), aliases={3: 0},
+    )
     return (
-        mixed[None], grad_tokens[None], vec[KERNEL + 3, 0:D], gw_in, vec[0:KERNEL], vec[KERNEL], gw_x.T,
-        gw_dt, vec[KERNEL + 1], g_a_log, vec[KERNEL + 2], gw_out, vec[KERNEL + 3, D:E], gw_q, gw_k,
-        gw_v, gw_o,
+        mixed[None], grad_tokens[None], g_gain_one[0], gw_in, g_conv_w, g_conv_b[0], gw_x.T, gw_dt,
+        g_dt_b[0], g_a_log, g_skip[0], gw_out, g_gain_two[0], gw_q, gw_k, gw_v, gw_o,
     )
 
 

time: 232 us -> 214 us (0.922)
  blocking collectives: 111 us -> 90 us
  waiting for transfers between devices: 11.1 us -> 19.7 us
  local copies, waits for them, and re-layouts: 8.71 us -> 0.94 us
  starting transfers between devices: 27.6 us -> 32.1 us
  Pallas kernels: 69.8 us -> 65.7 us
    all_to_all x2 -> x1, blocking collectives: 62.9 us -> 42.7 us  [trade(): return lax.all_to_all(x, SAME, 0, 0, tiled=True)]
    all_to_all x1 -> x2, starting transfers between devices: 7.65 us -> 12.3 us  [trade(): return lax.all_to_all(x, SAME, 0, 0, tiled=True)]
    slice x3 -> x0, local copies, waits for them, and re-layouts: 4.16 us -> none  [the longest x1 1.47 us: layer(): vec[KERNEL + 2]]
    pallas_call x9 -> x10, Pallas kernels: 69.8 us -> 65.7 us  [call(): pl.pallas_call(body, name=name, out_shape=[pltpu.HBM(s, t) if i in far_ou...]
    unnamed x25 -> x40, local copies, waits for them, and re-layouts: 3.82 us -> 0.1 us
    all_to_all x1 -> x2, waiting for transfers between devices: 0.34 us -> 3.49 us  [trade(): return lax.all_to_all(x, SAME, 0, 0, tiled=True)]
    ppermute x4 -> x5, starting transfers between devices: 10.8 us -> 10.5 us  [partner(): return lax.ppermute(x, 'core', [(0, 1), (1, 0)])]
  transfers between devices with their start and end apart: 8 -> 10, of which waited for: 5 -> 5; matrix products, arithmetic and copies ran while one was open for 1% -> 1% of each run, Pallas kernels for 12% -> 16%
where the time goes in v2:
time: 214 us; the launch traced here: 212 us
  blocking collectives  90 us (42%)
  Pallas kernels  65.7 us (31%)
  starting transfers between devices  32.1 us (15%)
  waiting for transfers between devices  19.7 us (9%)
  other arithmetic  2.14 us (1%)
    pallas_call x10, Pallas kernels, call(): pl.pallas_call(body, name=name, out_shape=[pltpu.HBM(s, t) if i in far_ou...  65.7 us
    all_to_all x3, blocking collectives, swap(): return lax.all_to_all(x, PLACE, 0, 0, tiled=True)  47.4 us
    all_to_all x1, blocking collectives, trade(): return lax.all_to_all(x, SAME, 0, 0, tiled=True)  42.7 us
    all_to_all x2, starting transfers between devices, trade(): return lax.all_to_all(x, SAME, 0, 0, tiled=True)  12.3 us
    ppermute x5, starting transfers between devices, partner(): return lax.ppermute(x, 'core', [(0, 1), (1, 0)])  10.5 us
    all_to_all x1, waiting for transfers between devices, swap(): return lax.all_to_all(x, PLACE, 0, 0, tiled=True)  7.96 us
    ppermute x2, starting transfers between devices, shift(): return lax.ppermute(x, PLACE, pairs)  5.65 us
    ppermute x2, waiting for transfers between devices, shift(): return lax.ppermute(x, PLACE, pairs)  5.19 us
  transfers between devices with their start and end apart: 10, of which 5 were waited for; matrix products, arithmetic and copies ran while one was open for 1% of the time, Pallas kernels for 16%

profile of v2, /device:TPU:1, one launch (start us, length us, event | category | flops | bytes accessed | tf_op | source)
XLA Modules:
  0.0 211.8 jit_solution(2012625026963526268)
XLA Ops:
  0.7 0.8 slice_bitcast_fusion
  1.6 4.4 %collective-permute-start = (bf16[16,512]{1,0:T(8,128)(2,1)S(1)}, bf16[16,512]{1,0:T(8,128)(2,1)S(1)}, u32[]{:S(2)}, u32[]{:S(2)}) collective-permute-start(bf16[16,512]{1,0:T(8,128)(2,1)S(1)} %slice_bitcast_fusion), channel_id=1, source_target_pairs={{0,1},{1,2},{2,3},{3,4},{4,5},{5,6},{6,7},{7,8},{8,9},{9,10},{10,1... | collective-permute-start | bytes 49160 | tf_op jit(solution)/shard_map/ppermute | solution.py:632
  6.0 0.8 pad_add_fusion.meta
  6.8 6.9 %mamba_in.1 = (bf16[16,24,1024]{2,1,0:T(8,128)(2,1)S(1)}, bf16[128,512]{1,0:T(8,128)(2,1)S(1)}, bf16[144,512]{1,0:T(8,128)(2,1)}, bf16[144,1024]{1,0:T(8,128)(2,...) custom-call(s32[9]{0:T(128)S(1)} %pad_add_fusion.meta, ...), custom_call_target="tpu_custom_call" | custom-call | tf_op jit(solution)/shard_map/mamba_in/pallas_call | solution.py:617
  13.7 19.2 %all_to_all.35.got.forward = bf16[16,24,1024]{2,1,0:T(8,128)(2,1)S(1)} all-to-all(bf16[16,24,1024]{2,1,0:T(8,128)(2,1)S(1)} %get-tuple-element.81), channel_id=1, replica_groups=mesh['y'=4,'core'=2,'seq'=4,'head'=4] {'seq','head'}, dimensions={0} | all-to-all | bytes 1572864 | tf_op jit(solution)/shard_map/all_to_all | solution.py:636
  33.0 4.9 %mamba_out.1 = (bf16[16,192,128]{2,1,0:T(8,128)(2,1)S(1)}, f32[16,1024]{1,0:T(8,128)}, f32[128,1024]{1,0:T(8,128)S(1)}, bf16[128,1024]{1,0:T(8,128)(2,1)S(1)}, f...) custom-call(s32[9]{0:T(128)S(1)} %pad_add_fusion.meta, bf16[16,24,1024]{2,1,0:T(8,128)(2,1)S(1)} %all_to_all.35.got.forward, ...), custom_call_target="tpu_custom_call" | custom-call | tf_op jit(solution)/shard_map/mamba_out/pallas_call | solution.py:617
  37.9 14.4 %all_to_all.36.got = bf16[16,192,128]{2,1,0:T(8,128)(2,1)S(1)} all-to-all(bf16[16,192,128]{2,1,0:T(8,128)(2,1)S(1)} %get-tuple-element.87), channel_id=1, replica_groups=mesh['y'=4,'core'=2,'seq'=4,'head'=4] {'seq','head'}, dimensions={0} | all-to-all | bytes 1572864 | tf_op jit(solution)/shard_map/all_to_all | solution.py:636
  52.3 7.1 %attention.1 = bf16[16,192,128]{2,1,0:T(8,128)(2,1)S(1)} custom-call(s32[9]{0:T(128)S(1)} %pad_add_fusion.meta, bf16[16,192,128]{2,1,0:T(8,128)(2,1)S(1)} %all_to_all.36.got), custom_call_target="tpu_custom_call" | custom-call | tf_op jit(solution)/shard_map/attention/pallas_call | solution.py:617
  59.5 13.8 %all_to_all.37.got = bf16[16,192,128]{2,1,0:T(8,128)(2,1)S(1)} all-to-all(bf16[16,192,128]{2,1,0:T(8,128)(2,1)S(1)} %attention.1), channel_id=1, replica_groups=mesh['y'=4,'core'=2,'seq'=4,'head'=4] {'seq','head'}, dimensions={0} | all-to-all | bytes 1572864 | tf_op jit(solution)/shard_map/all_to_all | solution.py:636
  73.3 5.8 %middle_back.1 = (bf16[16,16,1024]{2,1,0:T(8,128)(2,1)}, bf16[128,512]{1,0:T(8,128)(2,1)}, f32[128,512]{1,0:T(8,128)}, f32[128,1024]{1,0:T(8,128)}, bf16[128,102...) custom-call(s32[9]{0:T(128)S(1)} %pad_add_fusion.meta, ...), custom_call_target="tpu_custom_call" | custom-call | tf_op jit(solution)/shard_map/middle_back/pallas_call | solution.py:617
  79.1 5.6 %collective-permute-start.1 = (bf16[128,3072]{1,0:T(8,128)(2,1)S(1)}, bf16[128,3072]{1,0:T(8,128)(2,1)S(1)}, u32[]{:S(2)}, u32[]{:S(2)}) collective-permute-start(bf16[128,3072]{1,0:T(8,128)(2,1)S(1)} %get-tuple-element.95), channel_id=1, source_target_pairs={{0,16},{16,0},{1,17},{17,1},{2,18},{18,2},{3,19},{19,3},{4,20},{20... | collective-permute-start | bytes 2359304 | tf_op jit(solution)/shard_map/ppermute | solution.py:640
  84.7 3.6 %all-to-all-start.3 = ((bf16[16,16,1024]{2,1,0:T(8,128)(2,1)}), bf16[16,16,1024]{2,1,0:T(8,128)(2,1)S(1)}, u32[]{:S(2)}, u32[]{:S(2)}) async-start(bf16[16,16,1024]{2,1,0:T(8,128)(2,1)} %get-tuple-element.96), calls=%async_computation.3 | async-start | bytes 1048576 | tf_op jit(solution)/shard_map/all_to_all | solution.py:636
  88.3 2.7 %early_weights.1 = bf16[8192,128]{1,0:T(8,128)(2,1)} custom-call(s32[9]{0:T(128)S(1)} %pad_add_fusion.meta, bf16[128,3072]{1,0:T(8,128)(2,1)S(1)} %get-tuple-element.94.keep, bf16[128,3072]{1,0:T(8,128)(2,1)S(1)} %collective-permute-done.1.got), custom_call_target="tpu_custom_call" | custom-call | tf_op jit(solution)/shard_map/early_weights/pallas_call | solution.py:617
  91.0 8.0 %all-to-all-done.3.got = bf16[16,16,1024]{2,1,0:T(8,128)(2,1)S(1)} async-done(((bf16[16,16,1024]{2,1,0:T(8,128)(2,1)}), bf16[16,16,1024]{2,1,0:T(8,128)(2,1)S(1)}, u32[]{:S(2)}, u32[]{:S(2)}) %all-to-all-start.3) | async-done | bytes 524320 | tf_op jit(solution)/shard_map/all_to_all | solution.py:636
  98.9 7.7 %all-to-all-start.4 = ((bf16[64,128,128]{2,1,0:T(8,128)(2,1)}), bf16[64,128,128]{2,1,0:T(8,128)(2,1)}, u32[]{:S(2)}, u32[]{:S(2)}) async-start(bf16[64,128,128]{2,1,0:T(8,128)(2,1)} %bitcast.14), calls=%async_computation.4 | async-start | bytes 4194304 | tf_op jit(solution)/shard_map/all_to_all | solution.py:644
  106.7 21.2 %mamba_back.1 = (f32[128,512]{1,0:T(8,128)}, f32[8,512]{1,0:T(8,128)}, bf16[144,512]{1,0:T(8,128)(2,1)}, bf16[1088,128]{1,0:T(8,128)(2,1)S(1)}, f32[512,128]{1,0:T(8,128)}) custom-call(s32[9]{0:T(128)S(1)} %pad_add_fusion.meta, bf16[16,16,1024]{2,1,0:T(8,128)(2,1)} %copy-done.16, bf16[16,24,1024]{2,1,0:T(8,128)(2,1)} %copy-done, ...), custom_call_target="tpu_custom_call" | custom-call | tf_op jit(solution)/shard_map/mamba_back/pallas_call | solution.py:617
  127.8 1.6 collective-permute-start.3
  129.4 0.1 collective-permute-start.2
  129.5 1.3 collective-permute-done.2.low_other
  130.8 3.5 %all-to-all-done.4.early = bf16[64,128,128]{2,1,0:T(8,128)(2,1)} async-done(((bf16[64,128,128]{2,1,0:T(8,128)(2,1)}), bf16[64,128,128]{2,1,0:T(8,128)(2,1)}, u32[]{:S(2)}, u32[]{:S(2)}) %all-to-all-start.4) | async-done | bytes 2097184 | tf_op jit(solution)/shard_map/all_to_all | solution.py:644
  134.3 4.4 %late_weights.1 = bf16[64,168,128]{2,1,0:T(8,128)(2,1)} custom-call(bf16[144,512]{1,0:T(8,128)(2,1)} %get-tuple-element.108.keep, f32[512,128]{1,0:T(8,128)} %get-tuple-element.109.part_keep, bf16[144,512]{1,0:T(8,128)(2,1)} %get-tuple-element.90.low_ext.low_own, bf16[144,512]{1,0:T(8,128)(2,1)} %copy-done.18, bf16[1088,128]{1,0:T(8,128)(2,1)} %copy-done.17, ...), custom_call_target="tpu_custom_call" | custom-call | tf_op jit(solution)/shard_map/late_weights/pallas_call | solution.py:617
  138.7 42.7 %all_to_all.38.got.mine = bf16[64,168,128]{2,1,0:T(8,128)(2,1)} all-to-all(bf16[64,168,128]{2,1,0:T(8,128)(2,1)} %late_weights.1), channel_id=1, replica_groups=mesh['y'=4,'core'=2,'seq'=4,'head'=4] {'y','seq','head'}, dimensions={0} | all-to-all | bytes 5505024 | tf_op jit(solution)/shard_map/all_to_all | solution.py:644
  181.3 2.5 %collective-permute-start.4 = (bf16[64,168,128]{2,1,0:T(8,128)(2,1)}, bf16[64,168,128]{2,1,0:T(8,128)(2,1)}, u32[]{:S(2)}, u32[]{:S(2)}) collective-permute-start(bf16[64,168,128]{2,1,0:T(8,128)(2,1)} %all_to_all.38.got.mine), channel_id=1, source_target_pairs={{0,16},{16,0},{1,17},{17,1},{2,18},{18,2},{3,19},{19,3},{4,20},{20... | collective-permute-start | bytes 8257544 | tf_op jit(solution)/shard_map/ppermute | solution.py:640
  183.8 2.8 %add_late.1 = bf16[64,40,128]{2,1,0:T(8,128)(2,1)} custom-call(bf16[64,168,128]{2,1,0:T(8,128)(2,1)} %all_to_all.38.got.mine), custom_call_target="tpu_custom_call" | custom-call | tf_op jit(solution)/shard_map/add_late/pallas_call | solution.py:617
  186.6 4.6 %all-to-all-start.6 = ((bf16[64,40,128]{2,1,0:T(8,128)(2,1)}), bf16[64,40,128]{2,1,0:T(8,128)(2,1)S(1)}, u32[]{:S(2)}, u32[]{:S(2)}) async-start(bf16[64,40,128]{2,1,0:T(8,128)(2,1)} %add_late.1), calls=%async_computation.6 | async-start | bytes 1310720 | tf_op jit(solution)/shard_map/all_to_all | solution.py:644
  191.3 1.3 collective-permute-start.5
  192.6 5.2 %collective-permute-done.5 = f32[8,512]{1,0:T(8,128)S(1)} collective-permute-done((f32[8,512]{1,0:T(8,128)S(1)}, f32[8,512]{1,0:T(8,128)S(1)}, u32[]{:S(2)}, u32[]{:S(2)}) %collective-permute-start.5) | collective-permute-done | bytes 16416 | tf_op jit(solution)/shard_map/ppermute | solution.py:632
  197.8 1.3 add_dynamic-update-slice_fusion
  199.1 7.0 %finish_early.1 = (f32[512,512]{1,0:T(8,128)}, f32[512,512]{1,0:T(8,128)}, f32[512,512]{1,0:T(8,128)}, f32[512,512]{1,0:T(8,128)}, f32[1024,512]{1,0:T(8,128)}, /*index=5*/f32[512,2048]{1,0:T(8,128)}) custom-call(s32[9]{0:T(128)S(1)} %pad_add_fusion.meta, bf16[64,168,128]{2,1,0:T(8,128)(2,1)} %all_to_all.38.got.mine, ...), custom_call_target="tpu_custom_call" | custom-call | tf_op jit(solution)/shard_map/finish_early/pallas_call | solution.py:617
  206.2 0.8 collective-permute-start.6
  206.9 1.7 collective-permute-done.6.other
  208.6 2.9 %finish_late.1 = (f32[512,2048]{1,0:T(8,128)}, f32[64,1024]{1,0:T(8,128)}, f32[32,1024]{1,0:T(8,128)}, f32[16,1024]{1,0:T(8,128)}, f32[4,1024]{1,0:T(4,128)}, /*...) custom-call(s32[9]{0:T(128)S(1)} %pad_add_fusion.meta, ...), custom_call_target="tpu_custom_call", output_to_operand_aliasing={{0}: (3, {})} | custom-call | tf_op jit(solution)/shard_map/finish_late/pallas_call | solution.py:617
  (45 shorter events, 0.1 us)
Async XLA Ops:
  0.7 32.3 %copy-start.9 = (bf16[1,128,512]{2,1,0:T(8,128)(2,1)S(1)}, bf16[1,128,512]{2,1,0:T(8,128)(2,1)}, u32[]{:S(2)}) copy-start(bf16[1,128,512]{2,1,0:T(8,128)(2,1)} %param.20) | copy-start | bytes 393220
  0.7 32.3 %copy-start.14 = (f32[1024]{0:T(1024)S(1)}, f32[1024]{0:T(1024)}, u32[]{:S(2)}) copy-start(f32[1024]{0:T(1024)} %param.30) | copy-start | bytes 12292
  0.7 32.2 %copy-start.15 = (f32[512]{0:T(512)S(1)}, f32[512]{0:T(512)}, u32[]{:S(2)}) copy-start(f32[512]{0:T(512)} %param.32) | copy-start | bytes 6148
  0.7 32.2 %copy-start.2 = (bf16[1024,512]{1,0:T(8,128)(2,1)S(1)}, bf16[1024,512]{1,0:T(8,128)(2,1)}, u32[]{:S(2)}) copy-start(bf16[1024,512]{1,0:T(8,128)(2,1)} %w_out.3) | copy-start | bytes 3145732
  0.7 32.2 %copy-start.6 = (bf16[512,512]{1,0:T(8,128)(2,1)S(1)}, bf16[512,512]{1,0:T(8,128)(2,1)}, u32[]{:S(2)}) copy-start(bf16[512,512]{1,0:T(8,128)(2,1)} %w_q.3) | copy-start | bytes 1572868
  1.6 5.2 %collective-permute-start = (bf16[16,512]{1,0:T(8,128)(2,1)S(1)}, bf16[16,512]{1,0:T(8,128)(2,1)S(1)}, u32[]{:S(2)}, u32[]{:S(2)}) collective-permute-start(bf16[16,512]{1,0:T(8,128)(2,1)S(1)} %slice_bitcast_fusion), channel_id=1, source_target_pairs={{0,1},{1,2},{2,3},{3,4},{4,5},{5,6},{6,7},{7,8},{8,9},{9,10},{10,1... | collective-permute-start | bytes 49160 | tf_op jit(solution)/shard_map/ppermute | solution.py:632
  5.9 27.0 %copy-start.7 = (bf16[512,512]{1,0:T(8,128)(2,1)S(1)}, bf16[512,512]{1,0:T(8,128)(2,1)}, u32[]{:S(2)}) copy-start(bf16[512,512]{1,0:T(8,128)(2,1)} %w_k.3) | copy-start | bytes 1572868
  5.9 27.0 %copy-start.8 = (bf16[512,512]{1,0:T(8,128)(2,1)S(1)}, bf16[512,512]{1,0:T(8,128)(2,1)}, u32[]{:S(2)}) copy-start(bf16[512,512]{1,0:T(8,128)(2,1)} %w_v.3) | copy-start | bytes 1572868
  6.0 27.0 %copy-start.10 = (f32[16,1024]{1,0:T(8,128)S(1)}, f32[16,1024]{1,0:T(8,128)}, u32[]{:S(2)}) copy-start(f32[16,1024]{1,0:T(8,128)} %a_log.7) | copy-start | bytes 196612
  6.8 31.1 %copy-start.13 = (bf16[16,512]{1,0:T(8,128)(2,1)}, bf16[16,512]{1,0:T(8,128)(2,1)S(1)}, u32[]{:S(2)}) copy-start(bf16[16,512]{1,0:T(8,128)(2,1)S(1)} %collective-permute-done.halo) | copy-start | bytes 49156
  13.7 59.6 %copy-start.1 = (f32[128,1024]{1,0:T(8,128)}, f32[128,1024]{1,0:T(8,128)S(1)}, u32[]{:S(2)}) copy-start(f32[128,1024]{1,0:T(8,128)S(1)} %get-tuple-element.82.step) | copy-start | bytes 1572868
  13.7 59.6 %copy-start.3 = (bf16[128,1024]{1,0:T(8,128)(2,1)}, bf16[128,1024]{1,0:T(8,128)(2,1)S(1)}, u32[]{:S(2)}) copy-start(bf16[128,1024]{1,0:T(8,128)(2,1)S(1)} %get-tuple-element.83.act) | copy-start | bytes 786436
  13.7 59.6 %copy-start.4 = (f32[16,32,128]{2,1,0:T(8,128)}, f32[16,32,128]{2,1,0:T(8,128)S(1)}, u32[]{:S(2)}) copy-start(f32[16,32,128]{2,1,0:T(8,128)S(1)} %get-tuple-element.84.bc) | copy-start | bytes 786436
  32.9 19.4 %copy-start = (bf16[16,24,1024]{2,1,0:T(8,128)(2,1)}, bf16[16,24,1024]{2,1,0:T(8,128)(2,1)S(1)}, u32[]{:S(2)}) copy-start(bf16[16,24,1024]{2,1,0:T(8,128)(2,1)S(1)} %all_to_all.35.got.forward) | copy-start | bytes 2359300
  37.9 35.4 %copy-start.5 = (bf16[512,512]{1,0:T(8,128)(2,1)S(1)}, bf16[512,512]{1,0:T(8,128)(2,1)}, u32[]{:S(2)}) copy-start(bf16[512,512]{1,0:T(8,128)(2,1)} %w_o.3) | copy-start | bytes 1572868
  37.9 35.4 %copy-start.11 = (bf16[144,512]{1,0:T(8,128)(2,1)S(1)}, bf16[144,512]{1,0:T(8,128)(2,1)}, u32[]{:S(2)}) copy-start(bf16[144,512]{1,0:T(8,128)(2,1)} %get-tuple-element.90.low_ext.low_own) | copy-start | bytes 442372
  37.9 35.4 %copy-start.12 = (bf16[1,128,512]{2,1,0:T(8,128)(2,1)S(1)}, bf16[1,128,512]{2,1,0:T(8,128)(2,1)}, u32[]{:S(2)}) copy-start(bf16[1,128,512]{2,1,0:T(8,128)(2,1)} %param.37) | copy-start | bytes 393220
  79.1 9.2 %collective-permute-start.1 = (bf16[128,3072]{1,0:T(8,128)(2,1)S(1)}, bf16[128,3072]{1,0:T(8,128)(2,1)S(1)}, u32[]{:S(2)}, u32[]{:S(2)}) collective-permute-start(bf16[128,3072]{1,0:T(8,128)(2,1)S(1)} %get-tuple-element.95), channel_id=1, source_target_pairs={{0,16},{16,0},{1,17},{17,1},{2,18},{18,2},{3,19},{19,3},{4,20},{20... | collective-permute-start | bytes 2359304 | tf_op jit(solution)/shard_map/ppermute | solution.py:640
  84.7 14.3 %all-to-all-start.3 = ((bf16[16,16,1024]{2,1,0:T(8,128)(2,1)}), bf16[16,16,1024]{2,1,0:T(8,128)(2,1)S(1)}, u32[]{:S(2)}, u32[]{:S(2)}) async-start(bf16[16,16,1024]{2,1,0:T(8,128)(2,1)} %get-tuple-element.96), calls=%async_computation.3 | async-start | bytes 1048576 | tf_op jit(solution)/shard_map/all_to_all | solution.py:636
  98.9 7.7 %copy-start.16 = (bf16[16,16,1024]{2,1,0:T(8,128)(2,1)}, bf16[16,16,1024]{2,1,0:T(8,128)(2,1)S(1)}, u32[]{:S(2)}) copy-start(bf16[16,16,1024]{2,1,0:T(8,128)(2,1)S(1)} %all-to-all-done.3.got) | copy-start | bytes 1572868
  98.9 35.3 %all-to-all-start.4 = ((bf16[64,128,128]{2,1,0:T(8,128)(2,1)}), bf16[64,128,128]{2,1,0:T(8,128)(2,1)}, u32[]{:S(2)}, u32[]{:S(2)}) async-start(bf16[64,128,128]{2,1,0:T(8,128)(2,1)} %bitcast.14), calls=%async_computation.4 | async-start | bytes 4194304 | tf_op jit(solution)/shard_map/all_to_all | solution.py:644
  127.8 3.0 %collective-permute-start.3 = (bf16[1088,128]{1,0:T(8,128)(2,1)S(1)}, bf16[1088,128]{1,0:T(8,128)(2,1)S(1)}, u32[]{:S(2)}, u32[]{:S(2)}) collective-permute-start(bf16[1088,128]{1,0:T(8,128)(2,1)S(1)} %get-tuple-element.110), channel_id=1, source_target_pairs={{0,16},{16,0},{1,17},{17,1},{2,18},{18,2},{3,19},{19,3},{4,20},{20... | collective-permute-start | bytes 835592 | tf_op jit(solution)/shard_map/ppermute | solution.py:640
  129.4 1.4 collective-permute-start.2
  130.8 3.5 %copy-start.18 = (bf16[144,512]{1,0:T(8,128)(2,1)}, bf16[144,512]{1,0:T(8,128)(2,1)S(1)}, u32[]{:S(2)}) copy-start(bf16[144,512]{1,0:T(8,128)(2,1)S(1)} %collective-permute-done.2.low_other) | copy-start | bytes 442372
  130.8 3.5 %copy-start.17 = (bf16[1088,128]{1,0:T(8,128)(2,1)}, bf16[1088,128]{1,0:T(8,128)(2,1)S(1)}, u32[]{:S(2)}) copy-start(bf16[1088,128]{1,0:T(8,128)(2,1)S(1)} %collective-permute-done.3.got) | copy-start | bytes 835588
  181.3 9.9 %copy-start.19 = (f32[8,512]{1,0:T(8,128)S(1)}, f32[8,512]{1,0:T(8,128)}, u32[]{:S(2)}) copy-start(f32[8,512]{1,0:T(8,128)} %get-tuple-element.114) | copy-start | bytes 49156
  181.3 17.8 %collective-permute-start.4 = (bf16[64,168,128]{2,1,0:T(8,128)(2,1)}, bf16[64,168,128]{2,1,0:T(8,128)(2,1)}, u32[]{:S(2)}, u32[]{:S(2)}) collective-permute-start(bf16[64,168,128]{2,1,0:T(8,128)(2,1)} %all_to_all.38.got.mine), channel_id=1, source_target_pairs={{0,16},{16,0},{1,17},{17,1},{2,18},{18,2},{3,19},{19,3},{4,20},{20... | collective-permute-start | bytes 8257544 | tf_op jit(solution)/shard_map/ppermute | solution.py:640
  186.6 19.5 %all-to-all-start.6 = ((bf16[64,40,128]{2,1,0:T(8,128)(2,1)}), bf16[64,40,128]{2,1,0:T(8,128)(2,1)S(1)}, u32[]{:S(2)}, u32[]{:S(2)}) async-start(bf16[64,40,128]{2,1,0:T(8,128)(2,1)} %add_late.1), calls=%async_computation.6 | async-start | bytes 1310720 | tf_op jit(solution)/shard_map/all_to_all | solution.py:644
  191.3 6.5 %collective-permute-start.5 = (f32[8,512]{1,0:T(8,128)S(1)}, f32[8,512]{1,0:T(8,128)S(1)}, u32[]{:S(2)}, u32[]{:S(2)}) collective-permute-start(f32[8,512]{1,0:T(8,128)S(1)} %copy-done.19), channel_id=1, source_target_pairs={{1,0},{2,1},{3,2},{4,3},{5,4},{6,5},{7,6},{8,7},{9,8},{10,9},{11,1... | collective-permute-start | bytes 49160 | tf_op jit(solution)/shard_map/ppermute | solution.py:632
  206.2 2.5 %collective-permute-start.6 = (bf16[64,40,128]{2,1,0:T(8,128)(2,1)S(1)}, bf16[64,40,128]{2,1,0:T(8,128)(2,1)S(1)}, u32[]{:S(2)}, u32[]{:S(2)}) collective-permute-start(bf16[64,40,128]{2,1,0:T(8,128)(2,1)S(1)} %all-to-all-done.6.mine), channel_id=1, source_target_pairs={{0,16},{16,0},{1,17},{17,1},{2,18},{18,2},{3,19},{19,3},{4,20},{20... | collective-permute-start | bytes 1966088 | tf_op jit(solution)/shard_map/ppermute | solution.py:640

commit v3 on v2

--- a/solution.py
+++ b/solution.py
@@ -12,13 +12,14 @@
 LANES, STEPS = 128, 8
 TILES = [slice(q * LANES, (q + 1) * LANES) for q in range(E // LANES)]
 ROWS = T + HALF
+SENT = N * 8 + 16
 RESET = 1e4
 LOG2E = 1.4426950408889634
 EPS = 1e-05
 MASKED = -1e30
 PLACE = ("seq", "head")
 ALL = ("y", "core", "seq", "head")
-SAME, SHARES, MAIN, SMALL = ("y", "seq", "head"), 64, 32, 8
+SAME, SHARES, MAIN, SMALL, LATE = ("y", "seq", "head"), 64, 32, 8, 40
 bf16, f32, i32 = jnp.bfloat16, jnp.float32, jnp.int32
 
 
@@ -117,7 +118,7 @@
 def mamba_in(
     meta, tokens, halo, gain, w_in, conv_w, conv_b, w_x, w_dt, dt_b, a_log, cot, w_o,
     send, grad_att, low_out, ext_out, gate_out, conv_out, act_out, step_out, pre_out, bc_out, dt_out,
-    ext, dec, sa, xp, end, rates2, zero,
+    ext, dec, sa, xp, rates2, zero,
 ):
     grad_att[...] = mm_nt(cot[...], w_o[...]).astype(bf16)
     own = tokens[...].astype(f32)
@@ -160,15 +161,26 @@
     total = jnp.sum(held, axis=0, keepdims=True)
     high = total.astype(bf16)
     rest = (total - high.astype(f32)).astype(bf16)
-    end[N : N + 8] = jnp.concatenate([high.astype(f32), rest.astype(f32), jnp.zeros((6, E), f32)], axis=0)
     rates2[...] = -jnp.exp(a_log[...]) * LOG2E
     zero[...] = jnp.zeros((N, E), f32)
     states = scan_forward(dec, sa, bc_out, rates2, zero)
-    for q, tile in enumerate(TILES):
-        end[0:N, tile] = states[q]
-    ended = end[...].astype(bf16)
+    sums = [high[:, tile].astype(f32) for tile in TILES] + [rest[:, tile].astype(f32) for tile in TILES]
+    ended = jnp.concatenate(list(states) + sums, axis=0).astype(bf16)
     for j in range(BLOCKS):
         send[j] = ended
+
+
+def joined(blocks, first, last, ends, rates2):
+    def join(turn, states):
+        sent = blocks[first(turn)].astype(f32)
+        own = sent if ends is None else ends[first(turn)].astype(f32)
+        total = sent[N * 8 : N * 8 + 8] + sent[N * 8 + 8 : N * 8 + 16]
+        return tuple(
+            jnp.exp2(rates2[:, tile] * total[q : q + 1]) * states[q] + own[q * N : (q + 1) * N]
+            for q, tile in enumerate(TILES)
+        )
+
+    return lax.fori_loop(0, last, join, tuple(jnp.zeros((N, LANES), f32) for _ in TILES))
 
 
 def roll_half(x):
@@ -185,13 +197,8 @@
     dec[...] = step[...] + reset_of(meta, columns(0, meta))
     act_f = act[...].astype(f32)
     sa[...] = step[...] * act_f
-
-    def join(j, state):
-        tail = got[j, N : N + 8].astype(f32)
-        total = tail[0:1] + tail[1:2]
-        return jnp.exp2(rates2[...] * total) * state + got[j, 0:N].astype(f32)
-
-    start_out[...] = lax.fori_loop(0, place, join, jnp.zeros((N, E), f32))
+    for tile, state in zip(TILES, joined(got, lambda turn: turn, place, None, rates2)):
+        start_out[:, tile] = state
     scan_forward(dec, sa, bc, rates2, start_out, ssm)
     result = ssm[...] + d_skip[...] * act_f
     ssm_out[...] = result
@@ -289,7 +296,7 @@
     meta, got, cot, middle, normed, low_ext, gated, gate, ssm, act, step, bc, a_log, d_skip,
     w_o, w_q, w_k, w_v, w_out, gain,
     send, mixed, grad_mid_out, g_out, grad_gate_out, keep, give, g_gain, g_skip,
-    att, dq, dk, dv, dec, end, rates2,
+    att, dq, dk, dv, dec, rates2,
 ):
     low = lax.broadcasted_iota(i32, (HALF, 128), 1) < HALF
     low_t = lax.broadcasted_iota(i32, (T, 128), 1) < HALF
@@ -353,33 +360,36 @@
         return tuple(carry)
 
     carry = lax.fori_loop(0, T // STEPS, block, tuple(jnp.zeros((N, LANES), f32) for _ in TILES))
-    for q, tile in enumerate(TILES):
-        end[:, tile] = carry[q]
-    ended = end[...].astype(bf16)
+    ended = jnp.concatenate(carry, axis=0).astype(bf16)
     for j in range(BLOCKS):
         send[j] = ended
 
 
 def mamba_back(
-    meta, got, forward, start, g, act, step, pre, bc, dt_low, conv, ext_low, a_log, d_skip,
-    conv_w, w_x, w_dt, tokens, halo, gain, w_in, grad_gate, grad_mid, g_gain_two, g_skip,
+    meta, got, forward, start, g, act, step, pre_far, bc, dt_low_far, conv_far, ext_low_far, a_log, d_skip,
+    conv_w, w_x_far, w_dt_far, tokens_far, halo, gain, w_in_far, grad_gate_far, grad_mid_far, g_gain_two, g_skip,
     grad_tokens, tail, keep, give, part_keep,
     dec, sa, decay, kept, gs, ab, ext, padded, grad_ext, vec, wide, rates, rates2, sum_b, sum_c,
+    pre, dt_low, conv, ext_low, w_x, w_dt, tokens, w_in, grad_gate, grad_mid, sems,
 ):
     place = meta[1]
+    loads = [
+        pltpu.make_async_copy(source, held, sems.at[i])
+        for i, (source, held) in enumerate(
+            ((pre_far, pre), (dt_low_far, dt_low), (conv_far, conv), (ext_low_far, ext_low), (w_x_far, w_x), (w_dt_far, w_dt), (tokens_far, tokens), (w_in_far, w_in), (grad_gate_far, grad_gate), (grad_mid_far, grad_mid))
+        )
+    ]
+    for load in loads:
+        load.start()
     dec[...] = step[...] + reset_of(meta, columns(0, meta))
     act_f = act[...].astype(f32)
     sa[...] = step[...] * act_f
     rates[...] = -jnp.exp(a_log[...])
     rates2[...] = rates[...] * LOG2E
 
-    def join(turn, state):
-        j = BLOCKS - 1 - turn
-        tail = forward[j, N : N + 8].astype(f32)
-        total = tail[0:1] + tail[1:2]
-        return jnp.exp2(rates2[...] * total) * state + got[j].astype(f32)
-
-    wide[R : R + N] = lax.fori_loop(0, BLOCKS - 1 - place, join, jnp.zeros((N, E), f32))
+    ahead_carry = joined(forward, lambda turn: BLOCKS - 1 - turn, BLOCKS - 1 - place, got, rates2)
+    for tile, state in zip(TILES, ahead_carry):
+        wide[R : R + N, tile] = state
 
     def ahead(i, states):
         states = list(states)
@@ -441,6 +451,8 @@
             values = sums[:, n, :]
             high = values.astype(bf16)
             turned = turned + mm(high, one) + mm((values - high.astype(f32)).astype(bf16), one)
+    for load in loads:
+        load.wait()
     adjoint_b = ab[...]
     grad_step = gs[...] + adjoint_b * act_f
     grad_act = g[...] * d_skip[...] + adjoint_b * step[...]
@@ -527,10 +539,7 @@
                     out[(4 * j + q) * D : (4 * j + q + 1) * D] = result[:, q * LANES : (q + 1) * LANES]
 
 
-def late_weights(keep, part_keep, low_own, low_other, got, early, out, whole):
-    total = early[0].astype(f32)
-    for j in range(1, SHARES):
-        total = total + early[j].astype(f32)
+def late_weights(keep, part_keep, low_own, low_other, got, out, whole):
     left = jnp.concatenate([low_own[...], low_other[...]], axis=0)
     rows = HALO + T
     for j in range(D // LANES):
@@ -541,13 +550,24 @@
     for d in range(SHARES):
         main = whole[d * MAIN : (d + 1) * MAIN]
         small = whole[4 * D + d * SMALL : 4 * D + (d + 1) * SMALL]
-        out[d] = jnp.concatenate([total, main, small], axis=0).astype(bf16)
-
-
-def add_late(got, out):
-    total = got[0].astype(f32)[T:]
+        out[d] = jnp.concatenate([main, small], axis=0).astype(bf16)
+
+
+def add_early(early, late, out):
+    total = early[0].astype(f32)
     for j in range(1, SHARES):
-        total = total + got[j].astype(f32)[T:]
+        total = total + early[j].astype(f32)
+    for j in range(SHARES):
+        out[j] = jnp.concatenate([late[j].astype(f32), total], axis=0).astype(bf16)
+
+
+def add_late(got, out, held, sem):
+    copy = pltpu.make_async_copy(got.at[:, pl.ds(0, 3 * N)], held, sem)
+    copy.start()
+    copy.wait()
+    total = held[0].astype(f32)[0:LATE]
+    for j in range(1, SHARES):
+        total = total + held[j].astype(f32)[0:LATE]
     low = total.astype(bf16)
     for j in range(SHARES):
         out[j] = low
@@ -556,7 +576,7 @@
 def finish_early(meta, mine, other, gw_o, gw_q, gw_k, gw_v, gw_out, gw_in, gate, sem):
     is_zero = meta[2 + DOCS] == 0
     for d in reversed(range(SHARES)):
-        a, b = mine[d].astype(f32)[0:T], other[d].astype(f32)[0:T]
+        a, b = mine[d].astype(f32)[LATE:], other[d].astype(f32)[LATE:]
         j, q, r = d // 16, d // 4 % 4, d % 4 * T
         tile = TILES[q]
         (gw_o, gw_q, gw_k, gw_v)[j][r : r + T, tile] = jnp.where(is_zero, a, b)
@@ -574,9 +594,10 @@
 
 def finish_late(
     meta, mine, other, _, gw_in, gw_x, gw_dt, g_a_log, g_conv_w, g_conv_b, g_dt_b, g_skip, g_gain_one,
-    g_gain_two, conv, sem,
+    g_gain_two, conv, sems,
 ):
     is_zero = meta[2 + DOCS] == 0
+    copies = []
     for d in range(SHARES):
         a, b = mine[d].astype(f32), other[d].astype(f32)
         zero = jnp.where(is_zero, a, b)
@@ -584,6 +605,11 @@
         j, r = d // 16, d % 16 * MAIN
         conv[r : r + MAIN, j * LANES : (j + 1) * LANES] = zero[0:MAIN]
         conv[r : r + MAIN, D + j * LANES : D + (j + 1) * LANES] = one[0:MAIN]
+        if d % 16 == 15:
+            for side in range(2):
+                cols = pl.ds(side * D + j * LANES, LANES)
+                copies.append(pltpu.make_async_copy(conv.at[:, cols], gw_in.at[:, cols], sems.at[side, j]))
+                copies[-1].start()
         q, r = d // 8, d % 8 * SMALL
         tile = TILES[q]
         gw_x[r : r + SMALL, tile] = zero[MAIN:]
@@ -597,21 +623,20 @@
                 out[:, tile] = one[at + i : at + i + 1]
             out = g_gain_one if q < 4 else g_gain_two
             out[:, TILES[q % 4]] = one[at + 3 : at + 4]
-    copy = pltpu.make_async_copy(conv, gw_in.at[:, pl.ds(0, E)], sem)
-    copy.start()
-    copy.wait()
+    for copy in copies:
+        copy.wait()
 
 
 MEGABYTES = dict(
-    mamba_in=16, mamba_out=16, attention=16, middle_back=20, early_weights=12, mamba_back=36, late_weights=12,
-    add_late=10, finish_early=24, finish_late=12,
+    mamba_in=16, mamba_out=16, attention=16, middle_back=20, early_weights=12, mamba_back=38, late_weights=12,
+    add_late=8, add_early=14, finish_early=24, finish_late=12,
 )
 
 
-def call(body, name, outs, scratch, *args, smem=True, outside=(), aliases=None, far=(), far_out=()):
+def call(body, name, outs, scratch, *args, smem=True, outside=(), aliases=None, far=(), far_out=(), there=(), sems=()):
     aliases = aliases or {}
     args = [pltpu.with_memory_space_constraint(x, pltpu.HBM) if i in far else x for i, x in enumerate(args)]
-    specs = [pl.BlockSpec(memory_space=pl.ANY if i in aliases else pltpu.VMEM) for i in range(len(args))]
+    specs = [pl.BlockSpec(memory_space=pl.ANY if i in aliases or i in there else pltpu.VMEM) for i in range(len(args))]
     if smem:
         specs[0] = pl.BlockSpec(memory_space=pltpu.SMEM)
     return pl.pallas_call(
@@ -621,7 +646,7 @@
         in_specs=specs,
         out_specs=[pl.BlockSpec(memory_space=pl.ANY if i in outside else pltpu.VMEM) for i in range(len(outs))],
         scratch_shapes=[pltpu.VMEM(s, t) for s, t in scratch]
-        + ([pltpu.SemaphoreType.DMA] if outside else []),
+        + [pltpu.SemaphoreType.DMA(n) for n in sems],
         input_output_aliases=aliases,
         compiler_params=pltpu.CompilerParams(vmem_limit_bytes=MEGABYTES[name] << 20),
     )(*args)
@@ -659,9 +684,9 @@
     w_x = w_x.T
     send, grad_att, low_ext, ext, gate, conv, act, step, pre, bc, dt_low = call(
         mamba_in, "mamba_in",
-        [((BLOCKS, N + 8, E), bf16), tdl, ((HALO + T, D), bf16), ((HALO + T, E), bf16), tel, te, tel, te, te,
+        [((BLOCKS, SENT, LANES), bf16), tdl, ((HALO + T, D), bf16), ((HALO + T, E), bf16), tel, te, tel, te, te,
          ((T // STEPS, 2 * N, 128), f32), ((T, R), bf16)],
-        [((HALO + T, E), f32), te, te, ((T, 128), f32), ((N + 8, E), f32), tn, tn],
+        [((HALO + T, E), f32), te, te, ((T, 128), f32), tn, tn],
         meta, tokens, halo, row(gain_one), w_in, conv_w, row(conv_b), w_x, w_dt, row(dt_bias), a_log, cot, w_o,
         far=(1, 3, 4, 5, 6, 7, 8, 9, 10, 11, 12), far_out=(2, 3, 5, 8, 10),
     )
@@ -684,48 +709,57 @@
     wide = ((T, 6 * D), bf16)
     send, mixed, grad_mid, g, grad_gate, keep, give, g_gain_two, g_skip = call(
         middle_back, "middle_back",
-        [((BLOCKS, N, E), bf16), tdl, td, te, tel, wide, wide, ((1, D), f32), ((1, E), f32)],
-        [tdl] * 4 + [te, tn, tn],
+        [((BLOCKS, N * 8, LANES), bf16), tdl, td, te, tel, wide, wide, ((1, D), f32), ((1, E), f32)],
+        [tdl] * 4 + [te, tn],
         meta, swap(back), cot, middle, normed, low_ext, gated, gate, ssm, act, step, bc, a_log,
-        row(d_skip), w_o, w_q, w_k, w_v, w_out, row(gain_two), far_out=(1, 2, 3, 4, 7, 8),
+        row(d_skip), w_o, w_q, w_k, w_v, w_out, row(gain_two), far_out=(1, 2, 3, 4, 5, 7, 8),
     )
     (early,) = call(
         early_weights, "early_weights", [((16 * D, LANES), bf16)], [((2 * T, 6 * D), bf16)],
-        meta, keep, partner(give),
-    )
-    early, behind = lax.optimization_barrier((early, swap(send)))
+        meta, keep, partner(give), far=(1,),
+    )
+    early, behind, low_other = lax.optimization_barrier((early, swap(send), low_other))
     early = trade(early.reshape(SHARES, T, LANES))
     grad_tokens, tail, keep, give, part_keep = call(
         mamba_back, "mamba_back",
         [td, ((8, D), f32), ((HALO + T, D), bf16), ((4 * (HALO + T) + D, 128), bf16), ((D, 128), f32)],
         [te, te, ((T, N, E), f32), ((T, N, E), f32), te, te, ((HALO + T, E), f32),
          ((T + 8, E), f32), ((HALO + T, E), f32), ((N, E), f32), ((64, E), f32), tn, tn,
-         ((T, N, LANES), f32), ((T, N, LANES), f32)],
+         ((T, N, LANES), f32), ((T, N, LANES), f32),
+         te, ((T, R), bf16), te, ((HALO + T, E), bf16), ((64, E), bf16), ((R, E), bf16), tdl, ((D, 2 * E), bf16), tel, td],
         meta, behind, forward, start, g, act, step, pre, bc, dt_low, conv, ext, a_log,
         row(d_skip), conv_w, w_x, w_dt, tokens, halo, row(gain_one), w_in, grad_gate, grad_mid,
         g_gain_two, g_skip, far=tuple(range(1, 25)), far_out=(0, 1, 2, 4),
-    )
+        there=(7, 9, 10, 11, 15, 16, 17, 20, 21, 22), sems=((10,),),
+    )
+    early, tail = lax.optimization_barrier((early, shift(tail, -1)))
     (late,) = call(
-        late_weights, "late_weights", [((SHARES, T + MAIN + SMALL, LANES), bf16)], [((5 * D, LANES), f32)],
-        keep, part_keep, low_ext, low_other, partner(give), early, smem=False,
-        far=(0, 1, 2, 3, 4, 5), far_out=(0,),
-    )
-    shares = trade(late)
-    (late,) = call(add_late, "add_late", [((SHARES, MAIN + SMALL, LANES), bf16)], [], shares, smem=False, far=(0,))
+        late_weights, "late_weights", [((SHARES, LATE, LANES), bf16)], [((5 * D, LANES), f32)],
+        keep, part_keep, low_ext, low_other, partner(give), smem=False, far=(0, 1, 2, 3, 4), far_out=(0,),
+    )
+    (both,) = call(
+        add_early, "add_early", [((SHARES, LATE + T, LANES), bf16)], [], early, late, smem=False,
+        far=(1,), far_out=(0,),
+    )
+    shares = trade(both)
+    (late,) = call(
+        add_late, "add_late", [((SHARES, LATE, LANES), bf16)], [((SHARES, 3 * N, LANES), bf16)],
+        shares, smem=False, far=(0,), there=(0,), sems=((),),
+    )
     late = trade(late)
     gw_o, gw_q, gw_k, gw_v, gw_out, gw_in = call(
         finish_early, "finish_early",
         [((D, D), f32)] * 4 + [((E, D), f32), ((D, 2 * E), f32)], [((D, E), f32)],
-        meta, shares, partner(shares), outside=(5,), far=(1, 2),
-    )
-    grad_tokens = grad_tokens.at[T - 8 :].add(shift(tail, -1))
+        meta, shares, partner(shares), outside=(5,), far=(1, 2), sems=((),),
+    )
+    grad_tokens = grad_tokens.at[T - 8 :].add(tail)
     late, gw_in, grad_tokens = lax.optimization_barrier((late, gw_in, grad_tokens))
     gw_in, gw_x, gw_dt, g_a_log, g_conv_w, g_conv_b, g_dt_b, g_skip, g_gain_one, g_gain_two = call(
         finish_late, "finish_late",
         [((D, 2 * E), f32), ((64, E), f32), ((R, E), f32), tn, ((KERNEL, E), f32), ((1, E), f32),
          ((1, E), f32), ((1, E), f32), ((1, D), f32), ((1, D), f32)],
         [((D, E), f32)],
-        meta, late, partner(late), gw_in, outside=(0,), aliases={3: 0},
+        meta, late, partner(late), gw_in, outside=(0,), aliases={3: 0}, sems=((2, 4),),
     )
     return (
         mixed[None], grad_tokens[None], g_gain_one[0], gw_in, g_conv_w, g_conv_b[0], gw_x.T, gw_dt,

time: 214 us -> 210 us (0.981)
  waiting for transfers between devices: 19.7 us -> 15.8 us
    ppermute x2, waiting for transfers between devices: 5.19 us -> 1.68 us  [shift(): return lax.ppermute(x, PLACE, pairs)]
    all_to_all x1, blocking collectives: 42.7 us -> 45.3 us  [trade(): return lax.all_to_all(x, SAME, 0, 0, tiled=True)]
    all_to_all x2, waiting for transfers between devices: 3.49 us -> 5.85 us  [trade(): return lax.all_to_all(x, SAME, 0, 0, tiled=True)]
    all_to_all x3, blocking collectives: 47.4 us -> 45.1 us  [swap(): return lax.all_to_all(x, PLACE, 0, 0, tiled=True)]
    pallas_call x10 -> x11, Pallas kernels: 65.7 us -> 64.8 us  [call(): pl.pallas_call(body, name=name, out_shape=[pltpu.HBM(s, t) if i in far_ou...]
  transfers between devices with their start and end apart: 10 -> 10, of which waited for: 5 -> 5; matrix products, arithmetic and copies ran while one was open for 1% -> 1% of each run, Pallas kernels for 16% -> 17%
where the time goes in v3:
time: 210 us; the launch traced here: 209 us
  blocking collectives  90.4 us (43%)
  Pallas kernels  64.8 us (31%)
  starting transfers between devices  32.6 us (16%)
  waiting for transfers between devices  15.8 us (8%)
  local copies, waits for them, and re-layouts  2.31 us (1%)
  other arithmetic  2.14 us (1%)
    pallas_call x11, Pallas kernels, call(): pl.pallas_call(body, name=name, out_shape=[pltpu.HBM(s, t) if i in far_ou...  64.8 us
    all_to_all x1, blocking collectives, trade(): return lax.all_to_all(x, SAME, 0, 0, tiled=True)  45.3 us
    all_to_all x3, blocking collectives, swap(): return lax.all_to_all(x, PLACE, 0, 0, tiled=True)  45.1 us
    all_to_all x2, starting transfers between devices, trade(): return lax.all_to_all(x, SAME, 0, 0, tiled=True)  12.1 us
    ppermute x5, starting transfers between devices, partner(): return lax.ppermute(x, 'core', [(0, 1), (1, 0)])  11.3 us
    all_to_all x1, waiting for transfers between devices, swap(): return lax.all_to_all(x, PLACE, 0, 0, tiled=True)  6.54 us
    all_to_all x2, waiting for transfers between devices, trade(): return lax.all_to_all(x, SAME, 0, 0, tiled=True)  5.85 us
    ppermute x2, starting transfers between devices, shift(): return lax.ppermute(x, PLACE, pairs)  5.64 us
  transfers between devices with their start and end apart: 10, of which 5 were waited for; matrix products, arithmetic and copies ran while one was open for 1% of the time, Pallas kernels for 17%

profile of v3, /device:TPU:1, one launch (start us, length us, event | category | flops | bytes accessed | tf_op | source)
XLA Modules:
  0.0 209.3 jit_solution(1065471481420465422)
XLA Ops:
  0.7 0.8 slice_bitcast_fusion
  1.5 4.4 %collective-permute-start = (bf16[16,512]{1,0:T(8,128)(2,1)S(1)}, bf16[16,512]{1,0:T(8,128)(2,1)S(1)}, u32[]{:S(2)}, u32[]{:S(2)}) collective-permute-start(bf16[16,512]{1,0:T(8,128)(2,1)S(1)} %slice_bitcast_fusion), channel_id=1, source_target_pairs={{0,1},{1,2},{2,3},{3,4},{4,5},{5,6},{6,7},{7,8},{8,9},{9,10},{10,1... | collective-permute-start | bytes 49160 | tf_op jit(solution)/shard_map/ppermute | solution.py:657
  6.0 0.8 pad_add_fusion.meta
  6.8 6.8 %mamba_in.1 = (bf16[16,144,128]{2,1,0:T(8,128)(2,1)S(1)}, bf16[128,512]{1,0:T(8,128)(2,1)S(1)}, bf16[144,512]{1,0:T(8,128)(2,1)}, bf16[144,1024]{1,0:T(8,128)(2,...) custom-call(s32[9]{0:T(128)S(1)} %pad_add_fusion.meta, ...), custom_call_target="tpu_custom_call" | custom-call | tf_op jit(solution)/shard_map/mamba_in/pallas_call | solution.py:642
  13.6 17.2 %all_to_all.35.got.forward = bf16[16,144,128]{2,1,0:T(8,128)(2,1)S(1)} all-to-all(bf16[16,144,128]{2,1,0:T(8,128)(2,1)S(1)} %get-tuple-element.84), channel_id=1, replica_groups=mesh['y'=4,'core'=2,'seq'=4,'head'=4] {'seq','head'}, dimensions={0} | all-to-all | bytes 1179648 | tf_op jit(solution)/shard_map/all_to_all | solution.py:661
  30.9 4.6 %mamba_out.1 = (bf16[16,192,128]{2,1,0:T(8,128)(2,1)S(1)}, f32[16,1024]{1,0:T(8,128)}, f32[128,1024]{1,0:T(8,128)S(1)}, bf16[128,1024]{1,0:T(8,128)(2,1)S(1)}, f...) custom-call(s32[9]{0:T(128)S(1)} %pad_add_fusion.meta, bf16[16,144,128]{2,1,0:T(8,128)(2,1)S(1)} %all_to_all.35.got.forward, ...), custom_call_target="tpu_custom_call" | custom-call | tf_op jit(solution)/shard_map/mamba_out/pallas_call | solution.py:642
  35.5 14.1 %all_to_all.36.got = bf16[16,192,128]{2,1,0:T(8,128)(2,1)S(1)} all-to-all(bf16[16,192,128]{2,1,0:T(8,128)(2,1)S(1)} %get-tuple-element.90), channel_id=1, replica_groups=mesh['y'=4,'core'=2,'seq'=4,'head'=4] {'seq','head'}, dimensions={0} | all-to-all | bytes 1572864 | tf_op jit(solution)/shard_map/all_to_all | solution.py:661
  49.6 7.1 %attention.1 = bf16[16,192,128]{2,1,0:T(8,128)(2,1)S(1)} custom-call(s32[9]{0:T(128)S(1)} %pad_add_fusion.meta, bf16[16,192,128]{2,1,0:T(8,128)(2,1)S(1)} %all_to_all.36.got), custom_call_target="tpu_custom_call" | custom-call | tf_op jit(solution)/shard_map/attention/pallas_call | solution.py:642
  56.7 13.8 %all_to_all.37.got = bf16[16,192,128]{2,1,0:T(8,128)(2,1)S(1)} all-to-all(bf16[16,192,128]{2,1,0:T(8,128)(2,1)S(1)} %attention.1), channel_id=1, replica_groups=mesh['y'=4,'core'=2,'seq'=4,'head'=4] {'seq','head'}, dimensions={0} | all-to-all | bytes 1572864 | tf_op jit(solution)/shard_map/all_to_all | solution.py:661
  70.6 5.8 %middle_back.1 = (bf16[16,128,128]{2,1,0:T(8,128)(2,1)}, bf16[128,512]{1,0:T(8,128)(2,1)}, f32[128,512]{1,0:T(8,128)}, f32[128,1024]{1,0:T(8,128)}, bf16[128,102...) custom-call(s32[9]{0:T(128)S(1)} %pad_add_fusion.meta, ...), custom_call_target="tpu_custom_call" | custom-call | tf_op jit(solution)/shard_map/middle_back/pallas_call | solution.py:642
  76.4 5.6 %collective-permute-start.1 = (bf16[128,3072]{1,0:T(8,128)(2,1)S(1)}, bf16[128,3072]{1,0:T(8,128)(2,1)S(1)}, u32[]{:S(2)}, u32[]{:S(2)}) collective-permute-start(bf16[128,3072]{1,0:T(8,128)(2,1)S(1)} %get-tuple-element.98), channel_id=1, source_target_pairs={{0,16},{16,0},{1,17},{17,1},{2,18},{18,2},{3,19},{19,3},{4,20},{20... | collective-permute-start | bytes 2359304 | tf_op jit(solution)/shard_map/ppermute | solution.py:665
  82.0 3.6 %all-to-all-start.3 = ((bf16[16,128,128]{2,1,0:T(8,128)(2,1)}), bf16[16,128,128]{2,1,0:T(8,128)(2,1)S(1)}, u32[]{:S(2)}, u32[]{:S(2)}) async-start(bf16[16,128,128]{2,1,0:T(8,128)(2,1)} %get-tuple-element.99), calls=%async_computation.3 | async-start | bytes 1048576 | tf_op jit(solution)/shard_map/all_to_all | solution.py:661
  86.4 3.3 %early_weights.1 = bf16[8192,128]{1,0:T(8,128)(2,1)} custom-call(s32[9]{0:T(128)S(1)} %copy-done.17, bf16[128,3072]{1,0:T(8,128)(2,1)} %get-tuple-element.97.keep, bf16[128,3072]{1,0:T(8,128)(2,1)S(1)} %collective-permute-done.1.got), custom_call_target="tpu_custom_call" | custom-call | tf_op jit(solution)/shard_map/early_weights/pallas_call | solution.py:642
  89.8 6.5 %all-to-all-done.3.got = bf16[16,128,128]{2,1,0:T(8,128)(2,1)S(1)} async-done(((bf16[16,128,128]{2,1,0:T(8,128)(2,1)}), bf16[16,128,128]{2,1,0:T(8,128)(2,1)S(1)}, u32[]{:S(2)}, u32[]{:S(2)}) %all-to-all-start.3) | async-done | bytes 524320 | tf_op jit(solution)/shard_map/all_to_all | solution.py:661
  96.3 7.5 %all-to-all-start.4 = ((bf16[64,128,128]{2,1,0:T(8,128)(2,1)}), bf16[64,128,128]{2,1,0:T(8,128)(2,1)S(1)}, u32[]{:S(2)}, u32[]{:S(2)}) async-start(bf16[64,128,128]{2,1,0:T(8,128)(2,1)} %bitcast.14), calls=%async_computation.4 | async-start | bytes 4194304 | tf_op jit(solution)/shard_map/all_to_all | solution.py:669
  103.8 19.4 %mamba_back.1 = (f32[128,512]{1,0:T(8,128)}, f32[8,512]{1,0:T(8,128)}, bf16[144,512]{1,0:T(8,128)(2,1)}, bf16[1088,128]{1,0:T(8,128)(2,1)S(1)}, f32[512,128]{1,0:T(8,128)}) custom-call(s32[9]{0:T(128)S(1)} %copy-done.18, bf16[16,128,128]{2,1,0:T(8,128)(2,1)} %copy-done.21, bf16[16,144,128]{2,1,0:T(8,128)(2,1)} %copy-done, ...), custom_call_target="tpu_custom_call" | custom-call | tf_op jit(solution)/shard_map/mamba_back/pallas_call | solution.py:642
  123.2 1.4 collective-permute-start.4
  124.6 1.3 collective-permute-start.3
  125.9 0.7 copy-done.22
  126.6 2.7 %late_weights.1.late = bf16[64,40,128]{2,1,0:T(8,128)(2,1)} custom-call(bf16[144,512]{1,0:T(8,128)(2,1)} %get-tuple-element.114.keep, f32[512,128]{1,0:T(8,128)} %get-tuple-element.115.part_keep, bf16[144,512]{1,0:T(8,128)(2,1)} %get-tuple-element.93.low_ext.low_own, bf16[144,512]{1,0:T(8,128)(2,1)} %copy-done.23, bf16[1088,128]{1,0:T(8,128)(2,1)} %copy-done.22), custom_call_target="tpu_custom_call" | custom-call | tf_op jit(solution)/shard_map/late_weights/pallas_call | solution.py:642
  129.3 1.7 collective-permute-done.3
  131.1 3.1 %add_early.1 = bf16[64,168,128]{2,1,0:T(8,128)(2,1)} custom-call(bf16[64,128,128]{2,1,0:T(8,128)(2,1)S(1)} %all-to-all-done.4.early, bf16[64,40,128]{2,1,0:T(8,128)(2,1)} %late_weights.1.late), custom_call_target="tpu_custom_call" | custom-call | tf_op jit(solution)/shard_map/add_early/pallas_call | solution.py:642
  134.2 45.3 %all_to_all.38.got.mine = bf16[64,168,128]{2,1,0:T(8,128)(2,1)} all-to-all(bf16[64,168,128]{2,1,0:T(8,128)(2,1)} %add_early.1), channel_id=1, replica_groups=mesh['y'=4,'core'=2,'seq'=4,'head'=4] {'y','seq','head'}, dimensions={0} | all-to-all | bytes 5505024 | tf_op jit(solution)/shard_map/all_to_all | solution.py:669
  179.5 2.7 %collective-permute-start.5 = (bf16[64,168,128]{2,1,0:T(8,128)(2,1)}, bf16[64,168,128]{2,1,0:T(8,128)(2,1)}, u32[]{:S(2)}, u32[]{:S(2)}) collective-permute-start(bf16[64,168,128]{2,1,0:T(8,128)(2,1)} %all_to_all.38.got.mine), channel_id=1, source_target_pairs={{0,16},{16,0},{1,17},{17,1},{2,18},{18,2},{3,19},{19,3},{4,20},{20... | collective-permute-start | bytes 8257544 | tf_op jit(solution)/shard_map/ppermute | solution.py:665
  182.2 2.1 %add_late.1 = bf16[64,40,128]{2,1,0:T(8,128)(2,1)} custom-call(bf16[64,168,128]{2,1,0:T(8,128)(2,1)} %all_to_all.38.got.mine), custom_call_target="tpu_custom_call" | custom-call | tf_op jit(solution)/shard_map/add_late/pallas_call | solution.py:642
  184.4 4.7 %all-to-all-start.6 = ((bf16[64,40,128]{2,1,0:T(8,128)(2,1)}), bf16[64,40,128]{2,1,0:T(8,128)(2,1)S(1)}, u32[]{:S(2)}, u32[]{:S(2)}) async-start(bf16[64,40,128]{2,1,0:T(8,128)(2,1)} %add_late.1), calls=%async_computation.6 | async-start | bytes 1310720 | tf_op jit(solution)/shard_map/all_to_all | solution.py:669
  189.0 1.3 add_dynamic-update-slice_fusion
  190.4 7.1 %finish_early.1 = (f32[512,512]{1,0:T(8,128)}, f32[512,512]{1,0:T(8,128)}, f32[512,512]{1,0:T(8,128)}, f32[512,512]{1,0:T(8,128)}, f32[1024,512]{1,0:T(8,128)}, /*index=5*/f32[512,2048]{1,0:T(8,128)}) custom-call(s32[9]{0:T(128)S(1)} %copy-done.18, bf16[64,168,128]{2,1,0:T(8,128)(2,1)} %all_to_all.38.got.mine, bf16[64,168,128]{2,1,0:T(8,128)(2,1)} %collective-permute-done.5.other), custom_call_target="tpu_custom_call" | custom-call | tf_op jit(solution)/shard_map/finish_early/pallas_call | solution.py:642
  197.4 5.7 %all-to-all-done.6.mine = bf16[64,40,128]{2,1,0:T(8,128)(2,1)S(1)} async-done(((bf16[64,40,128]{2,1,0:T(8,128)(2,1)}), bf16[64,40,128]{2,1,0:T(8,128)(2,1)S(1)}, u32[]{:S(2)}, u32[]{:S(2)}) %all-to-all-start.6) | async-done | bytes 655392 | tf_op jit(solution)/shard_map/all_to_all | solution.py:669
  203.1 1.5 collective-permute-start.6
  204.6 1.7 collective-permute-done.6.other
  206.3 2.8 %finish_late.1 = (f32[512,2048]{1,0:T(8,128)}, f32[64,1024]{1,0:T(8,128)}, f32[32,1024]{1,0:T(8,128)}, f32[16,1024]{1,0:T(8,128)}, f32[4,1024]{1,0:T(4,128)}, /*...) custom-call(s32[9]{0:T(128)S(1)} %copy-done.18, ...), custom_call_target="tpu_custom_call", output_to_operand_aliasing={{0}: (3, {})} | custom-call | tf_op jit(solution)/shard_map/finish_late/pallas_call | solution.py:642
  (54 shorter events, 1.1 us)
Async XLA Ops:
  0.7 30.2 %copy-start.10 = (bf16[1,128,512]{2,1,0:T(8,128)(2,1)S(1)}, bf16[1,128,512]{2,1,0:T(8,128)(2,1)}, u32[]{:S(2)}) copy-start(bf16[1,128,512]{2,1,0:T(8,128)(2,1)} %param.20) | copy-start | bytes 393220
  0.7 30.2 %copy-start.11 = (f32[16,1024]{1,0:T(8,128)S(1)}, f32[16,1024]{1,0:T(8,128)}, u32[]{:S(2)}) copy-start(f32[16,1024]{1,0:T(8,128)} %a_log.7) | copy-start | bytes 196612
  0.7 30.2 %copy-start.2 = (bf16[1024,512]{1,0:T(8,128)(2,1)S(1)}, bf16[1024,512]{1,0:T(8,128)(2,1)}, u32[]{:S(2)}) copy-start(bf16[1024,512]{1,0:T(8,128)(2,1)} %w_out.3) | copy-start | bytes 3145732
  0.7 30.2 %copy-start.6 = (bf16[512,512]{1,0:T(8,128)(2,1)S(1)}, bf16[512,512]{1,0:T(8,128)(2,1)}, u32[]{:S(2)}) copy-start(bf16[512,512]{1,0:T(8,128)(2,1)} %w_q.3) | copy-start | bytes 1572868
  1.5 5.2 %collective-permute-start = (bf16[16,512]{1,0:T(8,128)(2,1)S(1)}, bf16[16,512]{1,0:T(8,128)(2,1)S(1)}, u32[]{:S(2)}, u32[]{:S(2)}) collective-permute-start(bf16[16,512]{1,0:T(8,128)(2,1)S(1)} %slice_bitcast_fusion), channel_id=1, source_target_pairs={{0,1},{1,2},{2,3},{3,4},{4,5},{5,6},{6,7},{7,8},{8,9},{9,10},{10,1... | collective-permute-start | bytes 49160 | tf_op jit(solution)/shard_map/ppermute | solution.py:657
  5.9 24.9 %copy-start.8 = (bf16[512,512]{1,0:T(8,128)(2,1)S(1)}, bf16[512,512]{1,0:T(8,128)(2,1)}, u32[]{:S(2)}) copy-start(bf16[512,512]{1,0:T(8,128)(2,1)} %w_k.3) | copy-start | bytes 1572868
  5.9 24.9 %copy-start.9 = (bf16[512,512]{1,0:T(8,128)(2,1)S(1)}, bf16[512,512]{1,0:T(8,128)(2,1)}, u32[]{:S(2)}) copy-start(bf16[512,512]{1,0:T(8,128)(2,1)} %w_v.3) | copy-start | bytes 1572868
  5.9 24.9 %copy-start.19 = (f32[1024]{0:T(1024)S(1)}, f32[1024]{0:T(1024)}, u32[]{:S(2)}) copy-start(f32[1024]{0:T(1024)} %param.30) | copy-start | bytes 12292
  6.0 24.9 %copy-start.20 = (f32[512]{0:T(512)S(1)}, f32[512]{0:T(512)}, u32[]{:S(2)}) copy-start(f32[512]{0:T(512)} %param.32) | copy-start | bytes 6148
  6.8 63.7 %copy-start.16 = (s32[9]{0:T(128)}, s32[9]{0:T(128)S(1)}, u32[]{:S(2)}) copy-start(s32[9]{0:T(128)S(1)} %pad_add_fusion.meta) | copy-start | bytes 112
  6.8 28.7 %copy-start.15 = (bf16[16,512]{1,0:T(8,128)(2,1)}, bf16[16,512]{1,0:T(8,128)(2,1)S(1)}, u32[]{:S(2)}) copy-start(bf16[16,512]{1,0:T(8,128)(2,1)S(1)} %collective-permute-done.halo) | copy-start | bytes 49156
  13.6 56.9 %copy-start.1 = (f32[128,1024]{1,0:T(8,128)}, f32[128,1024]{1,0:T(8,128)S(1)}, u32[]{:S(2)}) copy-start(f32[128,1024]{1,0:T(8,128)S(1)} %get-tuple-element.85.step) | copy-start | bytes 1572868
  13.6 56.9 %copy-start.3 = (bf16[128,1024]{1,0:T(8,128)(2,1)}, bf16[128,1024]{1,0:T(8,128)(2,1)S(1)}, u32[]{:S(2)}) copy-start(bf16[128,1024]{1,0:T(8,128)(2,1)S(1)} %get-tuple-element.86.act) | copy-start | bytes 786436
  13.6 56.9 %copy-start.4 = (f32[16,32,128]{2,1,0:T(8,128)}, f32[16,32,128]{2,1,0:T(8,128)S(1)}, u32[]{:S(2)}) copy-start(f32[16,32,128]{2,1,0:T(8,128)S(1)} %get-tuple-element.87.bc) | copy-start | bytes 786436
  30.8 18.8 %copy-start = (bf16[16,144,128]{2,1,0:T(8,128)(2,1)}, bf16[16,144,128]{2,1,0:T(8,128)(2,1)S(1)}, u32[]{:S(2)}) copy-start(bf16[16,144,128]{2,1,0:T(8,128)(2,1)S(1)} %all_to_all.35.got.forward) | copy-start | bytes 1769476
  35.5 35.0 %copy-start.5 = (bf16[512,512]{1,0:T(8,128)(2,1)S(1)}, bf16[512,512]{1,0:T(8,128)(2,1)}, u32[]{:S(2)}) copy-start(bf16[512,512]{1,0:T(8,128)(2,1)} %w_o.3) | copy-start | bytes 1572868
  35.5 35.0 %copy-start.7 = (bf16[512,512]{1,0:T(8,128)(2,1)S(1)}, bf16[512,512]{1,0:T(8,128)(2,1)}, u32[]{:S(2)}) copy-start(bf16[512,512]{1,0:T(8,128)(2,1)} %w_q.3) | copy-start | bytes 1572868
  35.5 35.0 %copy-start.12 = (bf16[144,512]{1,0:T(8,128)(2,1)S(1)}, bf16[144,512]{1,0:T(8,128)(2,1)}, u32[]{:S(2)}) copy-start(bf16[144,512]{1,0:T(8,128)(2,1)} %get-tuple-element.93.low_ext.low_own) | copy-start | bytes 442372
  35.5 35.0 %copy-start.14 = (bf16[1,128,512]{2,1,0:T(8,128)(2,1)S(1)}, bf16[1,128,512]{2,1,0:T(8,128)(2,1)}, u32[]{:S(2)}) copy-start(bf16[1,128,512]{2,1,0:T(8,128)(2,1)} %param.37) | copy-start | bytes 393220
  70.6 15.1 %copy-start.13 = (bf16[144,512]{1,0:T(8,128)(2,1)S(1)}, bf16[144,512]{1,0:T(8,128)(2,1)}, u32[]{:S(2)}) copy-start(bf16[144,512]{1,0:T(8,128)(2,1)} %get-tuple-element.93.low_ext.low_own) | copy-start | bytes 442372
  76.4 9.4 %collective-permute-start.1 = (bf16[128,3072]{1,0:T(8,128)(2,1)S(1)}, bf16[128,3072]{1,0:T(8,128)(2,1)S(1)}, u32[]{:S(2)}, u32[]{:S(2)}) collective-permute-start(bf16[128,3072]{1,0:T(8,128)(2,1)S(1)} %get-tuple-element.98), channel_id=1, source_target_pairs={{0,16},{16,0},{1,17},{17,1},{2,18},{18,2},{3,19},{19,3},{4,20},{20... | collective-permute-start | bytes 2359304 | tf_op jit(solution)/shard_map/ppermute | solution.py:665
  82.0 14.3 %all-to-all-start.3 = ((bf16[16,128,128]{2,1,0:T(8,128)(2,1)}), bf16[16,128,128]{2,1,0:T(8,128)(2,1)S(1)}, u32[]{:S(2)}, u32[]{:S(2)}) async-start(bf16[16,128,128]{2,1,0:T(8,128)(2,1)} %get-tuple-element.99), calls=%async_computation.3 | async-start | bytes 1048576 | tf_op jit(solution)/shard_map/all_to_all | solution.py:661
  85.6 4.1 %collective-permute-start.2 = (bf16[144,512]{1,0:T(8,128)(2,1)S(1)}, bf16[144,512]{1,0:T(8,128)(2,1)S(1)}, u32[]{:S(2)}, u32[]{:S(2)}) collective-permute-start(bf16[144,512]{1,0:T(8,128)(2,1)S(1)} %copy-done.13), channel_id=1, source_target_pairs={{0,16},{16,0},{1,17},{17,1},{2,18},{18,2},{3,19},{19,3},{4,20},{20... | collective-permute-start | bytes 442376 | tf_op jit(solution)/shard_map/ppermute | solution.py:665
  89.8 14.0 %copy-start.18 = (s32[9]{0:T(128)S(1)}, s32[9]{0:T(128)}, u32[]{:S(2)}) copy-start(s32[9]{0:T(128)} %copy-done.16) | copy-start | bytes 112
  89.8 33.5 %copy-start.23 = (bf16[144,512]{1,0:T(8,128)(2,1)}, bf16[144,512]{1,0:T(8,128)(2,1)S(1)}, u32[]{:S(2)}) copy-start(bf16[144,512]{1,0:T(8,128)(2,1)S(1)} %collective-permute-done.2.low_other) | copy-start | bytes 442372
  96.3 7.5 %copy-start.21 = (bf16[16,128,128]{2,1,0:T(8,128)(2,1)}, bf16[16,128,128]{2,1,0:T(8,128)(2,1)S(1)}, u32[]{:S(2)}) copy-start(bf16[16,128,128]{2,1,0:T(8,128)(2,1)S(1)} %all-to-all-done.3.got) | copy-start | bytes 1572868
  96.3 34.8 %all-to-all-start.4 = ((bf16[64,128,128]{2,1,0:T(8,128)(2,1)}), bf16[64,128,128]{2,1,0:T(8,128)(2,1)S(1)}, u32[]{:S(2)}, u32[]{:S(2)}) async-start(bf16[64,128,128]{2,1,0:T(8,128)(2,1)} %bitcast.14), calls=%async_computation.4 | async-start | bytes 4194304 | tf_op jit(solution)/shard_map/all_to_all | solution.py:669
  123.2 2.7 %collective-permute-start.4 = (bf16[1088,128]{1,0:T(8,128)(2,1)S(1)}, bf16[1088,128]{1,0:T(8,128)(2,1)S(1)}, u32[]{:S(2)}, u32[]{:S(2)}) collective-permute-start(bf16[1088,128]{1,0:T(8,128)(2,1)S(1)} %get-tuple-element.117), channel_id=1, source_target_pairs={{0,16},{16,0},{1,17},{17,1},{2,18},{18,2},{3,19},{19,3},{4,20},{20... | collective-permute-start | bytes 835592 | tf_op jit(solution)/shard_map/ppermute | solution.py:665
  124.6 6.3 %collective-permute-start.3 = (f32[8,512]{1,0:T(8,128)}, f32[8,512]{1,0:T(8,128)S(1)}, u32[]{:S(2)}, u32[]{:S(2)}) collective-permute-start(f32[8,512]{1,0:T(8,128)} %get-tuple-element.112), channel_id=1, source_target_pairs={{1,0},{2,1},{3,2},{4,3},{5,4},{6,5},{7,6},{8,7},{9,8},{10,9},{11,1... | collective-permute-start | bytes 49160 | tf_op jit(solution)/shard_map/ppermute | solution.py:657
  179.5 10.8 %collective-permute-start.5 = (bf16[64,168,128]{2,1,0:T(8,128)(2,1)}, bf16[64,168,128]{2,1,0:T(8,128)(2,1)}, u32[]{:S(2)}, u32[]{:S(2)}) collective-permute-start(bf16[64,168,128]{2,1,0:T(8,128)(2,1)} %all_to_all.38.got.mine), channel_id=1, source_target_pairs={{0,16},{16,0},{1,17},{17,1},{2,18},{18,2},{3,19},{19,3},{4,20},{20... | collective-permute-start | bytes 8257544 | tf_op jit(solution)/shard_map/ppermute | solution.py:665
  184.4 18.8 %all-to-all-start.6 = ((bf16[64,40,128]{2,1,0:T(8,128)(2,1)}), bf16[64,40,128]{2,1,0:T(8,128)(2,1)S(1)}, u32[]{:S(2)}, u32[]{:S(2)}) async-start(bf16[64,40,128]{2,1,0:T(8,128)(2,1)} %add_late.1), calls=%async_computation.6 | async-start | bytes 1310720 | tf_op jit(solution)/shard_map/all_to_all | solution.py:669
  203.1 3.2 %collective-permute-start.6 = (bf16[64,40,128]{2,1,0:T(8,128)(2,1)S(1)}, bf16[64,40,128]{2,1,0:T(8,128)(2,1)S(1)}, u32[]{:S(2)}, u32[]{:S(2)}) collective-permute-start(bf16[64,40,128]{2,1,0:T(8,128)(2,1)S(1)} %all-to-all-done.6.mine), channel_id=1, source_target_pairs={{0,16},{16,0},{1,17},{17,1},{2,18},{18,2},{3,19},{19,3},{4,20},{20... | collective-permute-start | bytes 1966088 | tf_op jit(solution)/shard_map/ppermute | solution.py:665
  (2 other events, 1.4 us)

commit v4 on v3

--- a/solution.py
+++ b/solution.py
@@ -295,8 +295,8 @@
 def middle_back(
     meta, got, cot, middle, normed, low_ext, gated, gate, ssm, act, step, bc, a_log, d_skip,
     w_o, w_q, w_k, w_v, w_out, gain,
-    send, mixed, grad_mid_out, g_out, grad_gate_out, keep, give, g_gain, g_skip,
-    att, dq, dk, dv, dec, rates2,
+    send, mixed_far, grad_mid_far, g_far, grad_gate_far, keep_far, give, g_gain, g_skip,
+    att, dq, dk, dv, dec, rates2, mixed, grad_mid_out, g_out, grad_gate_out, keep, sems,
 ):
     low = lax.broadcasted_iota(i32, (HALF, 128), 1) < HALF
     low_t = lax.broadcasted_iota(i32, (T, 128), 1) < HALF
@@ -344,6 +344,14 @@
             second[:, 2 * E : 3 * E] = grad_gate
 
     g_skip[...] = jnp.sum(g * act[...].astype(f32), axis=0, keepdims=True)
+    saves = [
+        pltpu.make_async_copy(held, place, sems.at[i])
+        for i, (held, place) in enumerate(
+            ((mixed, mixed_far), (grad_mid_out, grad_mid_far), (g_out, g_far), (grad_gate_out, grad_gate_far), (keep, keep_far))
+        )
+    ]
+    for save in saves:
+        save.start()
     dec[...] = step[...] + reset_of(meta, columns(0, meta))
     rates2[...] = -jnp.exp(a_log[...]) * LOG2E
 
@@ -363,6 +371,8 @@
     ended = jnp.concatenate(carry, axis=0).astype(bf16)
     for j in range(BLOCKS):
         send[j] = ended
+    for save in saves:
+        save.wait()
 
 
 def mamba_back(
@@ -710,9 +720,10 @@
     send, mixed, grad_mid, g, grad_gate, keep, give, g_gain_two, g_skip = call(
         middle_back, "middle_back",
         [((BLOCKS, N * 8, LANES), bf16), tdl, td, te, tel, wide, wide, ((1, D), f32), ((1, E), f32)],
-        [tdl] * 4 + [te, tn],
+        [tdl] * 4 + [te, tn, tdl, td, te, tel, wide],
         meta, swap(back), cot, middle, normed, low_ext, gated, gate, ssm, act, step, bc, a_log,
         row(d_skip), w_o, w_q, w_k, w_v, w_out, row(gain_two), far_out=(1, 2, 3, 4, 5, 7, 8),
+        outside=(1, 2, 3, 4, 5), sems=((5,),),
     )
     (early,) = call(
         early_weights, "early_weights", [((16 * D, LANES), bf16)], [((2 * T, 6 * D), bf16)],
@@ -732,10 +743,9 @@
         g_gain_two, g_skip, far=tuple(range(1, 25)), far_out=(0, 1, 2, 4),
         there=(7, 9, 10, 11, 15, 16, 17, 20, 21, 22), sems=((10,),),
     )
-    early, tail = lax.optimization_barrier((early, shift(tail, -1)))
     (late,) = call(
         late_weights, "late_weights", [((SHARES, LATE, LANES), bf16)], [((5 * D, LANES), f32)],
-        keep, part_keep, low_ext, low_other, partner(give), smem=False, far=(0, 1, 2, 3, 4), far_out=(0,),
+        keep, part_keep, low_ext, low_other, partner(give), smem=False, far=(0, 1, 2, 3), far_out=(0,),
     )
     (both,) = call(
         add_early, "add_early", [((SHARES, LATE + T, LANES), bf16)], [], early, late, smem=False,
@@ -752,7 +762,8 @@
         [((D, D), f32)] * 4 + [((E, D), f32), ((D, 2 * E), f32)], [((D, E), f32)],
         meta, shares, partner(shares), outside=(5,), far=(1, 2), sems=((),),
     )
-    grad_tokens = grad_tokens.at[T - 8 :].add(tail)
+    grad_tokens, gw_in = lax.optimization_barrier((grad_tokens, gw_in))
+    grad_tokens = grad_tokens.at[T - 8 :].add(shift(tail, -1))
     late, gw_in, grad_tokens = lax.optimization_barrier((late, gw_in, grad_tokens))
     gw_in, gw_x, gw_dt, g_a_log, g_conv_w, g_conv_b, g_dt_b, g_skip, g_gain_one, g_gain_two = call(
         finish_late, "finish_late",

time: 210 us -> 207 us (0.986)
  blocking collectives: 90.4 us -> 87.5 us
    all_to_all x1, blocking collectives: 45.3 us -> 42.4 us  [trade(): return lax.all_to_all(x, SAME, 0, 0, tiled=True)]
where the time goes in v4:
time: 207 us; the launch traced here: 206 us
  blocking collectives  87.5 us (42%)
  Pallas kernels  64.2 us (31%)
  starting transfers between devices  33.1 us (16%)
  waiting for transfers between devices  16.4 us (8%)
  other arithmetic  2.14 us (1%)
    pallas_call x11, Pallas kernels, call(): pl.pallas_call(body, name=name, out_shape=[pltpu.HBM(s, t) if i in far_ou...  64.2 us
    all_to_all x3, blocking collectives, swap(): return lax.all_to_all(x, PLACE, 0, 0, tiled=True)  45.1 us
    all_to_all x1, blocking collectives, trade(): return lax.all_to_all(x, SAME, 0, 0, tiled=True)  42.4 us
    all_to_all x2, starting transfers between devices, trade(): return lax.all_to_all(x, SAME, 0, 0, tiled=True)  12.3 us
    ppermute x5, starting transfers between devices, partner(): return lax.ppermute(x, 'core', [(0, 1), (1, 0)])  11.6 us
    all_to_all x2, waiting for transfers between devices, trade(): return lax.all_to_all(x, SAME, 0, 0, tiled=True)  7.1 us
    all_to_all x1, waiting for transfers between devices, swap(): return lax.all_to_all(x, PLACE, 0, 0, tiled=True)  6.34 us
    ppermute x2, starting transfers between devices, shift(): return lax.ppermute(x, PLACE, pairs)  5.65 us
  transfers between devices with their start and end apart: 10, of which 5 were waited for; matrix products, arithmetic and copies ran while one was open for 1% of the time, Pallas kernels for 17%

profile of v4, /device:TPU:1, one launch (start us, length us, event | category | flops | bytes accessed | tf_op | source)
XLA Modules:
  0.0 206.2 jit_solution(17711623392254772501)
XLA Ops:
  0.7 0.8 slice_bitcast_fusion
  1.5 4.4 %collective-permute-start = (bf16[16,512]{1,0:T(8,128)(2,1)S(1)}, bf16[16,512]{1,0:T(8,128)(2,1)S(1)}, u32[]{:S(2)}, u32[]{:S(2)}) collective-permute-start(bf16[16,512]{1,0:T(8,128)(2,1)S(1)} %slice_bitcast_fusion), channel_id=1, source_target_pairs={{0,1},{1,2},{2,3},{3,4},{4,5},{5,6},{6,7},{7,8},{8,9},{9,10},{10,1... | collective-permute-start | bytes 49160 | tf_op jit(solution)/shard_map/ppermute | solution.py:667
  6.0 0.8 pad_add_fusion.meta
  6.8 6.8 %mamba_in.1 = (bf16[16,144,128]{2,1,0:T(8,128)(2,1)S(1)}, bf16[128,512]{1,0:T(8,128)(2,1)S(1)}, bf16[144,512]{1,0:T(8,128)(2,1)}, bf16[144,1024]{1,0:T(8,128)(2,...) custom-call(s32[9]{0:T(128)S(1)} %pad_add_fusion.meta, ...), custom_call_target="tpu_custom_call" | custom-call | tf_op jit(solution)/shard_map/mamba_in/pallas_call | solution.py:652
  13.6 17.2 %all_to_all.35.got.forward = bf16[16,144,128]{2,1,0:T(8,128)(2,1)S(1)} all-to-all(bf16[16,144,128]{2,1,0:T(8,128)(2,1)S(1)} %get-tuple-element.84), channel_id=1, replica_groups=mesh['y'=4,'core'=2,'seq'=4,'head'=4] {'seq','head'}, dimensions={0} | all-to-all | bytes 1179648 | tf_op jit(solution)/shard_map/all_to_all | solution.py:671
  30.9 4.6 %mamba_out.1 = (bf16[16,192,128]{2,1,0:T(8,128)(2,1)S(1)}, f32[16,1024]{1,0:T(8,128)}, f32[128,1024]{1,0:T(8,128)S(1)}, bf16[128,1024]{1,0:T(8,128)(2,1)S(1)}, f...) custom-call(s32[9]{0:T(128)S(1)} %pad_add_fusion.meta, bf16[16,144,128]{2,1,0:T(8,128)(2,1)S(1)} %all_to_all.35.got.forward, ...), custom_call_target="tpu_custom_call" | custom-call | tf_op jit(solution)/shard_map/mamba_out/pallas_call | solution.py:652
  35.5 14.1 %all_to_all.36.got = bf16[16,192,128]{2,1,0:T(8,128)(2,1)S(1)} all-to-all(bf16[16,192,128]{2,1,0:T(8,128)(2,1)S(1)} %get-tuple-element.90), channel_id=1, replica_groups=mesh['y'=4,'core'=2,'seq'=4,'head'=4] {'seq','head'}, dimensions={0} | all-to-all | bytes 1572864 | tf_op jit(solution)/shard_map/all_to_all | solution.py:671
  49.6 7.1 %attention.1 = bf16[16,192,128]{2,1,0:T(8,128)(2,1)S(1)} custom-call(s32[9]{0:T(128)S(1)} %pad_add_fusion.meta, bf16[16,192,128]{2,1,0:T(8,128)(2,1)S(1)} %all_to_all.36.got), custom_call_target="tpu_custom_call" | custom-call | tf_op jit(solution)/shard_map/attention/pallas_call | solution.py:652
  56.7 13.8 %all_to_all.37.got = bf16[16,192,128]{2,1,0:T(8,128)(2,1)S(1)} all-to-all(bf16[16,192,128]{2,1,0:T(8,128)(2,1)S(1)} %attention.1), channel_id=1, replica_groups=mesh['y'=4,'core'=2,'seq'=4,'head'=4] {'seq','head'}, dimensions={0} | all-to-all | bytes 1572864 | tf_op jit(solution)/shard_map/all_to_all | solution.py:671
  70.6 5.4 %middle_back.1 = (bf16[16,128,128]{2,1,0:T(8,128)(2,1)}, bf16[128,512]{1,0:T(8,128)(2,1)}, f32[128,512]{1,0:T(8,128)}, f32[128,1024]{1,0:T(8,128)}, bf16[128,102...) custom-call(s32[9]{0:T(128)S(1)} %pad_add_fusion.meta, ...), custom_call_target="tpu_custom_call" | custom-call | tf_op jit(solution)/shard_map/middle_back/pallas_call | solution.py:652
  76.0 5.7 %collective-permute-start.1 = (bf16[128,3072]{1,0:T(8,128)(2,1)S(1)}, bf16[128,3072]{1,0:T(8,128)(2,1)S(1)}, u32[]{:S(2)}, u32[]{:S(2)}) collective-permute-start(bf16[128,3072]{1,0:T(8,128)(2,1)S(1)} %get-tuple-element.98), channel_id=1, source_target_pairs={{0,16},{16,0},{1,17},{17,1},{2,18},{18,2},{3,19},{19,3},{4,20},{20... | collective-permute-start | bytes 2359304 | tf_op jit(solution)/shard_map/ppermute | solution.py:675
  81.7 3.6 %all-to-all-start.3 = ((bf16[16,128,128]{2,1,0:T(8,128)(2,1)}), bf16[16,128,128]{2,1,0:T(8,128)(2,1)S(1)}, u32[]{:S(2)}, u32[]{:S(2)}) async-start(bf16[16,128,128]{2,1,0:T(8,128)(2,1)} %get-tuple-element.99), calls=%async_computation.3 | async-start | bytes 1048576 | tf_op jit(solution)/shard_map/all_to_all | solution.py:671
  86.1 3.3 %early_weights.1 = bf16[8192,128]{1,0:T(8,128)(2,1)} custom-call(s32[9]{0:T(128)S(1)} %copy-done.17, bf16[128,3072]{1,0:T(8,128)(2,1)} %get-tuple-element.97.keep, bf16[128,3072]{1,0:T(8,128)(2,1)S(1)} %collective-permute-done.1.got), custom_call_target="tpu_custom_call" | custom-call | tf_op jit(solution)/shard_map/early_weights/pallas_call | solution.py:652
  89.4 6.3 %all-to-all-done.3.got = bf16[16,128,128]{2,1,0:T(8,128)(2,1)S(1)} async-done(((bf16[16,128,128]{2,1,0:T(8,128)(2,1)}), bf16[16,128,128]{2,1,0:T(8,128)(2,1)S(1)}, u32[]{:S(2)}, u32[]{:S(2)}) %all-to-all-start.3) | async-done | bytes 524320 | tf_op jit(solution)/shard_map/all_to_all | solution.py:671
  95.8 7.6 %all-to-all-start.4 = ((bf16[64,128,128]{2,1,0:T(8,128)(2,1)}), bf16[64,128,128]{2,1,0:T(8,128)(2,1)S(1)}, u32[]{:S(2)}, u32[]{:S(2)}) async-start(bf16[64,128,128]{2,1,0:T(8,128)(2,1)} %bitcast.14), calls=%async_computation.4 | async-start | bytes 4194304 | tf_op jit(solution)/shard_map/all_to_all | solution.py:679
  103.4 19.4 %mamba_back.1 = (f32[128,512]{1,0:T(8,128)}, f32[8,512]{1,0:T(8,128)}, bf16[144,512]{1,0:T(8,128)(2,1)}, bf16[1088,128]{1,0:T(8,128)(2,1)S(1)}, f32[512,128]{1,0:T(8,128)}) custom-call(s32[9]{0:T(128)S(1)} %copy-done.18, bf16[16,128,128]{2,1,0:T(8,128)(2,1)} %copy-done.21, bf16[16,144,128]{2,1,0:T(8,128)(2,1)} %copy-done, ...), custom_call_target="tpu_custom_call" | custom-call | tf_op jit(solution)/shard_map/mamba_back/pallas_call | solution.py:652
  122.9 1.4 collective-permute-start.3
  124.2 1.2 collective-permute-done.3.got
  125.4 2.6 %late_weights.1.late = bf16[64,40,128]{2,1,0:T(8,128)(2,1)} custom-call(bf16[144,512]{1,0:T(8,128)(2,1)} %get-tuple-element.112.keep, f32[512,128]{1,0:T(8,128)} %get-tuple-element.113.part_keep, bf16[144,512]{1,0:T(8,128)(2,1)} %get-tuple-element.93.low_ext.low_own, bf16[144,512]{1,0:T(8,128)(2,1)} %copy-done.22, ...), custom_call_target="tpu_custom_call" | custom-call | tf_op jit(solution)/shard_map/late_weights/pallas_call | solution.py:652
  128.0 2.7 %all-to-all-done.4.early = bf16[64,128,128]{2,1,0:T(8,128)(2,1)S(1)} async-done(((bf16[64,128,128]{2,1,0:T(8,128)(2,1)}), bf16[64,128,128]{2,1,0:T(8,128)(2,1)S(1)}, u32[]{:S(2)}, u32[]{:S(2)}) %all-to-all-start.4) | async-done | bytes 2097184 | tf_op jit(solution)/shard_map/all_to_all | solution.py:679
  130.7 3.1 %add_early.1 = bf16[64,168,128]{2,1,0:T(8,128)(2,1)} custom-call(bf16[64,128,128]{2,1,0:T(8,128)(2,1)S(1)} %all-to-all-done.4.early, bf16[64,40,128]{2,1,0:T(8,128)(2,1)} %late_weights.1.late), custom_call_target="tpu_custom_call" | custom-call | tf_op jit(solution)/shard_map/add_early/pallas_call | solution.py:652
  133.9 42.4 %all_to_all.38.got.mine = bf16[64,168,128]{2,1,0:T(8,128)(2,1)} all-to-all(bf16[64,168,128]{2,1,0:T(8,128)(2,1)} %add_early.1), channel_id=1, replica_groups=mesh['y'=4,'core'=2,'seq'=4,'head'=4] {'y','seq','head'}, dimensions={0} | all-to-all | bytes 5505024 | tf_op jit(solution)/shard_map/all_to_all | solution.py:679
  176.2 2.9 %collective-permute-start.4 = (bf16[64,168,128]{2,1,0:T(8,128)(2,1)}, bf16[64,168,128]{2,1,0:T(8,128)(2,1)}, u32[]{:S(2)}, u32[]{:S(2)}) collective-permute-start(bf16[64,168,128]{2,1,0:T(8,128)(2,1)} %all_to_all.38.got.mine), channel_id=1, source_target_pairs={{0,16},{16,0},{1,17},{17,1},{2,18},{18,2},{3,19},{19,3},{4,20},{20... | collective-permute-start | bytes 8257544 | tf_op jit(solution)/shard_map/ppermute | solution.py:675
  179.2 2.1 %add_late.1 = bf16[64,40,128]{2,1,0:T(8,128)(2,1)} custom-call(bf16[64,168,128]{2,1,0:T(8,128)(2,1)} %all_to_all.38.got.mine), custom_call_target="tpu_custom_call" | custom-call | tf_op jit(solution)/shard_map/add_late/pallas_call | solution.py:652
  181.3 4.6 %all-to-all-start.6 = ((bf16[64,40,128]{2,1,0:T(8,128)(2,1)}), bf16[64,40,128]{2,1,0:T(8,128)(2,1)S(1)}, u32[]{:S(2)}, u32[]{:S(2)}) async-start(bf16[64,40,128]{2,1,0:T(8,128)(2,1)} %add_late.1), calls=%async_computation.6 | async-start | bytes 1310720 | tf_op jit(solution)/shard_map/all_to_all | solution.py:679
  185.9 1.3 collective-permute-start.5
  187.3 7.1 %finish_early.1 = (f32[512,512]{1,0:T(8,128)}, f32[512,512]{1,0:T(8,128)}, f32[512,512]{1,0:T(8,128)}, f32[512,512]{1,0:T(8,128)}, f32[1024,512]{1,0:T(8,128)}, /*index=5*/f32[512,2048]{1,0:T(8,128)}) custom-call(s32[9]{0:T(128)S(1)} %copy-done.18, bf16[64,168,128]{2,1,0:T(8,128)(2,1)} %all_to_all.38.got.mine, bf16[64,168,128]{2,1,0:T(8,128)(2,1)} %collective-permute-done.4.other), custom_call_target="tpu_custom_call" | custom-call | tf_op jit(solution)/shard_map/finish_early/pallas_call | solution.py:652
  194.4 1.3 add_dynamic-update-slice_fusion
  195.7 4.4 %all-to-all-done.6.mine = bf16[64,40,128]{2,1,0:T(8,128)(2,1)S(1)} async-done(((bf16[64,40,128]{2,1,0:T(8,128)(2,1)}), bf16[64,40,128]{2,1,0:T(8,128)(2,1)S(1)}, u32[]{:S(2)}, u32[]{:S(2)}) %all-to-all-start.6) | async-done | bytes 655392 | tf_op jit(solution)/shard_map/all_to_all | solution.py:679
  200.1 1.5 collective-permute-start.6
  201.5 1.7 collective-permute-done.6.other
  203.3 2.8 %finish_late.1 = (f32[512,2048]{1,0:T(8,128)}, f32[64,1024]{1,0:T(8,128)}, f32[32,1024]{1,0:T(8,128)}, f32[16,1024]{1,0:T(8,128)}, f32[4,1024]{1,0:T(4,128)}, /*...) custom-call(s32[9]{0:T(128)S(1)} %copy-done.18, ...), custom_call_target="tpu_custom_call", output_to_operand_aliasing={{0}: (3, {})} | custom-call | tf_op jit(solution)/shard_map/finish_late/pallas_call | solution.py:652
  (54 shorter events, 1.0 us)
Async XLA Ops:
  0.7 30.2 %copy-start.10 = (bf16[1,128,512]{2,1,0:T(8,128)(2,1)S(1)}, bf16[1,128,512]{2,1,0:T(8,128)(2,1)}, u32[]{:S(2)}) copy-start(bf16[1,128,512]{2,1,0:T(8,128)(2,1)} %param.20) | copy-start | bytes 393220
  0.7 30.2 %copy-start.11 = (f32[16,1024]{1,0:T(8,128)S(1)}, f32[16,1024]{1,0:T(8,128)}, u32[]{:S(2)}) copy-start(f32[16,1024]{1,0:T(8,128)} %a_log.7) | copy-start | bytes 196612
  0.7 30.2 %copy-start.2 = (bf16[1024,512]{1,0:T(8,128)(2,1)S(1)}, bf16[1024,512]{1,0:T(8,128)(2,1)}, u32[]{:S(2)}) copy-start(bf16[1024,512]{1,0:T(8,128)(2,1)} %w_out.3) | copy-start | bytes 3145732
  0.7 30.2 %copy-start.6 = (bf16[512,512]{1,0:T(8,128)(2,1)S(1)}, bf16[512,512]{1,0:T(8,128)(2,1)}, u32[]{:S(2)}) copy-start(bf16[512,512]{1,0:T(8,128)(2,1)} %w_q.3) | copy-start | bytes 1572868
  1.5 5.2 %collective-permute-start = (bf16[16,512]{1,0:T(8,128)(2,1)S(1)}, bf16[16,512]{1,0:T(8,128)(2,1)S(1)}, u32[]{:S(2)}, u32[]{:S(2)}) collective-permute-start(bf16[16,512]{1,0:T(8,128)(2,1)S(1)} %slice_bitcast_fusion), channel_id=1, source_target_pairs={{0,1},{1,2},{2,3},{3,4},{4,5},{5,6},{6,7},{7,8},{8,9},{9,10},{10,1... | collective-permute-start | bytes 49160 | tf_op jit(solution)/shard_map/ppermute | solution.py:667
  5.9 24.9 %copy-start.8 = (bf16[512,512]{1,0:T(8,128)(2,1)S(1)}, bf16[512,512]{1,0:T(8,128)(2,1)}, u32[]{:S(2)}) copy-start(bf16[512,512]{1,0:T(8,128)(2,1)} %w_k.3) | copy-start | bytes 1572868
  5.9 24.9 %copy-start.9 = (bf16[512,512]{1,0:T(8,128)(2,1)S(1)}, bf16[512,512]{1,0:T(8,128)(2,1)}, u32[]{:S(2)}) copy-start(bf16[512,512]{1,0:T(8,128)(2,1)} %w_v.3) | copy-start | bytes 1572868
  5.9 24.9 %copy-start.19 = (f32[1024]{0:T(1024)S(1)}, f32[1024]{0:T(1024)}, u32[]{:S(2)}) copy-start(f32[1024]{0:T(1024)} %param.30) | copy-start | bytes 12292
  6.0 24.9 %copy-start.20 = (f32[512]{0:T(512)S(1)}, f32[512]{0:T(512)}, u32[]{:S(2)}) copy-start(f32[512]{0:T(512)} %param.32) | copy-start | bytes 6148
  6.8 63.7 %copy-start.16 = (s32[9]{0:T(128)}, s32[9]{0:T(128)S(1)}, u32[]{:S(2)}) copy-start(s32[9]{0:T(128)S(1)} %pad_add_fusion.meta) | copy-start | bytes 112
  6.8 28.7 %copy-start.15 = (bf16[16,512]{1,0:T(8,128)(2,1)}, bf16[16,512]{1,0:T(8,128)(2,1)S(1)}, u32[]{:S(2)}) copy-start(bf16[16,512]{1,0:T(8,128)(2,1)S(1)} %collective-permute-done.halo) | copy-start | bytes 49156
  13.6 56.9 %copy-start.1 = (f32[128,1024]{1,0:T(8,128)}, f32[128,1024]{1,0:T(8,128)S(1)}, u32[]{:S(2)}) copy-start(f32[128,1024]{1,0:T(8,128)S(1)} %get-tuple-element.85.step) | copy-start | bytes 1572868
  13.6 56.9 %copy-start.3 = (bf16[128,1024]{1,0:T(8,128)(2,1)}, bf16[128,1024]{1,0:T(8,128)(2,1)S(1)}, u32[]{:S(2)}) copy-start(bf16[128,1024]{1,0:T(8,128)(2,1)S(1)} %get-tuple-element.86.act) | copy-start | bytes 786436
  13.6 56.9 %copy-start.4 = (f32[16,32,128]{2,1,0:T(8,128)}, f32[16,32,128]{2,1,0:T(8,128)S(1)}, u32[]{:S(2)}) copy-start(f32[16,32,128]{2,1,0:T(8,128)S(1)} %get-tuple-element.87.bc) | copy-start | bytes 786436
  30.8 18.8 %copy-start = (bf16[16,144,128]{2,1,0:T(8,128)(2,1)}, bf16[16,144,128]{2,1,0:T(8,128)(2,1)S(1)}, u32[]{:S(2)}) copy-start(bf16[16,144,128]{2,1,0:T(8,128)(2,1)S(1)} %all_to_all.35.got.forward) | copy-start | bytes 1769476
  35.5 35.0 %copy-start.5 = (bf16[512,512]{1,0:T(8,128)(2,1)S(1)}, bf16[512,512]{1,0:T(8,128)(2,1)}, u32[]{:S(2)}) copy-start(bf16[512,512]{1,0:T(8,128)(2,1)} %w_o.3) | copy-start | bytes 1572868
  35.5 35.0 %copy-start.7 = (bf16[512,512]{1,0:T(8,128)(2,1)S(1)}, bf16[512,512]{1,0:T(8,128)(2,1)}, u32[]{:S(2)}) copy-start(bf16[512,512]{1,0:T(8,128)(2,1)} %w_q.3) | copy-start | bytes 1572868
  35.5 35.0 %copy-start.12 = (bf16[144,512]{1,0:T(8,128)(2,1)S(1)}, bf16[144,512]{1,0:T(8,128)(2,1)}, u32[]{:S(2)}) copy-start(bf16[144,512]{1,0:T(8,128)(2,1)} %get-tuple-element.93.low_ext.low_own) | copy-start | bytes 442372
  35.5 35.0 %copy-start.14 = (bf16[1,128,512]{2,1,0:T(8,128)(2,1)S(1)}, bf16[1,128,512]{2,1,0:T(8,128)(2,1)}, u32[]{:S(2)}) copy-start(bf16[1,128,512]{2,1,0:T(8,128)(2,1)} %param.37) | copy-start | bytes 393220
  70.6 14.7 %copy-start.13 = (bf16[144,512]{1,0:T(8,128)(2,1)S(1)}, bf16[144,512]{1,0:T(8,128)(2,1)}, u32[]{:S(2)}) copy-start(bf16[144,512]{1,0:T(8,128)(2,1)} %get-tuple-element.93.low_ext.low_own) | copy-start | bytes 442372
  76.0 9.4 %collective-permute-start.1 = (bf16[128,3072]{1,0:T(8,128)(2,1)S(1)}, bf16[128,3072]{1,0:T(8,128)(2,1)S(1)}, u32[]{:S(2)}, u32[]{:S(2)}) collective-permute-start(bf16[128,3072]{1,0:T(8,128)(2,1)S(1)} %get-tuple-element.98), channel_id=1, source_target_pairs={{0,16},{16,0},{1,17},{17,1},{2,18},{18,2},{3,19},{19,3},{4,20},{20... | collective-permute-start | bytes 2359304 | tf_op jit(solution)/shard_map/ppermute | solution.py:675
  81.7 14.1 %all-to-all-start.3 = ((bf16[16,128,128]{2,1,0:T(8,128)(2,1)}), bf16[16,128,128]{2,1,0:T(8,128)(2,1)S(1)}, u32[]{:S(2)}, u32[]{:S(2)}) async-start(bf16[16,128,128]{2,1,0:T(8,128)(2,1)} %get-tuple-element.99), calls=%async_computation.3 | async-start | bytes 1048576 | tf_op jit(solution)/shard_map/all_to_all | solution.py:671
  85.3 4.2 %collective-permute-start.2 = (bf16[144,512]{1,0:T(8,128)(2,1)S(1)}, bf16[144,512]{1,0:T(8,128)(2,1)S(1)}, u32[]{:S(2)}, u32[]{:S(2)}) collective-permute-start(bf16[144,512]{1,0:T(8,128)(2,1)S(1)} %copy-done.13), channel_id=1, source_target_pairs={{0,16},{16,0},{1,17},{17,1},{2,18},{18,2},{3,19},{19,3},{4,20},{20... | collective-permute-start | bytes 442376 | tf_op jit(solution)/shard_map/ppermute | solution.py:675
  89.4 14.0 %copy-start.18 = (s32[9]{0:T(128)S(1)}, s32[9]{0:T(128)}, u32[]{:S(2)}) copy-start(s32[9]{0:T(128)} %copy-done.16) | copy-start | bytes 112
  89.4 33.4 %copy-start.22 = (bf16[144,512]{1,0:T(8,128)(2,1)}, bf16[144,512]{1,0:T(8,128)(2,1)S(1)}, u32[]{:S(2)}) copy-start(bf16[144,512]{1,0:T(8,128)(2,1)S(1)} %collective-permute-done.2.low_other) | copy-start | bytes 442372
  95.8 35.0 %all-to-all-start.4 = ((bf16[64,128,128]{2,1,0:T(8,128)(2,1)}), bf16[64,128,128]{2,1,0:T(8,128)(2,1)S(1)}, u32[]{:S(2)}, u32[]{:S(2)}) async-start(bf16[64,128,128]{2,1,0:T(8,128)(2,1)} %bitcast.14), calls=%async_computation.4 | async-start | bytes 4194304 | tf_op jit(solution)/shard_map/all_to_all | solution.py:679
  122.9 2.6 %collective-permute-start.3 = (bf16[1088,128]{1,0:T(8,128)(2,1)S(1)}, bf16[1088,128]{1,0:T(8,128)(2,1)S(1)}, u32[]{:S(2)}, u32[]{:S(2)}) collective-permute-start(bf16[1088,128]{1,0:T(8,128)(2,1)S(1)} %get-tuple-element.115), channel_id=1, source_target_pairs={{0,16},{16,0},{1,17},{17,1},{2,18},{18,2},{3,19},{19,3},{4,20},{20... | collective-permute-start | bytes 835592 | tf_op jit(solution)/shard_map/ppermute | solution.py:675
  176.2 9.7 %copy-start.23 = (f32[8,512]{1,0:T(8,128)S(1)}, f32[8,512]{1,0:T(8,128)}, u32[]{:S(2)}) copy-start(f32[8,512]{1,0:T(8,128)} %get-tuple-element.120) | copy-start | bytes 49156
  176.2 11.0 %collective-permute-start.4 = (bf16[64,168,128]{2,1,0:T(8,128)(2,1)}, bf16[64,168,128]{2,1,0:T(8,128)(2,1)}, u32[]{:S(2)}, u32[]{:S(2)}) collective-permute-start(bf16[64,168,128]{2,1,0:T(8,128)(2,1)} %all_to_all.38.got.mine), channel_id=1, source_target_pairs={{0,16},{16,0},{1,17},{17,1},{2,18},{18,2},{3,19},{19,3},{4,20},{20... | collective-permute-start | bytes 8257544 | tf_op jit(solution)/shard_map/ppermute | solution.py:675
  181.3 18.8 %all-to-all-start.6 = ((bf16[64,40,128]{2,1,0:T(8,128)(2,1)}), bf16[64,40,128]{2,1,0:T(8,128)(2,1)S(1)}, u32[]{:S(2)}, u32[]{:S(2)}) async-start(bf16[64,40,128]{2,1,0:T(8,128)(2,1)} %add_late.1), calls=%async_computation.6 | async-start | bytes 1310720 | tf_op jit(solution)/shard_map/all_to_all | solution.py:679
  185.9 8.4 %collective-permute-start.5 = (f32[8,512]{1,0:T(8,128)S(1)}, f32[8,512]{1,0:T(8,128)S(1)}, u32[]{:S(2)}, u32[]{:S(2)}) collective-permute-start(f32[8,512]{1,0:T(8,128)S(1)} %copy-done.23), channel_id=1, source_target_pairs={{1,0},{2,1},{3,2},{4,3},{5,4},{6,5},{7,6},{8,7},{9,8},{10,9},{11,1... | collective-permute-start | bytes 49160 | tf_op jit(solution)/shard_map/ppermute | solution.py:667
  200.1 3.2 %collective-permute-start.6 = (bf16[64,40,128]{2,1,0:T(8,128)(2,1)S(1)}, bf16[64,40,128]{2,1,0:T(8,128)(2,1)S(1)}, u32[]{:S(2)}, u32[]{:S(2)}) collective-permute-start(bf16[64,40,128]{2,1,0:T(8,128)(2,1)S(1)} %all-to-all-done.6.mine), channel_id=1, source_target_pairs={{0,16},{16,0},{1,17},{17,1},{2,18},{18,2},{3,19},{19,3},{4,20},{20... | collective-permute-start | bytes 1966088 | tf_op jit(solution)/shard_map/ppermute | solution.py:675
  (2 other events, 8.3 us)

commit v5 on v4

--- a/solution.py
+++ b/solution.py
@@ -563,12 +563,19 @@
         out[d] = jnp.concatenate([main, small], axis=0).astype(bf16)
 
 
-def add_early(early, late, out):
+def add_early(early, late, out, held, sems):
     total = early[0].astype(f32)
     for j in range(1, SHARES):
         total = total + early[j].astype(f32)
+    copies = []
     for j in range(SHARES):
-        out[j] = jnp.concatenate([late[j].astype(f32), total], axis=0).astype(bf16)
+        held[j] = jnp.concatenate([late[j].astype(f32), total], axis=0).astype(bf16)
+        if j % BLOCKS == BLOCKS - 1:
+            part = pl.ds(j + 1 - BLOCKS, BLOCKS)
+            copies.append(pltpu.make_async_copy(held.at[part], out.at[part], sems.at[j // BLOCKS]))
+            copies[-1].start()
+    for copy in copies:
+        copy.wait()
 
 
 def add_late(got, out, held, sem):
@@ -603,8 +610,9 @@
 
 
 def finish_late(
-    meta, mine, other, _, gw_in, gw_x, gw_dt, g_a_log, g_conv_w, g_conv_b, g_dt_b, g_skip, g_gain_one,
-    g_gain_two, conv, sems,
+    meta, mine, other, _, gw_in, gw_x_far, gw_dt_far, g_a_log_far, g_conv_w_far, g_conv_b_far,
+    g_dt_b_far, g_skip_far, g_gain_one_far, g_gain_two_far,
+    conv, gw_x, gw_dt, g_a_log, g_conv_w, g_conv_b, g_dt_b, g_skip, g_gain_one, g_gain_two, sems,
 ):
     is_zero = meta[2 + DOCS] == 0
     copies = []
@@ -633,6 +641,20 @@
                 out[:, tile] = one[at + i : at + i + 1]
             out = g_gain_one if q < 4 else g_gain_two
             out[:, TILES[q % 4]] = one[at + 3 : at + 4]
+    smalls = (
+        (gw_x, gw_x_far),
+        (gw_dt, gw_dt_far),
+        (g_a_log, g_a_log_far),
+        (g_conv_w, g_conv_w_far),
+        (g_conv_b, g_conv_b_far),
+        (g_dt_b, g_dt_b_far),
+        (g_skip, g_skip_far),
+        (g_gain_one, g_gain_one_far),
+        (g_gain_two, g_gain_two_far),
+    )
+    for i, (held, place) in enumerate(smalls):
+        copies.append(pltpu.make_async_copy(held, place, sems.at[2 + i // 4, i % 4]))
+        copies[-1].start()
     for copy in copies:
         copy.wait()
 
@@ -748,8 +770,8 @@
         keep, part_keep, low_ext, low_other, partner(give), smem=False, far=(0, 1, 2, 3), far_out=(0,),
     )
     (both,) = call(
-        add_early, "add_early", [((SHARES, LATE + T, LANES), bf16)], [], early, late, smem=False,
-        far=(1,), far_out=(0,),
+        add_early, "add_early", [((SHARES, LATE + T, LANES), bf16)], [((SHARES, LATE + T, LANES), bf16)],
+        early, late, smem=False, far=(1,), far_out=(0,), outside=(0,), sems=((4,),),
     )
     shares = trade(both)
     (late,) = call(
@@ -769,8 +791,9 @@
         finish_late, "finish_late",
         [((D, 2 * E), f32), ((64, E), f32), ((R, E), f32), tn, ((KERNEL, E), f32), ((1, E), f32),
          ((1, E), f32), ((1, E), f32), ((1, D), f32), ((1, D), f32)],
-        [((D, E), f32)],
-        meta, late, partner(late), gw_in, outside=(0,), aliases={3: 0}, sems=((2, 4),),
+        [((D, E), f32), ((64, E), f32), ((R, E), f32), tn, ((KERNEL, E), f32), ((1, E), f32),
+         ((1, E), f32), ((1, E), f32), ((1, D), f32), ((1, D), f32)],
+        meta, late, partner(late), gw_in, outside=tuple(range(10)), aliases={3: 0}, sems=((5, 4),),
     )
     return (
         mixed[None], grad_tokens[None], g_gain_one[0], gw_in, g_conv_w, g_conv_b[0], gw_x.T, gw_dt,

time: 207 us -> 207 us (level)
  no operation moved by 1% of the time
where the time goes in v5:
time: 207 us; the launch traced here: 206 us
  blocking collectives  87.5 us (42%)
  Pallas kernels  63.6 us (31%)
  starting transfers between devices  33.1 us (16%)
  waiting for transfers between devices  16.4 us (8%)
  other arithmetic  2.14 us (1%)
    pallas_call x11, Pallas kernels, call(): pl.pallas_call(body, name=name, out_shape=[pltpu.HBM(s, t) if i in far_ou...  63.6 us
    all_to_all x3, blocking collectives, swap(): return lax.all_to_all(x, PLACE, 0, 0, tiled=True)  45.1 us
    all_to_all x1, blocking collectives, trade(): return lax.all_to_all(x, SAME, 0, 0, tiled=True)  42.4 us
    all_to_all x2, starting transfers between devices, trade(): return lax.all_to_all(x, SAME, 0, 0, tiled=True)  12.3 us
    ppermute x5, starting transfers between devices, partner(): return lax.ppermute(x, 'core', [(0, 1), (1, 0)])  11.6 us
    all_to_all x2, waiting for transfers between devices, trade(): return lax.all_to_all(x, SAME, 0, 0, tiled=True)  7.1 us
    all_to_all x1, waiting for transfers between devices, swap(): return lax.all_to_all(x, PLACE, 0, 0, tiled=True)  6.34 us
    ppermute x2, starting transfers between devices, shift(): return lax.ppermute(x, PLACE, pairs)  5.65 us
  transfers between devices with their start and end apart: 10, of which 5 were waited for; matrix products, arithmetic and copies ran while one was open for 1% of the time, Pallas kernels for 17%

profile of v5, /device:TPU:1, one launch (start us, length us, event | category | flops | bytes accessed | tf_op | source)
XLA Modules:
  0.0 205.6 jit_solution(9104317049084778113)
XLA Ops:
  0.7 0.8 slice_bitcast_fusion
  1.5 4.4 %collective-permute-start = (bf16[16,512]{1,0:T(8,128)(2,1)S(1)}, bf16[16,512]{1,0:T(8,128)(2,1)S(1)}, u32[]{:S(2)}, u32[]{:S(2)}) collective-permute-start(bf16[16,512]{1,0:T(8,128)(2,1)S(1)} %slice_bitcast_fusion), channel_id=1, source_target_pairs={{0,1},{1,2},{2,3},{3,4},{4,5},{5,6},{6,7},{7,8},{8,9},{9,10},{10,1... | collective-permute-start | bytes 49160 | tf_op jit(solution)/shard_map/ppermute | solution.py:689
  6.0 0.8 pad_add_fusion.meta
  6.8 6.8 %mamba_in.1 = (bf16[16,144,128]{2,1,0:T(8,128)(2,1)S(1)}, bf16[128,512]{1,0:T(8,128)(2,1)S(1)}, bf16[144,512]{1,0:T(8,128)(2,1)}, bf16[144,1024]{1,0:T(8,128)(2,...) custom-call(s32[9]{0:T(128)S(1)} %pad_add_fusion.meta, ...), custom_call_target="tpu_custom_call" | custom-call | tf_op jit(solution)/shard_map/mamba_in/pallas_call | solution.py:674
  13.6 17.2 %all_to_all.35.got.forward = bf16[16,144,128]{2,1,0:T(8,128)(2,1)S(1)} all-to-all(bf16[16,144,128]{2,1,0:T(8,128)(2,1)S(1)} %get-tuple-element.84), channel_id=1, replica_groups=mesh['y'=4,'core'=2,'seq'=4,'head'=4] {'seq','head'}, dimensions={0} | all-to-all | bytes 1179648 | tf_op jit(solution)/shard_map/all_to_all | solution.py:693
  30.9 4.6 %mamba_out.1 = (bf16[16,192,128]{2,1,0:T(8,128)(2,1)S(1)}, f32[16,1024]{1,0:T(8,128)}, f32[128,1024]{1,0:T(8,128)S(1)}, bf16[128,1024]{1,0:T(8,128)(2,1)S(1)}, f...) custom-call(s32[9]{0:T(128)S(1)} %pad_add_fusion.meta, bf16[16,144,128]{2,1,0:T(8,128)(2,1)S(1)} %all_to_all.35.got.forward, ...), custom_call_target="tpu_custom_call" | custom-call | tf_op jit(solution)/shard_map/mamba_out/pallas_call | solution.py:674
  35.5 14.1 %all_to_all.36.got = bf16[16,192,128]{2,1,0:T(8,128)(2,1)S(1)} all-to-all(bf16[16,192,128]{2,1,0:T(8,128)(2,1)S(1)} %get-tuple-element.90), channel_id=1, replica_groups=mesh['y'=4,'core'=2,'seq'=4,'head'=4] {'seq','head'}, dimensions={0} | all-to-all | bytes 1572864 | tf_op jit(solution)/shard_map/all_to_all | solution.py:693
  49.6 7.1 %attention.1 = bf16[16,192,128]{2,1,0:T(8,128)(2,1)S(1)} custom-call(s32[9]{0:T(128)S(1)} %pad_add_fusion.meta, bf16[16,192,128]{2,1,0:T(8,128)(2,1)S(1)} %all_to_all.36.got), custom_call_target="tpu_custom_call" | custom-call | tf_op jit(solution)/shard_map/attention/pallas_call | solution.py:674
  56.7 13.8 %all_to_all.37.got = bf16[16,192,128]{2,1,0:T(8,128)(2,1)S(1)} all-to-all(bf16[16,192,128]{2,1,0:T(8,128)(2,1)S(1)} %attention.1), channel_id=1, replica_groups=mesh['y'=4,'core'=2,'seq'=4,'head'=4] {'seq','head'}, dimensions={0} | all-to-all | bytes 1572864 | tf_op jit(solution)/shard_map/all_to_all | solution.py:693
  70.6 5.4 %middle_back.1 = (bf16[16,128,128]{2,1,0:T(8,128)(2,1)}, bf16[128,512]{1,0:T(8,128)(2,1)}, f32[128,512]{1,0:T(8,128)}, f32[128,1024]{1,0:T(8,128)}, bf16[128,102...) custom-call(s32[9]{0:T(128)S(1)} %pad_add_fusion.meta, ...), custom_call_target="tpu_custom_call" | custom-call | tf_op jit(solution)/shard_map/middle_back/pallas_call | solution.py:674
  76.0 5.7 %collective-permute-start.1 = (bf16[128,3072]{1,0:T(8,128)(2,1)S(1)}, bf16[128,3072]{1,0:T(8,128)(2,1)S(1)}, u32[]{:S(2)}, u32[]{:S(2)}) collective-permute-start(bf16[128,3072]{1,0:T(8,128)(2,1)S(1)} %get-tuple-element.98), channel_id=1, source_target_pairs={{0,16},{16,0},{1,17},{17,1},{2,18},{18,2},{3,19},{19,3},{4,20},{20... | collective-permute-start | bytes 2359304 | tf_op jit(solution)/shard_map/ppermute | solution.py:697
  81.7 3.6 %all-to-all-start.3 = ((bf16[16,128,128]{2,1,0:T(8,128)(2,1)}), bf16[16,128,128]{2,1,0:T(8,128)(2,1)S(1)}, u32[]{:S(2)}, u32[]{:S(2)}) async-start(bf16[16,128,128]{2,1,0:T(8,128)(2,1)} %get-tuple-element.99), calls=%async_computation.3 | async-start | bytes 1048576 | tf_op jit(solution)/shard_map/all_to_all | solution.py:693
  86.1 3.3 %early_weights.1 = bf16[8192,128]{1,0:T(8,128)(2,1)} custom-call(s32[9]{0:T(128)S(1)} %copy-done.17, bf16[128,3072]{1,0:T(8,128)(2,1)} %get-tuple-element.97.keep, bf16[128,3072]{1,0:T(8,128)(2,1)S(1)} %collective-permute-done.1.got), custom_call_target="tpu_custom_call" | custom-call | tf_op jit(solution)/shard_map/early_weights/pallas_call | solution.py:674
  89.4 6.3 %all-to-all-done.3.got = bf16[16,128,128]{2,1,0:T(8,128)(2,1)S(1)} async-done(((bf16[16,128,128]{2,1,0:T(8,128)(2,1)}), bf16[16,128,128]{2,1,0:T(8,128)(2,1)S(1)}, u32[]{:S(2)}, u32[]{:S(2)}) %all-to-all-start.3) | async-done | bytes 524320 | tf_op jit(solution)/shard_map/all_to_all | solution.py:693
  95.8 7.6 %all-to-all-start.4 = ((bf16[64,128,128]{2,1,0:T(8,128)(2,1)}), bf16[64,128,128]{2,1,0:T(8,128)(2,1)S(1)}, u32[]{:S(2)}, u32[]{:S(2)}) async-start(bf16[64,128,128]{2,1,0:T(8,128)(2,1)} %bitcast.14), calls=%async_computation.4 | async-start | bytes 4194304 | tf_op jit(solution)/shard_map/all_to_all | solution.py:701
  103.4 19.4 %mamba_back.1 = (f32[128,512]{1,0:T(8,128)}, f32[8,512]{1,0:T(8,128)}, bf16[144,512]{1,0:T(8,128)(2,1)}, bf16[1088,128]{1,0:T(8,128)(2,1)S(1)}, f32[512,128]{1,0:T(8,128)}) custom-call(s32[9]{0:T(128)S(1)} %copy-done.18, bf16[16,128,128]{2,1,0:T(8,128)(2,1)} %copy-done.21, bf16[16,144,128]{2,1,0:T(8,128)(2,1)} %copy-done, ...), custom_call_target="tpu_custom_call" | custom-call | tf_op jit(solution)/shard_map/mamba_back/pallas_call | solution.py:674
  122.9 1.4 collective-permute-start.3
  124.2 1.2 collective-permute-done.3.got
  125.4 2.6 %late_weights.1.late = bf16[64,40,128]{2,1,0:T(8,128)(2,1)} custom-call(bf16[144,512]{1,0:T(8,128)(2,1)} %get-tuple-element.112.keep, f32[512,128]{1,0:T(8,128)} %get-tuple-element.113.part_keep, bf16[144,512]{1,0:T(8,128)(2,1)} %get-tuple-element.93.low_ext.low_own, bf16[144,512]{1,0:T(8,128)(2,1)} %copy-done.22, ...), custom_call_target="tpu_custom_call" | custom-call | tf_op jit(solution)/shard_map/late_weights/pallas_call | solution.py:674
  128.0 2.7 %all-to-all-done.4.early = bf16[64,128,128]{2,1,0:T(8,128)(2,1)S(1)} async-done(((bf16[64,128,128]{2,1,0:T(8,128)(2,1)}), bf16[64,128,128]{2,1,0:T(8,128)(2,1)S(1)}, u32[]{:S(2)}, u32[]{:S(2)}) %all-to-all-start.4) | async-done | bytes 2097184 | tf_op jit(solution)/shard_map/all_to_all | solution.py:701
  130.7 3.0 %add_early.1 = bf16[64,168,128]{2,1,0:T(8,128)(2,1)} custom-call(bf16[64,128,128]{2,1,0:T(8,128)(2,1)S(1)} %all-to-all-done.4.early, bf16[64,40,128]{2,1,0:T(8,128)(2,1)} %late_weights.1.late), custom_call_target="tpu_custom_call" | custom-call | tf_op jit(solution)/shard_map/add_early/pallas_call | solution.py:674
  133.8 42.4 %all_to_all.38.got.mine = bf16[64,168,128]{2,1,0:T(8,128)(2,1)} all-to-all(bf16[64,168,128]{2,1,0:T(8,128)(2,1)} %add_early.1), channel_id=1, replica_groups=mesh['y'=4,'core'=2,'seq'=4,'head'=4] {'y','seq','head'}, dimensions={0} | all-to-all | bytes 5505024 | tf_op jit(solution)/shard_map/all_to_all | solution.py:701
  176.1 2.9 %collective-permute-start.4 = (bf16[64,168,128]{2,1,0:T(8,128)(2,1)}, bf16[64,168,128]{2,1,0:T(8,128)(2,1)}, u32[]{:S(2)}, u32[]{:S(2)}) collective-permute-start(bf16[64,168,128]{2,1,0:T(8,128)(2,1)} %all_to_all.38.got.mine), channel_id=1, source_target_pairs={{0,16},{16,0},{1,17},{17,1},{2,18},{18,2},{3,19},{19,3},{4,20},{20... | collective-permute-start | bytes 8257544 | tf_op jit(solution)/shard_map/ppermute | solution.py:697
  179.1 2.1 %add_late.1 = bf16[64,40,128]{2,1,0:T(8,128)(2,1)} custom-call(bf16[64,168,128]{2,1,0:T(8,128)(2,1)} %all_to_all.38.got.mine), custom_call_target="tpu_custom_call" | custom-call | tf_op jit(solution)/shard_map/add_late/pallas_call | solution.py:674
  181.2 4.6 %all-to-all-start.6 = ((bf16[64,40,128]{2,1,0:T(8,128)(2,1)}), bf16[64,40,128]{2,1,0:T(8,128)(2,1)S(1)}, u32[]{:S(2)}, u32[]{:S(2)}) async-start(bf16[64,40,128]{2,1,0:T(8,128)(2,1)} %add_late.1), calls=%async_computation.6 | async-start | bytes 1310720 | tf_op jit(solution)/shard_map/all_to_all | solution.py:701
  185.9 1.3 collective-permute-start.5
  187.2 7.1 %finish_early.1 = (f32[512,512]{1,0:T(8,128)}, f32[512,512]{1,0:T(8,128)}, f32[512,512]{1,0:T(8,128)}, f32[512,512]{1,0:T(8,128)}, f32[1024,512]{1,0:T(8,128)}, /*index=5*/f32[512,2048]{1,0:T(8,128)}) custom-call(s32[9]{0:T(128)S(1)} %copy-done.18, bf16[64,168,128]{2,1,0:T(8,128)(2,1)} %all_to_all.38.got.mine, bf16[64,168,128]{2,1,0:T(8,128)(2,1)} %collective-permute-done.4.other), custom_call_target="tpu_custom_call" | custom-call | tf_op jit(solution)/shard_map/finish_early/pallas_call | solution.py:674
  194.3 1.3 add_dynamic-update-slice_fusion
  195.6 4.4 %all-to-all-done.6.mine = bf16[64,40,128]{2,1,0:T(8,128)(2,1)S(1)} async-done(((bf16[64,40,128]{2,1,0:T(8,128)(2,1)}), bf16[64,40,128]{2,1,0:T(8,128)(2,1)S(1)}, u32[]{:S(2)}, u32[]{:S(2)}) %all-to-all-start.6) | async-done | bytes 655392 | tf_op jit(solution)/shard_map/all_to_all | solution.py:701
  200.0 1.5 collective-permute-start.6
  201.5 1.7 collective-permute-done.6.other
  203.2 2.2 %finish_late.1 = (f32[512,2048]{1,0:T(8,128)}, f32[64,1024]{1,0:T(8,128)}, f32[32,1024]{1,0:T(8,128)}, f32[16,1024]{1,0:T(8,128)}, f32[4,1024]{1,0:T(4,128)}, /*...) custom-call(s32[9]{0:T(128)S(1)} %copy-done.18, ...), custom_call_target="tpu_custom_call", output_to_operand_aliasing={{0}: (3, {})} | custom-call | tf_op jit(solution)/shard_map/finish_late/pallas_call | solution.py:674
  (54 shorter events, 1.0 us)
Async XLA Ops:
  0.7 30.2 %copy-start.10 = (bf16[1,128,512]{2,1,0:T(8,128)(2,1)S(1)}, bf16[1,128,512]{2,1,0:T(8,128)(2,1)}, u32[]{:S(2)}) copy-start(bf16[1,128,512]{2,1,0:T(8,128)(2,1)} %param.20) | copy-start | bytes 393220
  0.7 30.2 %copy-start.11 = (f32[16,1024]{1,0:T(8,128)S(1)}, f32[16,1024]{1,0:T(8,128)}, u32[]{:S(2)}) copy-start(f32[16,1024]{1,0:T(8,128)} %a_log.7) | copy-start | bytes 196612
  0.7 30.2 %copy-start.2 = (bf16[1024,512]{1,0:T(8,128)(2,1)S(1)}, bf16[1024,512]{1,0:T(8,128)(2,1)}, u32[]{:S(2)}) copy-start(bf16[1024,512]{1,0:T(8,128)(2,1)} %w_out.3) | copy-start | bytes 3145732
  0.7 30.2 %copy-start.6 = (bf16[512,512]{1,0:T(8,128)(2,1)S(1)}, bf16[512,512]{1,0:T(8,128)(2,1)}, u32[]{:S(2)}) copy-start(bf16[512,512]{1,0:T(8,128)(2,1)} %w_q.3) | copy-start | bytes 1572868
  1.5 5.2 %collective-permute-start = (bf16[16,512]{1,0:T(8,128)(2,1)S(1)}, bf16[16,512]{1,0:T(8,128)(2,1)S(1)}, u32[]{:S(2)}, u32[]{:S(2)}) collective-permute-start(bf16[16,512]{1,0:T(8,128)(2,1)S(1)} %slice_bitcast_fusion), channel_id=1, source_target_pairs={{0,1},{1,2},{2,3},{3,4},{4,5},{5,6},{6,7},{7,8},{8,9},{9,10},{10,1... | collective-permute-start | bytes 49160 | tf_op jit(solution)/shard_map/ppermute | solution.py:689
  5.9 24.9 %copy-start.8 = (bf16[512,512]{1,0:T(8,128)(2,1)S(1)}, bf16[512,512]{1,0:T(8,128)(2,1)}, u32[]{:S(2)}) copy-start(bf16[512,512]{1,0:T(8,128)(2,1)} %w_k.3) | copy-start | bytes 1572868
  5.9 24.9 %copy-start.9 = (bf16[512,512]{1,0:T(8,128)(2,1)S(1)}, bf16[512,512]{1,0:T(8,128)(2,1)}, u32[]{:S(2)}) copy-start(bf16[512,512]{1,0:T(8,128)(2,1)} %w_v.3) | copy-start | bytes 1572868
  5.9 24.9 %copy-start.19 = (f32[1024]{0:T(1024)S(1)}, f32[1024]{0:T(1024)}, u32[]{:S(2)}) copy-start(f32[1024]{0:T(1024)} %param.30) | copy-start | bytes 12292
  6.0 24.9 %copy-start.20 = (f32[512]{0:T(512)S(1)}, f32[512]{0:T(512)}, u32[]{:S(2)}) copy-start(f32[512]{0:T(512)} %param.32) | copy-start | bytes 6148
  6.8 63.7 %copy-start.16 = (s32[9]{0:T(128)}, s32[9]{0:T(128)S(1)}, u32[]{:S(2)}) copy-start(s32[9]{0:T(128)S(1)} %pad_add_fusion.meta) | copy-start | bytes 112
  6.8 28.7 %copy-start.15 = (bf16[16,512]{1,0:T(8,128)(2,1)}, bf16[16,512]{1,0:T(8,128)(2,1)S(1)}, u32[]{:S(2)}) copy-start(bf16[16,512]{1,0:T(8,128)(2,1)S(1)} %collective-permute-done.halo) | copy-start | bytes 49156
  13.6 56.9 %copy-start.1 = (f32[128,1024]{1,0:T(8,128)}, f32[128,1024]{1,0:T(8,128)S(1)}, u32[]{:S(2)}) copy-start(f32[128,1024]{1,0:T(8,128)S(1)} %get-tuple-element.85.step) | copy-start | bytes 1572868
  13.6 56.9 %copy-start.3 = (bf16[128,1024]{1,0:T(8,128)(2,1)}, bf16[128,1024]{1,0:T(8,128)(2,1)S(1)}, u32[]{:S(2)}) copy-start(bf16[128,1024]{1,0:T(8,128)(2,1)S(1)} %get-tuple-element.86.act) | copy-start | bytes 786436
  13.6 56.9 %copy-start.4 = (f32[16,32,128]{2,1,0:T(8,128)}, f32[16,32,128]{2,1,0:T(8,128)S(1)}, u32[]{:S(2)}) copy-start(f32[16,32,128]{2,1,0:T(8,128)S(1)} %get-tuple-element.87.bc) | copy-start | bytes 786436
  30.8 18.8 %copy-start = (bf16[16,144,128]{2,1,0:T(8,128)(2,1)}, bf16[16,144,128]{2,1,0:T(8,128)(2,1)S(1)}, u32[]{:S(2)}) copy-start(bf16[16,144,128]{2,1,0:T(8,128)(2,1)S(1)} %all_to_all.35.got.forward) | copy-start | bytes 1769476
  35.5 35.0 %copy-start.5 = (bf16[512,512]{1,0:T(8,128)(2,1)S(1)}, bf16[512,512]{1,0:T(8,128)(2,1)}, u32[]{:S(2)}) copy-start(bf16[512,512]{1,0:T(8,128)(2,1)} %w_o.3) | copy-start | bytes 1572868
  35.5 35.0 %copy-start.7 = (bf16[512,512]{1,0:T(8,128)(2,1)S(1)}, bf16[512,512]{1,0:T(8,128)(2,1)}, u32[]{:S(2)}) copy-start(bf16[512,512]{1,0:T(8,128)(2,1)} %w_q.3) | copy-start | bytes 1572868
  35.5 35.0 %copy-start.12 = (bf16[144,512]{1,0:T(8,128)(2,1)S(1)}, bf16[144,512]{1,0:T(8,128)(2,1)}, u32[]{:S(2)}) copy-start(bf16[144,512]{1,0:T(8,128)(2,1)} %get-tuple-element.93.low_ext.low_own) | copy-start | bytes 442372
  35.5 35.0 %copy-start.14 = (bf16[1,128,512]{2,1,0:T(8,128)(2,1)S(1)}, bf16[1,128,512]{2,1,0:T(8,128)(2,1)}, u32[]{:S(2)}) copy-start(bf16[1,128,512]{2,1,0:T(8,128)(2,1)} %param.37) | copy-start | bytes 393220
  70.6 14.7 %copy-start.13 = (bf16[144,512]{1,0:T(8,128)(2,1)S(1)}, bf16[144,512]{1,0:T(8,128)(2,1)}, u32[]{:S(2)}) copy-start(bf16[144,512]{1,0:T(8,128)(2,1)} %get-tuple-element.93.low_ext.low_own) | copy-start | bytes 442372
  76.0 9.4 %collective-permute-start.1 = (bf16[128,3072]{1,0:T(8,128)(2,1)S(1)}, bf16[128,3072]{1,0:T(8,128)(2,1)S(1)}, u32[]{:S(2)}, u32[]{:S(2)}) collective-permute-start(bf16[128,3072]{1,0:T(8,128)(2,1)S(1)} %get-tuple-element.98), channel_id=1, source_target_pairs={{0,16},{16,0},{1,17},{17,1},{2,18},{18,2},{3,19},{19,3},{4,20},{20... | collective-permute-start | bytes 2359304 | tf_op jit(solution)/shard_map/ppermute | solution.py:697
  81.7 14.1 %all-to-all-start.3 = ((bf16[16,128,128]{2,1,0:T(8,128)(2,1)}), bf16[16,128,128]{2,1,0:T(8,128)(2,1)S(1)}, u32[]{:S(2)}, u32[]{:S(2)}) async-start(bf16[16,128,128]{2,1,0:T(8,128)(2,1)} %get-tuple-element.99), calls=%async_computation.3 | async-start | bytes 1048576 | tf_op jit(solution)/shard_map/all_to_all | solution.py:693
  85.3 4.2 %collective-permute-start.2 = (bf16[144,512]{1,0:T(8,128)(2,1)S(1)}, bf16[144,512]{1,0:T(8,128)(2,1)S(1)}, u32[]{:S(2)}, u32[]{:S(2)}) collective-permute-start(bf16[144,512]{1,0:T(8,128)(2,1)S(1)} %copy-done.13), channel_id=1, source_target_pairs={{0,16},{16,0},{1,17},{17,1},{2,18},{18,2},{3,19},{19,3},{4,20},{20... | collective-permute-start | bytes 442376 | tf_op jit(solution)/shard_map/ppermute | solution.py:697
  89.4 14.0 %copy-start.18 = (s32[9]{0:T(128)S(1)}, s32[9]{0:T(128)}, u32[]{:S(2)}) copy-start(s32[9]{0:T(128)} %copy-done.16) | copy-start | bytes 112
  89.4 33.4 %copy-start.22 = (bf16[144,512]{1,0:T(8,128)(2,1)}, bf16[144,512]{1,0:T(8,128)(2,1)S(1)}, u32[]{:S(2)}) copy-start(bf16[144,512]{1,0:T(8,128)(2,1)S(1)} %collective-permute-done.2.low_other) | copy-start | bytes 442372
  95.8 35.0 %all-to-all-start.4 = ((bf16[64,128,128]{2,1,0:T(8,128)(2,1)}), bf16[64,128,128]{2,1,0:T(8,128)(2,1)S(1)}, u32[]{:S(2)}, u32[]{:S(2)}) async-start(bf16[64,128,128]{2,1,0:T(8,128)(2,1)} %bitcast.14), calls=%async_computation.4 | async-start | bytes 4194304 | tf_op jit(solution)/shard_map/all_to_all | solution.py:701
  122.9 2.6 %collective-permute-start.3 = (bf16[1088,128]{1,0:T(8,128)(2,1)S(1)}, bf16[1088,128]{1,0:T(8,128)(2,1)S(1)}, u32[]{:S(2)}, u32[]{:S(2)}) collective-permute-start(bf16[1088,128]{1,0:T(8,128)(2,1)S(1)} %get-tuple-element.115), channel_id=1, source_target_pairs={{0,16},{16,0},{1,17},{17,1},{2,18},{18,2},{3,19},{19,3},{4,20},{20... | collective-permute-start | bytes 835592 | tf_op jit(solution)/shard_map/ppermute | solution.py:697
  176.1 9.7 %copy-start.23 = (f32[8,512]{1,0:T(8,128)S(1)}, f32[8,512]{1,0:T(8,128)}, u32[]{:S(2)}) copy-start(f32[8,512]{1,0:T(8,128)} %get-tuple-element.120) | copy-start | bytes 49156
  176.1 11.0 %collective-permute-start.4 = (bf16[64,168,128]{2,1,0:T(8,128)(2,1)}, bf16[64,168,128]{2,1,0:T(8,128)(2,1)}, u32[]{:S(2)}, u32[]{:S(2)}) collective-permute-start(bf16[64,168,128]{2,1,0:T(8,128)(2,1)} %all_to_all.38.got.mine), channel_id=1, source_target_pairs={{0,16},{16,0},{1,17},{17,1},{2,18},{18,2},{3,19},{19,3},{4,20},{20... | collective-permute-start | bytes 8257544 | tf_op jit(solution)/shard_map/ppermute | solution.py:697
  181.2 18.8 %all-to-all-start.6 = ((bf16[64,40,128]{2,1,0:T(8,128)(2,1)}), bf16[64,40,128]{2,1,0:T(8,128)(2,1)S(1)}, u32[]{:S(2)}, u32[]{:S(2)}) async-start(bf16[64,40,128]{2,1,0:T(8,128)(2,1)} %add_late.1), calls=%async_computation.6 | async-start | bytes 1310720 | tf_op jit(solution)/shard_map/all_to_all | solution.py:701
  185.9 8.4 %collective-permute-start.5 = (f32[8,512]{1,0:T(8,128)S(1)}, f32[8,512]{1,0:T(8,128)S(1)}, u32[]{:S(2)}, u32[]{:S(2)}) collective-permute-start(f32[8,512]{1,0:T(8,128)S(1)} %copy-done.23), channel_id=1, source_target_pairs={{1,0},{2,1},{3,2},{4,3},{5,4},{6,5},{7,6},{8,7},{9,8},{10,9},{11,1... | collective-permute-start | bytes 49160 | tf_op jit(solution)/shard_map/ppermute | solution.py:689
  200.0 3.2 %collective-permute-start.6 = (bf16[64,40,128]{2,1,0:T(8,128)(2,1)S(1)}, bf16[64,40,128]{2,1,0:T(8,128)(2,1)S(1)}, u32[]{:S(2)}, u32[]{:S(2)}) collective-permute-start(bf16[64,40,128]{2,1,0:T(8,128)(2,1)S(1)} %all-to-all-done.6.mine), channel_id=1, source_target_pairs={{0,16},{16,0},{1,17},{17,1},{2,18},{18,2},{3,19},{19,3},{4,20},{20... | collective-permute-start | bytes 1966088 | tf_op jit(solution)/shard_map/ppermute | solution.py:697
  (2 other events, 8.3 us)

commit v6 on v5

--- a/solution.py
+++ b/solution.py
@@ -578,12 +578,18 @@
         copy.wait()
 
 
-def add_late(got, out, held, sem):
-    copy = pltpu.make_async_copy(got.at[:, pl.ds(0, 3 * N)], held, sem)
-    copy.start()
-    copy.wait()
-    total = held[0].astype(f32)[0:LATE]
-    for j in range(1, SHARES):
+def add_late(got, out, held, sems):
+    parts = [pl.ds(i * BLOCKS, BLOCKS) for i in range(SHARES // BLOCKS)]
+    loads = [
+        pltpu.make_async_copy(got.at[part, pl.ds(0, 3 * N)], held.at[part], sems.at[i])
+        for i, part in enumerate(parts)
+    ]
+    for load in loads:
+        load.start()
+    total = jnp.zeros((LATE, LANES), f32)
+    for j in range(SHARES):
+        if j % BLOCKS == 0:
+            loads[j // BLOCKS].wait()
         total = total + held[j].astype(f32)[0:LATE]
     low = total.astype(bf16)
     for j in range(SHARES):
@@ -776,7 +782,7 @@
     shares = trade(both)
     (late,) = call(
         add_late, "add_late", [((SHARES, LATE, LANES), bf16)], [((SHARES, 3 * N, LANES), bf16)],
-        shares, smem=False, far=(0,), there=(0,), sems=((),),
+        shares, smem=False, far=(0,), there=(0,), sems=((4,),),
     )
     late = trade(late)
     gw_o, gw_q, gw_k, gw_v, gw_out, gw_in = call(

time: 207 us -> 207 us (level)
  no operation moved by 1% of the time
where the time goes in v6:
time: 207 us; the launch traced here: 206 us
  blocking collectives  87.5 us (42%)
  Pallas kernels  63.6 us (31%)
  starting transfers between devices  33.1 us (16%)
  waiting for transfers between devices  16.4 us (8%)
  other arithmetic  2.14 us (1%)
    pallas_call x11, Pallas kernels, call(): pl.pallas_call(body, name=name, out_shape=[pltpu.HBM(s, t) if i in far_ou...  63.6 us
    all_to_all x3, blocking collectives, swap(): return lax.all_to_all(x, PLACE, 0, 0, tiled=True)  45.1 us
    all_to_all x1, blocking collectives, trade(): return lax.all_to_all(x, SAME, 0, 0, tiled=True)  42.4 us
    all_to_all x2, starting transfers between devices, trade(): return lax.all_to_all(x, SAME, 0, 0, tiled=True)  12.3 us
    ppermute x5, starting transfers between devices, partner(): return lax.ppermute(x, 'core', [(0, 1), (1, 0)])  11.6 us
    all_to_all x2, waiting for transfers between devices, trade(): return lax.all_to_all(x, SAME, 0, 0, tiled=True)  7.1 us
    all_to_all x1, waiting for transfers between devices, swap(): return lax.all_to_all(x, PLACE, 0, 0, tiled=True)  6.34 us
    ppermute x2, starting transfers between devices, shift(): return lax.ppermute(x, PLACE, pairs)  5.65 us
  transfers between devices with their start and end apart: 10, of which 5 were waited for; matrix products, arithmetic and copies ran while one was open for 1% of the time, Pallas kernels for 17%

profile of v6, /device:TPU:1, one launch (start us, length us, event | category | flops | bytes accessed | tf_op | source)
XLA Modules:
  0.0 205.6 jit_solution(10220644427964115981)
XLA Ops:
  0.7 0.8 slice_bitcast_fusion
  1.5 4.4 %collective-permute-start = (bf16[16,512]{1,0:T(8,128)(2,1)S(1)}, bf16[16,512]{1,0:T(8,128)(2,1)S(1)}, u32[]{:S(2)}, u32[]{:S(2)}) collective-permute-start(bf16[16,512]{1,0:T(8,128)(2,1)S(1)} %slice_bitcast_fusion), channel_id=1, source_target_pairs={{0,1},{1,2},{2,3},{3,4},{4,5},{5,6},{6,7},{7,8},{8,9},{9,10},{10,1... | collective-permute-start | bytes 49160 | tf_op jit(solution)/shard_map/ppermute | solution.py:695
  6.0 0.8 pad_add_fusion.meta
  6.8 6.8 %mamba_in.1 = (bf16[16,144,128]{2,1,0:T(8,128)(2,1)S(1)}, bf16[128,512]{1,0:T(8,128)(2,1)S(1)}, bf16[144,512]{1,0:T(8,128)(2,1)}, bf16[144,1024]{1,0:T(8,128)(2,...) custom-call(s32[9]{0:T(128)S(1)} %pad_add_fusion.meta, ...), custom_call_target="tpu_custom_call" | custom-call | tf_op jit(solution)/shard_map/mamba_in/pallas_call | solution.py:680
  13.6 17.2 %all_to_all.35.got.forward = bf16[16,144,128]{2,1,0:T(8,128)(2,1)S(1)} all-to-all(bf16[16,144,128]{2,1,0:T(8,128)(2,1)S(1)} %get-tuple-element.84), channel_id=1, replica_groups=mesh['y'=4,'core'=2,'seq'=4,'head'=4] {'seq','head'}, dimensions={0} | all-to-all | bytes 1179648 | tf_op jit(solution)/shard_map/all_to_all | solution.py:699
  30.9 4.6 %mamba_out.1 = (bf16[16,192,128]{2,1,0:T(8,128)(2,1)S(1)}, f32[16,1024]{1,0:T(8,128)}, f32[128,1024]{1,0:T(8,128)S(1)}, bf16[128,1024]{1,0:T(8,128)(2,1)S(1)}, f...) custom-call(s32[9]{0:T(128)S(1)} %pad_add_fusion.meta, bf16[16,144,128]{2,1,0:T(8,128)(2,1)S(1)} %all_to_all.35.got.forward, ...), custom_call_target="tpu_custom_call" | custom-call | tf_op jit(solution)/shard_map/mamba_out/pallas_call | solution.py:680
  35.5 14.1 %all_to_all.36.got = bf16[16,192,128]{2,1,0:T(8,128)(2,1)S(1)} all-to-all(bf16[16,192,128]{2,1,0:T(8,128)(2,1)S(1)} %get-tuple-element.90), channel_id=1, replica_groups=mesh['y'=4,'core'=2,'seq'=4,'head'=4] {'seq','head'}, dimensions={0} | all-to-all | bytes 1572864 | tf_op jit(solution)/shard_map/all_to_all | solution.py:699
  49.6 7.1 %attention.1 = bf16[16,192,128]{2,1,0:T(8,128)(2,1)S(1)} custom-call(s32[9]{0:T(128)S(1)} %pad_add_fusion.meta, bf16[16,192,128]{2,1,0:T(8,128)(2,1)S(1)} %all_to_all.36.got), custom_call_target="tpu_custom_call" | custom-call | tf_op jit(solution)/shard_map/attention/pallas_call | solution.py:680
  56.7 13.8 %all_to_all.37.got = bf16[16,192,128]{2,1,0:T(8,128)(2,1)S(1)} all-to-all(bf16[16,192,128]{2,1,0:T(8,128)(2,1)S(1)} %attention.1), channel_id=1, replica_groups=mesh['y'=4,'core'=2,'seq'=4,'head'=4] {'seq','head'}, dimensions={0} | all-to-all | bytes 1572864 | tf_op jit(solution)/shard_map/all_to_all | solution.py:699
  70.6 5.4 %middle_back.1 = (bf16[16,128,128]{2,1,0:T(8,128)(2,1)}, bf16[128,512]{1,0:T(8,128)(2,1)}, f32[128,512]{1,0:T(8,128)}, f32[128,1024]{1,0:T(8,128)}, bf16[128,102...) custom-call(s32[9]{0:T(128)S(1)} %pad_add_fusion.meta, ...), custom_call_target="tpu_custom_call" | custom-call | tf_op jit(solution)/shard_map/middle_back/pallas_call | solution.py:680
  76.0 5.7 %collective-permute-start.1 = (bf16[128,3072]{1,0:T(8,128)(2,1)S(1)}, bf16[128,3072]{1,0:T(8,128)(2,1)S(1)}, u32[]{:S(2)}, u32[]{:S(2)}) collective-permute-start(bf16[128,3072]{1,0:T(8,128)(2,1)S(1)} %get-tuple-element.98), channel_id=1, source_target_pairs={{0,16},{16,0},{1,17},{17,1},{2,18},{18,2},{3,19},{19,3},{4,20},{20... | collective-permute-start | bytes 2359304 | tf_op jit(solution)/shard_map/ppermute | solution.py:703
  81.7 3.6 %all-to-all-start.3 = ((bf16[16,128,128]{2,1,0:T(8,128)(2,1)}), bf16[16,128,128]{2,1,0:T(8,128)(2,1)S(1)}, u32[]{:S(2)}, u32[]{:S(2)}) async-start(bf16[16,128,128]{2,1,0:T(8,128)(2,1)} %get-tuple-element.99), calls=%async_computation.3 | async-start | bytes 1048576 | tf_op jit(solution)/shard_map/all_to_all | solution.py:699
  86.1 3.3 %early_weights.1 = bf16[8192,128]{1,0:T(8,128)(2,1)} custom-call(s32[9]{0:T(128)S(1)} %copy-done.17, bf16[128,3072]{1,0:T(8,128)(2,1)} %get-tuple-element.97.keep, bf16[128,3072]{1,0:T(8,128)(2,1)S(1)} %collective-permute-done.1.got), custom_call_target="tpu_custom_call" | custom-call | tf_op jit(solution)/shard_map/early_weights/pallas_call | solution.py:680
  89.4 6.3 %all-to-all-done.3.got = bf16[16,128,128]{2,1,0:T(8,128)(2,1)S(1)} async-done(((bf16[16,128,128]{2,1,0:T(8,128)(2,1)}), bf16[16,128,128]{2,1,0:T(8,128)(2,1)S(1)}, u32[]{:S(2)}, u32[]{:S(2)}) %all-to-all-start.3) | async-done | bytes 524320 | tf_op jit(solution)/shard_map/all_to_all | solution.py:699
  95.8 7.6 %all-to-all-start.4 = ((bf16[64,128,128]{2,1,0:T(8,128)(2,1)}), bf16[64,128,128]{2,1,0:T(8,128)(2,1)S(1)}, u32[]{:S(2)}, u32[]{:S(2)}) async-start(bf16[64,128,128]{2,1,0:T(8,128)(2,1)} %bitcast.14), calls=%async_computation.4 | async-start | bytes 4194304 | tf_op jit(solution)/shard_map/all_to_all | solution.py:707
  103.4 19.4 %mamba_back.1 = (f32[128,512]{1,0:T(8,128)}, f32[8,512]{1,0:T(8,128)}, bf16[144,512]{1,0:T(8,128)(2,1)}, bf16[1088,128]{1,0:T(8,128)(2,1)S(1)}, f32[512,128]{1,0:T(8,128)}) custom-call(s32[9]{0:T(128)S(1)} %copy-done.18, bf16[16,128,128]{2,1,0:T(8,128)(2,1)} %copy-done.21, bf16[16,144,128]{2,1,0:T(8,128)(2,1)} %copy-done, ...), custom_call_target="tpu_custom_call" | custom-call | tf_op jit(solution)/shard_map/mamba_back/pallas_call | solution.py:680
  122.9 1.4 collective-permute-start.3
  124.2 1.2 collective-permute-done.3.got
  125.4 2.6 %late_weights.1.late = bf16[64,40,128]{2,1,0:T(8,128)(2,1)} custom-call(bf16[144,512]{1,0:T(8,128)(2,1)} %get-tuple-element.112.keep, f32[512,128]{1,0:T(8,128)} %get-tuple-element.113.part_keep, bf16[144,512]{1,0:T(8,128)(2,1)} %get-tuple-element.93.low_ext.low_own, bf16[144,512]{1,0:T(8,128)(2,1)} %copy-done.22, ...), custom_call_target="tpu_custom_call" | custom-call | tf_op jit(solution)/shard_map/late_weights/pallas_call | solution.py:680
  128.0 2.7 %all-to-all-done.4.early = bf16[64,128,128]{2,1,0:T(8,128)(2,1)S(1)} async-done(((bf16[64,128,128]{2,1,0:T(8,128)(2,1)}), bf16[64,128,128]{2,1,0:T(8,128)(2,1)S(1)}, u32[]{:S(2)}, u32[]{:S(2)}) %all-to-all-start.4) | async-done | bytes 2097184 | tf_op jit(solution)/shard_map/all_to_all | solution.py:707
  130.7 3.0 %add_early.1 = bf16[64,168,128]{2,1,0:T(8,128)(2,1)} custom-call(bf16[64,128,128]{2,1,0:T(8,128)(2,1)S(1)} %all-to-all-done.4.early, bf16[64,40,128]{2,1,0:T(8,128)(2,1)} %late_weights.1.late), custom_call_target="tpu_custom_call" | custom-call | tf_op jit(solution)/shard_map/add_early/pallas_call | solution.py:680
  133.8 42.4 %all_to_all.38.got.mine = bf16[64,168,128]{2,1,0:T(8,128)(2,1)} all-to-all(bf16[64,168,128]{2,1,0:T(8,128)(2,1)} %add_early.1), channel_id=1, replica_groups=mesh['y'=4,'core'=2,'seq'=4,'head'=4] {'y','seq','head'}, dimensions={0} | all-to-all | bytes 5505024 | tf_op jit(solution)/shard_map/all_to_all | solution.py:707
  176.1 2.9 %collective-permute-start.4 = (bf16[64,168,128]{2,1,0:T(8,128)(2,1)}, bf16[64,168,128]{2,1,0:T(8,128)(2,1)}, u32[]{:S(2)}, u32[]{:S(2)}) collective-permute-start(bf16[64,168,128]{2,1,0:T(8,128)(2,1)} %all_to_all.38.got.mine), channel_id=1, source_target_pairs={{0,16},{16,0},{1,17},{17,1},{2,18},{18,2},{3,19},{19,3},{4,20},{20... | collective-permute-start | bytes 8257544 | tf_op jit(solution)/shard_map/ppermute | solution.py:703
  179.1 2.2 %add_late.1 = bf16[64,40,128]{2,1,0:T(8,128)(2,1)} custom-call(bf16[64,168,128]{2,1,0:T(8,128)(2,1)} %all_to_all.38.got.mine), custom_call_target="tpu_custom_call" | custom-call | tf_op jit(solution)/shard_map/add_late/pallas_call | solution.py:680
  181.2 4.6 %all-to-all-start.6 = ((bf16[64,40,128]{2,1,0:T(8,128)(2,1)}), bf16[64,40,128]{2,1,0:T(8,128)(2,1)S(1)}, u32[]{:S(2)}, u32[]{:S(2)}) async-start(bf16[64,40,128]{2,1,0:T(8,128)(2,1)} %add_late.1), calls=%async_computation.6 | async-start | bytes 1310720 | tf_op jit(solution)/shard_map/all_to_all | solution.py:707
  185.9 1.3 collective-permute-start.5
  187.2 7.1 %finish_early.1 = (f32[512,512]{1,0:T(8,128)}, f32[512,512]{1,0:T(8,128)}, f32[512,512]{1,0:T(8,128)}, f32[512,512]{1,0:T(8,128)}, f32[1024,512]{1,0:T(8,128)}, /*index=5*/f32[512,2048]{1,0:T(8,128)}) custom-call(s32[9]{0:T(128)S(1)} %copy-done.18, bf16[64,168,128]{2,1,0:T(8,128)(2,1)} %all_to_all.38.got.mine, bf16[64,168,128]{2,1,0:T(8,128)(2,1)} %collective-permute-done.4.other), custom_call_target="tpu_custom_call" | custom-call | tf_op jit(solution)/shard_map/finish_early/pallas_call | solution.py:680
  194.3 1.3 add_dynamic-update-slice_fusion
  195.6 4.4 %all-to-all-done.6.mine = bf16[64,40,128]{2,1,0:T(8,128)(2,1)S(1)} async-done(((bf16[64,40,128]{2,1,0:T(8,128)(2,1)}), bf16[64,40,128]{2,1,0:T(8,128)(2,1)S(1)}, u32[]{:S(2)}, u32[]{:S(2)}) %all-to-all-start.6) | async-done | bytes 655392 | tf_op jit(solution)/shard_map/all_to_all | solution.py:707
  200.0 1.5 collective-permute-start.6
  201.5 1.7 collective-permute-done.6.other
  203.2 2.2 %finish_late.1 = (f32[512,2048]{1,0:T(8,128)}, f32[64,1024]{1,0:T(8,128)}, f32[32,1024]{1,0:T(8,128)}, f32[16,1024]{1,0:T(8,128)}, f32[4,1024]{1,0:T(4,128)}, /*...) custom-call(s32[9]{0:T(128)S(1)} %copy-done.18, ...), custom_call_target="tpu_custom_call", output_to_operand_aliasing={{0}: (3, {})} | custom-call | tf_op jit(solution)/shard_map/finish_late/pallas_call | solution.py:680
  (54 shorter events, 1.0 us)
Async XLA Ops:
  0.7 30.2 %copy-start.10 = (bf16[1,128,512]{2,1,0:T(8,128)(2,1)S(1)}, bf16[1,128,512]{2,1,0:T(8,128)(2,1)}, u32[]{:S(2)}) copy-start(bf16[1,128,512]{2,1,0:T(8,128)(2,1)} %param.20) | copy-start | bytes 393220
  0.7 30.2 %copy-start.11 = (f32[16,1024]{1,0:T(8,128)S(1)}, f32[16,1024]{1,0:T(8,128)}, u32[]{:S(2)}) copy-start(f32[16,1024]{1,0:T(8,128)} %a_log.7) | copy-start | bytes 196612
  0.7 30.2 %copy-start.2 = (bf16[1024,512]{1,0:T(8,128)(2,1)S(1)}, bf16[1024,512]{1,0:T(8,128)(2,1)}, u32[]{:S(2)}) copy-start(bf16[1024,512]{1,0:T(8,128)(2,1)} %w_out.3) | copy-start | bytes 3145732
  0.7 30.2 %copy-start.6 = (bf16[512,512]{1,0:T(8,128)(2,1)S(1)}, bf16[512,512]{1,0:T(8,128)(2,1)}, u32[]{:S(2)}) copy-start(bf16[512,512]{1,0:T(8,128)(2,1)} %w_q.3) | copy-start | bytes 1572868
  1.5 5.2 %collective-permute-start = (bf16[16,512]{1,0:T(8,128)(2,1)S(1)}, bf16[16,512]{1,0:T(8,128)(2,1)S(1)}, u32[]{:S(2)}, u32[]{:S(2)}) collective-permute-start(bf16[16,512]{1,0:T(8,128)(2,1)S(1)} %slice_bitcast_fusion), channel_id=1, source_target_pairs={{0,1},{1,2},{2,3},{3,4},{4,5},{5,6},{6,7},{7,8},{8,9},{9,10},{10,1... | collective-permute-start | bytes 49160 | tf_op jit(solution)/shard_map/ppermute | solution.py:695
  5.9 24.9 %copy-start.8 = (bf16[512,512]{1,0:T(8,128)(2,1)S(1)}, bf16[512,512]{1,0:T(8,128)(2,1)}, u32[]{:S(2)}) copy-start(bf16[512,512]{1,0:T(8,128)(2,1)} %w_k.3) | copy-start | bytes 1572868
  5.9 24.9 %copy-start.9 = (bf16[512,512]{1,0:T(8,128)(2,1)S(1)}, bf16[512,512]{1,0:T(8,128)(2,1)}, u32[]{:S(2)}) copy-start(bf16[512,512]{1,0:T(8,128)(2,1)} %w_v.3) | copy-start | bytes 1572868
  5.9 24.9 %copy-start.19 = (f32[1024]{0:T(1024)S(1)}, f32[1024]{0:T(1024)}, u32[]{:S(2)}) copy-start(f32[1024]{0:T(1024)} %param.30) | copy-start | bytes 12292
  6.0 24.9 %copy-start.20 = (f32[512]{0:T(512)S(1)}, f32[512]{0:T(512)}, u32[]{:S(2)}) copy-start(f32[512]{0:T(512)} %param.32) | copy-start | bytes 6148
  6.8 63.7 %copy-start.16 = (s32[9]{0:T(128)}, s32[9]{0:T(128)S(1)}, u32[]{:S(2)}) copy-start(s32[9]{0:T(128)S(1)} %pad_add_fusion.meta) | copy-start | bytes 112
  6.8 28.7 %copy-start.15 = (bf16[16,512]{1,0:T(8,128)(2,1)}, bf16[16,512]{1,0:T(8,128)(2,1)S(1)}, u32[]{:S(2)}) copy-start(bf16[16,512]{1,0:T(8,128)(2,1)S(1)} %collective-permute-done.halo) | copy-start | bytes 49156
  13.6 56.9 %copy-start.1 = (f32[128,1024]{1,0:T(8,128)}, f32[128,1024]{1,0:T(8,128)S(1)}, u32[]{:S(2)}) copy-start(f32[128,1024]{1,0:T(8,128)S(1)} %get-tuple-element.85.step) | copy-start | bytes 1572868
  13.6 56.9 %copy-start.3 = (bf16[128,1024]{1,0:T(8,128)(2,1)}, bf16[128,1024]{1,0:T(8,128)(2,1)S(1)}, u32[]{:S(2)}) copy-start(bf16[128,1024]{1,0:T(8,128)(2,1)S(1)} %get-tuple-element.86.act) | copy-start | bytes 786436
  13.6 56.9 %copy-start.4 = (f32[16,32,128]{2,1,0:T(8,128)}, f32[16,32,128]{2,1,0:T(8,128)S(1)}, u32[]{:S(2)}) copy-start(f32[16,32,128]{2,1,0:T(8,128)S(1)} %get-tuple-element.87.bc) | copy-start | bytes 786436
  30.8 18.8 %copy-start = (bf16[16,144,128]{2,1,0:T(8,128)(2,1)}, bf16[16,144,128]{2,1,0:T(8,128)(2,1)S(1)}, u32[]{:S(2)}) copy-start(bf16[16,144,128]{2,1,0:T(8,128)(2,1)S(1)} %all_to_all.35.got.forward) | copy-start | bytes 1769476
  35.5 35.0 %copy-start.5 = (bf16[512,512]{1,0:T(8,128)(2,1)S(1)}, bf16[512,512]{1,0:T(8,128)(2,1)}, u32[]{:S(2)}) copy-start(bf16[512,512]{1,0:T(8,128)(2,1)} %w_o.3) | copy-start | bytes 1572868
  35.5 35.0 %copy-start.7 = (bf16[512,512]{1,0:T(8,128)(2,1)S(1)}, bf16[512,512]{1,0:T(8,128)(2,1)}, u32[]{:S(2)}) copy-start(bf16[512,512]{1,0:T(8,128)(2,1)} %w_q.3) | copy-start | bytes 1572868
  35.5 35.0 %copy-start.12 = (bf16[144,512]{1,0:T(8,128)(2,1)S(1)}, bf16[144,512]{1,0:T(8,128)(2,1)}, u32[]{:S(2)}) copy-start(bf16[144,512]{1,0:T(8,128)(2,1)} %get-tuple-element.93.low_ext.low_own) | copy-start | bytes 442372
  35.5 35.0 %copy-start.14 = (bf16[1,128,512]{2,1,0:T(8,128)(2,1)S(1)}, bf16[1,128,512]{2,1,0:T(8,128)(2,1)}, u32[]{:S(2)}) copy-start(bf16[1,128,512]{2,1,0:T(8,128)(2,1)} %param.37) | copy-start | bytes 393220
  70.6 14.7 %copy-start.13 = (bf16[144,512]{1,0:T(8,128)(2,1)S(1)}, bf16[144,512]{1,0:T(8,128)(2,1)}, u32[]{:S(2)}) copy-start(bf16[144,512]{1,0:T(8,128)(2,1)} %get-tuple-element.93.low_ext.low_own) | copy-start | bytes 442372
  76.0 9.4 %collective-permute-start.1 = (bf16[128,3072]{1,0:T(8,128)(2,1)S(1)}, bf16[128,3072]{1,0:T(8,128)(2,1)S(1)}, u32[]{:S(2)}, u32[]{:S(2)}) collective-permute-start(bf16[128,3072]{1,0:T(8,128)(2,1)S(1)} %get-tuple-element.98), channel_id=1, source_target_pairs={{0,16},{16,0},{1,17},{17,1},{2,18},{18,2},{3,19},{19,3},{4,20},{20... | collective-permute-start | bytes 2359304 | tf_op jit(solution)/shard_map/ppermute | solution.py:703
  81.7 14.1 %all-to-all-start.3 = ((bf16[16,128,128]{2,1,0:T(8,128)(2,1)}), bf16[16,128,128]{2,1,0:T(8,128)(2,1)S(1)}, u32[]{:S(2)}, u32[]{:S(2)}) async-start(bf16[16,128,128]{2,1,0:T(8,128)(2,1)} %get-tuple-element.99), calls=%async_computation.3 | async-start | bytes 1048576 | tf_op jit(solution)/shard_map/all_to_all | solution.py:699
  85.3 4.2 %collective-permute-start.2 = (bf16[144,512]{1,0:T(8,128)(2,1)S(1)}, bf16[144,512]{1,0:T(8,128)(2,1)S(1)}, u32[]{:S(2)}, u32[]{:S(2)}) collective-permute-start(bf16[144,512]{1,0:T(8,128)(2,1)S(1)} %copy-done.13), channel_id=1, source_target_pairs={{0,16},{16,0},{1,17},{17,1},{2,18},{18,2},{3,19},{19,3},{4,20},{20... | collective-permute-start | bytes 442376 | tf_op jit(solution)/shard_map/ppermute | solution.py:703
  89.4 14.0 %copy-start.18 = (s32[9]{0:T(128)S(1)}, s32[9]{0:T(128)}, u32[]{:S(2)}) copy-start(s32[9]{0:T(128)} %copy-done.16) | copy-start | bytes 112
  89.4 33.4 %copy-start.22 = (bf16[144,512]{1,0:T(8,128)(2,1)}, bf16[144,512]{1,0:T(8,128)(2,1)S(1)}, u32[]{:S(2)}) copy-start(bf16[144,512]{1,0:T(8,128)(2,1)S(1)} %collective-permute-done.2.low_other) | copy-start | bytes 442372
  95.8 35.0 %all-to-all-start.4 = ((bf16[64,128,128]{2,1,0:T(8,128)(2,1)}), bf16[64,128,128]{2,1,0:T(8,128)(2,1)S(1)}, u32[]{:S(2)}, u32[]{:S(2)}) async-start(bf16[64,128,128]{2,1,0:T(8,128)(2,1)} %bitcast.14), calls=%async_computation.4 | async-start | bytes 4194304 | tf_op jit(solution)/shard_map/all_to_all | solution.py:707
  122.9 2.6 %collective-permute-start.3 = (bf16[1088,128]{1,0:T(8,128)(2,1)S(1)}, bf16[1088,128]{1,0:T(8,128)(2,1)S(1)}, u32[]{:S(2)}, u32[]{:S(2)}) collective-permute-start(bf16[1088,128]{1,0:T(8,128)(2,1)S(1)} %get-tuple-element.115), channel_id=1, source_target_pairs={{0,16},{16,0},{1,17},{17,1},{2,18},{18,2},{3,19},{19,3},{4,20},{20... | collective-permute-start | bytes 835592 | tf_op jit(solution)/shard_map/ppermute | solution.py:703
  176.1 9.8 %copy-start.23 = (f32[8,512]{1,0:T(8,128)S(1)}, f32[8,512]{1,0:T(8,128)}, u32[]{:S(2)}) copy-start(f32[8,512]{1,0:T(8,128)} %get-tuple-element.120) | copy-start | bytes 49156
  176.1 11.1 %collective-permute-start.4 = (bf16[64,168,128]{2,1,0:T(8,128)(2,1)}, bf16[64,168,128]{2,1,0:T(8,128)(2,1)}, u32[]{:S(2)}, u32[]{:S(2)}) collective-permute-start(bf16[64,168,128]{2,1,0:T(8,128)(2,1)} %all_to_all.38.got.mine), channel_id=1, source_target_pairs={{0,16},{16,0},{1,17},{17,1},{2,18},{18,2},{3,19},{19,3},{4,20},{20... | collective-permute-start | bytes 8257544 | tf_op jit(solution)/shard_map/ppermute | solution.py:703
  181.2 18.8 %all-to-all-start.6 = ((bf16[64,40,128]{2,1,0:T(8,128)(2,1)}), bf16[64,40,128]{2,1,0:T(8,128)(2,1)S(1)}, u32[]{:S(2)}, u32[]{:S(2)}) async-start(bf16[64,40,128]{2,1,0:T(8,128)(2,1)} %add_late.1), calls=%async_computation.6 | async-start | bytes 1310720 | tf_op jit(solution)/shard_map/all_to_all | solution.py:707
  185.9 8.4 %collective-permute-start.5 = (f32[8,512]{1,0:T(8,128)S(1)}, f32[8,512]{1,0:T(8,128)S(1)}, u32[]{:S(2)}, u32[]{:S(2)}) collective-permute-start(f32[8,512]{1,0:T(8,128)S(1)} %copy-done.23), channel_id=1, source_target_pairs={{1,0},{2,1},{3,2},{4,3},{5,4},{6,5},{7,6},{8,7},{9,8},{10,9},{11,1... | collective-permute-start | bytes 49160 | tf_op jit(solution)/shard_map/ppermute | solution.py:695
  200.0 3.2 %collective-permute-start.6 = (bf16[64,40,128]{2,1,0:T(8,128)(2,1)S(1)}, bf16[64,40,128]{2,1,0:T(8,128)(2,1)S(1)}, u32[]{:S(2)}, u32[]{:S(2)}) collective-permute-start(bf16[64,40,128]{2,1,0:T(8,128)(2,1)S(1)} %all-to-all-done.6.mine), channel_id=1, source_target_pairs={{0,16},{16,0},{1,17},{17,1},{2,18},{18,2},{3,19},{19,3},{4,20},{20... | collective-permute-start | bytes 1966088 | tf_op jit(solution)/shard_map/ppermute | solution.py:703
  (2 other events, 8.3 us)
